TPU v7x, 512 devices: a whole 4x4x16 slice. The times are simulated.
512 devices in a mesh: sweep: 4 (over y), ops: 128 (over z, x, core).
Axes of the slice: x: 4, y: 4, z: 16, core: 2. Of those that a mesh axis runs over, the one named last changes fastest.
Arguments:
- initial_trial_state: bfloat16 [4, 32, 128, 128], P('sweep'), may hold values from -6 to 6
- left_ops: bfloat16 [4, 128, 32, 128, 128], P('sweep', 'ops'), may hold values from -0.5 to 0.5
- right_ops: bfloat16 [4, 128, 32, 128, 128], P('sweep', 'ops'), may hold values from -0.5 to 0.5
- pair_sectors: int32 [4, 128, 32], P('sweep', 'ops'), may hold values 0 or 1
- sector_size: int32 [4, 32], P('sweep'), may hold values from 1 to 128, 3072 in all within a row
- left_env: bfloat16 [4, 32, 128, 128], P('sweep'), may hold values from -0.5 to 0.5
Outputs:
- psi_out: bfloat16 [4, 32, 128, 128], P('sweep')
- next_left: bfloat16 [4, 32, 128, 128], P('sweep')
Inputs may be any that keep to these rules, and one draw needn't show every extreme that they name: `sector_size`: at each position the sector sizes sum to 3072 and the largest is exactly 128.
All inputs are finite; a program needn't handle non-finite values. No bound on the sum of `pair_sectors` on one device may be relied on, other than what follows from the above.
Results may differ from a plain program's by a relative error of at most 0.012.
Values may be sent and summed in bfloat16 or wider, within the bound.
No kernel may reach another device: no remote copies, remote signals or barrier semaphores. Data moves between devices by JAX's collectives and lax.ppermute only.
A program may use at most 64 MiB of HBM per device.

v0:
```python
import math

import jax
import jax.numpy as jnp
from jax import lax
from jax.sharding import PartitionSpec as P

ITERS = 2


def passed_along(value, axis, by):
    devices = lax.axis_size(axis)
    pairs = [(i, i + by) for i in range(devices) if 0 <= i + by < devices]
    return lax.ppermute(value, axis, pairs)


def pair_terms(left, right_environment, live, xb):
    live_f = live.astype(jnp.float32)[:, :, None, None]
    front_multiplier = (
        live_f * jnp.einsum("kiab,ibc->kiac", left, xb, preferred_element_type=jnp.float32)
    ).astype(jnp.bfloat16)
    rear_multiplier = (
        live_f * jnp.einsum("kiba,ibc->kiac", left, xb, preferred_element_type=jnp.float32)
    ).astype(jnp.bfloat16)
    summand_piece = jnp.einsum(
        "qweo,qwxo->wex", front_multiplier, right_environment, preferred_element_type=jnp.float32
    )
    return summand_piece + jnp.einsum(
        "jbpf,jbfh->bph", rear_multiplier, right_environment, preferred_element_type=jnp.float32
    )


def shards(initial_trial_state, left_ops, right_ops, pair_sectors, sector_size, left_env):
    left = left_ops[0]
    right_environment = right_ops[0]
    live = pair_sectors[0]
    sizes = sector_size[0]
    env = left_env[0]
    nsec = env.shape[0]
    width = env.shape[1]
    total = nsec * width * width
    scale = 1.0 / math.sqrt(left.shape[0] * lax.axis_size("ops"))
    states = jnp.arange(width)
    alive = states[None, :] < sizes[:, None]
    weight = (alive[:, :, None] & alive[:, None, :]).astype(jnp.float32)
    x = weight * initial_trial_state[0].astype(jnp.float32)
    for step in range(ITERS):
        xb = x.astype(jnp.bfloat16)
        collapsed_aggregate = lax.psum(pair_terms(left, right_environment, live, xb), "ops")
        applied = jnp.einsum("iab,ibc->iac", env, xb, preferred_element_type=jnp.float32)
        sigma = weight * (scale * collapsed_aggregate + applied)
        rho = jnp.sum(x * sigma) / jnp.sum(x * x)
        y_new = x - 0.8 * (sigma - rho * x)
        x = y_new / jnp.sqrt(jnp.sum(y_new * y_new) / total + 1e-06)
    psi_b = x.astype(jnp.bfloat16)
    applied = jnp.einsum("iab,ibc->iac", env, psi_b, preferred_element_type=jnp.float32).astype(
        jnp.bfloat16
    )
    normalize_again = (
        jnp.einsum("iba,ibc->iac", psi_b, applied, preferred_element_type=jnp.float32)
        / math.sqrt(width)
    ).astype(jnp.bfloat16)
    received = passed_along(normalize_again, "sweep", 1)
    next_left = (env.astype(jnp.float32) + received.astype(jnp.float32)).astype(jnp.bfloat16)
    return (psi_b[None], next_left[None])


def solution(mesh):
    return jax.shard_map(
        shards,
        mesh=mesh,
        in_specs=(
            P("sweep", None, None, None),
            P("sweep", "ops", None, None, None),
            P("sweep", "ops", None, None, None),
            P("sweep", "ops", None),
            P("sweep", None),
            P("sweep", None, None, None),
        ),
        out_specs=(P("sweep", None, None, None), P("sweep", None, None, None)),
        check_vma=False,
    )
```

profile of v0, /device:TPU:25, one launch (start us, length us, event | category | flops | bytes accessed | tf_op | source)
XLA Modules:
  0.0 785.1 jit_solution(1954346398664557919)
XLA Ops:
  7.2 0.0 copy-start
  7.2 0.0 all-reduce.3.cloned.1.call-start
  7.2 0.7 convert_bitcast_fusion
  8.0 0.7 iota_compare_fusion
  8.7 0.0 copy-done
  8.7 0.0 copy-start.1
  8.7 0.0 copy-start.2
  8.7 4.6 fusion.26
  13.3 0.0 copy-done.1
  13.4 0.0 copy-done.2
  13.4 4.1 convolution_add_fusion.1
  17.5 0.0 copy-start.3
  17.5 0.0 all-reduce.3.cloned.1.call-update
  17.5 0.0 all-reduce.5.cloned.1.call-start
  17.6 352.1 %all-reduce.3.cloned.1.call-done = f32[32,128,128]{2,1,0:T(8,128)} async-done(((f32[32,128,128]{2,1,0:T(8,128)}), f32[32,128,128]{2,1,0:T(8,128)}) %all-reduce.3.cloned.1.call-update) | async-done | bytes 2097168 | tf_op jit(solution)/shard_map/psum | solution.py:49
  369.6 0.0 copy-done.3
  369.6 5.1 fusion.6
  376.1 2.7 multiply_reduce_fusion.3
  379.5 2.3 broadcast_divide_fusion
  381.8 4.1 fusion.23
  385.9 4.1 convolution_add_fusion
  390.0 0.0 all-reduce.5.cloned.1.call-update
  390.0 346.3 %all-reduce.5.cloned.1.call-done = f32[32,128,128]{2,1,0:T(8,128)} async-done(((f32[32,128,128]{2,1,0:T(8,128)}), f32[32,128,128]{2,1,0:T(8,128)}) %all-reduce.5.cloned.1.call-update) | async-done | bytes 2097168 | tf_op jit(solution)/shard_map/psum | solution.py:49
  736.2 3.9 multiply_reduce_fusion.1
  741.5 2.7 multiply_reduce_fusion
  744.9 3.0 divide_convert_fusion
  747.9 0.0 copy-start.4
  747.9 3.6 multiply_convert_fusion
  751.5 1.3 collective-permute-start
  752.8 24.1 %collective-permute-done = bf16[32,128,128]{2,1,0:T(8,128)(2,1)S(1)} collective-permute-done((bf16[32,128,128]{2,1,0:T(8,128)(2,1)S(1)}, bf16[32,128,128]{2,1,0:T(8,128)(2,1)S(1)}, u32[]{:S(2)}, u32[]{:S(2)}) %collective-permute-start) | collective-permute-done | bytes 1048608 | tf_op jit(solution)/shard_map/ppermute | solution.py:14
  777.0 0.0 copy-done.4
  777.0 1.3 fusion.17
Async XLA Ops:
  7.2 1.5 copy-start
  7.2 362.4 %all-reduce.3.cloned.1.call-start = ((), (), s32[]{:S(2)}) async-start(), calls=%async_computation | async-start | bytes 4194304 | tf_op jit(solution)/shard_map/psum | solution.py:49
  8.7 4.7 copy-start.1
  8.7 4.7 copy-start.2
  17.5 352.1 %copy-start.3 = (bf16[1,32,128,128]{3,2,1,0:T(8,128)(2,1)S(1)}, bf16[1,32,128,128]{3,2,1,0:T(8,128)(2,1)}, u32[]{:S(2)}) copy-start(bf16[1,32,128,128]{3,2,1,0:T(8,128)(2,1)} %param.11) | copy-start | bytes 3145732
  17.5 718.7 %all-reduce.5.cloned.1.call-start = ((), (), s32[]{:S(2)}) async-start(), calls=%async_computation.1 | async-start | bytes 4194304 | tf_op jit(solution)/shard_map/psum | solution.py:49
  747.9 29.0 %copy-start.4 = (bf16[1,32,128,128]{3,2,1,0:T(8,128)(2,1)S(1)}, bf16[1,32,128,128]{3,2,1,0:T(8,128)(2,1)}, u32[]{:S(2)}) copy-start(bf16[1,32,128,128]{3,2,1,0:T(8,128)(2,1)} %param.11) | copy-start | bytes 3145732
  751.5 25.4 %collective-permute-start = (bf16[32,128,128]{2,1,0:T(8,128)(2,1)S(1)}, bf16[32,128,128]{2,1,0:T(8,128)(2,1)S(1)}, u32[]{:S(2)}, u32[]{:S(2)}) collective-permute-start(bf16[32,128,128]{2,1,0:T(8,128)(2,1)S(1)} %multiply_convert_fusion), channel_id=1, source_target_pairs={{0,128},{128,256},{256,384},{1,129},{129,257},{257,385},{2,130},{1... | collective-permute-start | bytes 3145736 | tf_op jit(solution)/shard_map/ppermute | solution.py:14
Sparse Core Ops, SparseCore 0:
  17.6 351.9 all-reduce.2
  390.1 346.0 all-reduce.4
where the time goes:
time: 787 us; the launch traced here: 785 us
  waiting for transfers between devices  722 us (92%)
  matrix products  29.6 us (4%)
  between operations  18.1 us (2%)
  other arithmetic  13.5 us (2%)
    psum x2, waiting for transfers between devices, shards(): lax.psum(pair_terms(left, right_environment, live, xb), 'ops')  698 us
    ppermute x1, waiting for transfers between devices, passed_along(): return lax.ppermute(value, axis, pairs)  24.1 us
  transfers between devices with their start and end apart: 3, of which 3 were waited for; matrix products, arithmetic and copies ran while one was open for 0% of the time, Pallas kernels for 0%

commit v1 on v0

v1 whole, which is shorter than its diff:
```python
import math

import jax
import jax.numpy as jnp
from jax import lax
from jax.experimental import pallas as pl
from jax.experimental.pallas import tpu as pltpu
from jax.sharding import Mesh, PartitionSpec as P

ITERS = 2
NSEC = 32
WIDTH = 128
PAIRS = 128
ROWS = 3 * NSEC * WIDTH // 4
HALF = ROWS // 2
TOTAL = NSEC * WIDTH * WIDTH
X, ZL, ZH = 4, 4, 4
NEAR = ZL * X
PIECE = HALF // NEAR
SCALE = 1.0 / math.sqrt(PAIRS)

WHOLE = pl.BlockSpec(memory_space=pltpu.VMEM)
SCALARS = pl.BlockSpec(memory_space=pltpu.SMEM)


def square_mask(size):
    row = lax.broadcasted_iota(jnp.int32, (WIDTH, WIDTH), 0)
    col = lax.broadcasted_iota(jnp.int32, (WIDTH, WIDTH), 1)
    return (row < size) & (col < size)


def dot(a, b, left_dim, right_dim):
    return lax.dot_general(
        a, b, (((left_dim,), (right_dim,)), ((), ())), preferred_element_type=jnp.float32
    )


def fold(value):
    return jnp.sum(value.reshape(WIDTH // 8, 8, WIDTH), axis=0)


def step_factors(sizes, x_of, sigma, masked):
    def body(i, carry):
        offset, xx, xs, ss = carry
        size = sizes[i]
        x = x_of(i)
        s = jnp.where(square_mask(size), sigma[pl.ds(offset, WIDTH), :], 0.0)
        masked[i] = s
        return offset + size, xx + fold(x * x), xs + fold(x * s), ss + fold(s * s)

    zero = jnp.zeros((8, WIDTH), jnp.float32)
    _, xx, xs, ss = lax.fori_loop(0, NSEC, body, (jnp.int32(0), zero, zero, zero), unroll=2)
    xx, xs, ss = jnp.sum(xx), jnp.sum(xs), jnp.sum(ss)
    rho = xs / xx
    yy = xx + 0.64 * jnp.maximum(ss - rho * xs, 0.0)
    shrink = 1.0 / jnp.sqrt(jnp.full((8, WIDTH), yy / TOTAL + 1e-06))[0, 0]
    return (1.0 + 0.8 * rho) * shrink, 0.8 * shrink


def pair_sum(meta, sizes, live, xb_of, left, right, env, packed, mine, other):
    sector = meta[1]

    def body(i, offset):
        xb = xb_of(i)
        on = live[i].astype(jnp.float32)
        block = left[i]
        front = (on * dot(block, xb, 1, 0)).astype(jnp.bfloat16)
        rear = (on * dot(block, xb, 0, 0)).astype(jnp.bfloat16)
        context = right[i]
        total = SCALE * (dot(front, context, 1, 1) + dot(rear, context, 1, 0))
        packed[pl.ds(offset, WIDTH), :] = total

        @pl.when(i == sector)
        def _():
            packed[pl.ds(offset, WIDTH), :] += 0.25 * dot(env[0], xb, 1, 0)

        return offset + sizes[i]

    lax.fori_loop(0, NSEC, body, jnp.int32(0), unroll=2)
    core = meta[0]
    mine[...] = packed[pl.ds(pl.multiple_of(core * HALF, 8), HALF), :]
    other[...] = packed[pl.ds(pl.multiple_of((1 - core) * HALF, 8), HALF), :].astype(jnp.bfloat16)


def first_kernel(meta, sizes, live, x0, left, right, env, mine, other, packed):
    def xb_of(i):
        x = x0[i]
        return jnp.where(square_mask(sizes[i]), x, jnp.zeros_like(x))

    pair_sum(meta, sizes, live, xb_of, left, right, env, packed, mine, other)


def next_kernel(meta, sizes, live, x0, sigma, left, right, env, mine, other, x_out, packed, wide, masked):
    def x_of(i):
        return jnp.where(square_mask(sizes[i]), x0[i].astype(jnp.float32), 0.0)

    wide[pl.ds(0, ROWS), :] = sigma[...].astype(jnp.float32)
    grow, drop = step_factors(sizes, x_of, wide, masked)

    def xb_of(i):
        x = grow * x_of(i) - drop * masked[i]
        x_out[i] = x
        return x.astype(jnp.bfloat16)

    pair_sum(meta, sizes, live, xb_of, left, right, env, packed, mine, other)


def last_kernel(sizes, x, sigma, env, psi_out, renorm_out, wide, masked):
    def x_of(i):
        return x[i]

    wide[pl.ds(0, ROWS), :] = sigma[...].astype(jnp.float32)
    grow, drop = step_factors(sizes, x_of, wide, masked)

    def body(i, carry):
        psi = (grow * x_of(i) - drop * masked[i]).astype(jnp.bfloat16)
        psi_out[i] = psi
        applied = dot(env[i], psi, 1, 0).astype(jnp.bfloat16)
        renorm_out[i] = (dot(psi, applied, 0, 0) / math.sqrt(WIDTH)).astype(jnp.bfloat16)
        return carry

    lax.fori_loop(0, NSEC, body, 0, unroll=2)


def shape(dims, dtype):
    return jax.ShapeDtypeStruct(dims, dtype)


PACKED = pltpu.VMEM((ROWS + WIDTH, WIDTH), jnp.float32)
BLOCKS = pltpu.VMEM((NSEC, WIDTH, WIDTH), jnp.float32)
PARAMS = pltpu.CompilerParams(vmem_limit_bytes=32 * 1024 * 1024)


def one_sector(meta, sizes, live):
    return pl.BlockSpec((1, WIDTH, WIDTH), lambda i, meta, sizes, live: (meta[1], 0, 0))


def pair_call(kernel, extra, out_extra, scratch):
    return pl.pallas_call(
        kernel,
        grid_spec=pltpu.PrefetchScalarGridSpec(
            num_scalar_prefetch=3,
            grid=(1,),
            in_specs=[WHOLE] * (3 + extra)
            + [pl.BlockSpec((1, WIDTH, WIDTH), lambda i, meta, sizes, live: (meta[1], 0, 0))],
            out_specs=[WHOLE] * (2 + len(out_extra)),
            scratch_shapes=scratch,
        ),
        out_shape=[shape((HALF, WIDTH), jnp.float32), shape((HALF, WIDTH), jnp.bfloat16)] + out_extra,
        compiler_params=PARAMS,
    )


def exchange(value, axes):
    return lax.all_to_all(value, axes, 0, 0)


def all_summed(mine, other):
    came = lax.ppermute(other, "core", [(0, 1), (1, 0)])
    chip = (mine + came.astype(jnp.float32)).astype(jnp.bfloat16).reshape(NEAR, PIECE, WIDTH)
    near = jnp.sum(exchange(chip, ("zl", "x")).astype(jnp.float32), axis=0).astype(jnp.bfloat16)
    far = exchange(jnp.broadcast_to(near[None], (ZH, PIECE, WIDTH)), "zh")
    piece = jnp.sum(far.astype(jnp.float32), axis=0).astype(jnp.bfloat16)
    half = exchange(jnp.broadcast_to(piece[None], (NEAR, PIECE, WIDTH)), ("zl", "x"))
    return lax.all_gather(half.reshape(HALF, WIDTH), "core", tiled=True)


def shards(initial_trial_state, left_ops, right_ops, pair_sectors, sector_size, left_env):
    x0 = initial_trial_state[0]
    left = left_ops[0, 0]
    right = right_ops[0, 0]
    live = pair_sectors[0, 0]
    sizes = sector_size[0]
    env = left_env[0]
    core = lax.axis_index("core")
    sector = lax.axis_index(("zh", "zl", "x", "core")) // (PAIRS // NSEC)
    meta = jnp.stack([core, sector]).astype(jnp.int32)

    mine, other = pair_call(first_kernel, 0, [], [PACKED])(meta, sizes, live, x0, left, right, env)
    sigma = all_summed(mine, other)
    mine, other, x = pair_call(
        next_kernel, 1, [shape((NSEC, WIDTH, WIDTH), jnp.float32)], [PACKED, PACKED, BLOCKS]
    )(meta, sizes, live, x0, sigma, left, right, env)
    sigma = all_summed(mine, other)
    psi, renorm = pl.pallas_call(
        last_kernel,
        in_specs=[SCALARS] + [WHOLE] * 3,
        out_specs=[WHOLE] * 2,
        out_shape=[shape((NSEC, WIDTH, WIDTH), jnp.bfloat16)] * 2,
        scratch_shapes=[PACKED, BLOCKS],
        compiler_params=PARAMS,
    )(sizes, x, sigma, env)
    part = NSEC // 2
    sent = lax.dynamic_slice_in_dim(renorm, core * part, part, 0)
    positions = lax.axis_size("sweep")
    came = lax.ppermute(sent, "sweep", [(i, i + 1) for i in range(positions - 1)])
    came = lax.all_gather(came, "core", tiled=True)
    next_left = (env.astype(jnp.float32) + came.astype(jnp.float32)).astype(jnp.bfloat16)
    return psi[None], next_left[None]


def solution(mesh):
    positions = mesh.shape["sweep"]
    split = Mesh(
        mesh.devices.reshape(positions, ZH, ZL, X, 2), ("sweep", "zh", "zl", "x", "core")
    )
    ops = ("zh", "zl", "x", "core")
    return jax.shard_map(
        shards,
        mesh=split,
        in_specs=(
            P("sweep", None, None, None),
            P("sweep", ops, None, None, None),
            P("sweep", ops, None, None, None),
            P("sweep", ops, None),
            P("sweep", None),
            P("sweep", None, None, None),
        ),
        out_specs=(P("sweep", None, None, None), P("sweep", None, None, None)),
        check_vma=False,
    )
```

time: 787 us -> 216 us (0.27)
  waiting for transfers between devices: 722 us -> 38.3 us
  blocking collectives: 0 us -> 102 us
  Pallas kernels: 0 us -> 31.6 us
  matrix products: 29.6 us -> 0 us
  local copies, waits for them, and re-layouts: 0.03 us -> 12 us
  other arithmetic: 13.5 us -> 4.17 us
  starting transfers between devices: 1.37 us -> 10.5 us
    psum x2 -> x0, waiting for transfers between devices: 698 us -> none  [shards(): lax.psum(pair_terms(left, right_environment, live, xb), 'ops')]
    all_to_all x0 -> x5, blocking collectives: none -> 89.2 us  [exchange(): return lax.all_to_all(value, axes, 0, 0)]
    pallas_call x0 -> x3, Pallas kernels: none -> 31.6 us  [the longest x1 12.8 us: shards(): pair_call(next_kernel, 1, [shape((NSEC, WIDTH, WIDTH), jnp.float32)], [PA...]
    dot_general x7 -> x0, matrix products: 29.6 us -> none  [the longest x2 9.03 us: shards(): jnp.einsum('iab,ibc->iac', env, xb, preferred_element_type=jnp.float32)]
    all_gather x0 -> x2, blocking collectives: none -> 12.8 us  [all_summed(): return lax.all_gather(half.reshape(HALF, WIDTH), 'core', tiled=True)]
    all_gather x0 -> x1, waiting for transfers between devices: none -> 12 us  [shards(): came = lax.all_gather(came, 'core', tiled=True)]
    all_to_all x0 -> x1, waiting for transfers between devices: none -> 9.94 us  [exchange(): return lax.all_to_all(value, axes, 0, 0)]
    unnamed x10 -> x30, local copies, waits for them, and re-layouts: 0.03 us -> 9.59 us
  transfers between devices with their start and end apart: 3 -> 5, of which waited for: 3 -> 5; matrix products, arithmetic and copies ran while one was open for 0% -> 0% of each run, Pallas kernels for 0% -> 0%
where the time goes in v1:
time: 216 us; the launch traced here: 213 us
  blocking collectives  102 us (47%)
  waiting for transfers between devices  38.3 us (18%)
  Pallas kernels  31.6 us (15%)
  between operations  14.2 us (7%)
  local copies, waits for them, and re-layouts  12 us (6%)
  starting transfers between devices  10.5 us (5%)
  other arithmetic  4.17 us (2%)
    all_to_all x5, blocking collectives, exchange(): return lax.all_to_all(value, axes, 0, 0)  89.2 us
    ppermute x1, waiting for transfers between devices, shards(): lax.ppermute(sent, 'sweep', [(i, i + 1) for i in range(positions - 1)])  13.7 us
    all_gather x2, blocking collectives, all_summed(): return lax.all_gather(half.reshape(HALF, WIDTH), 'core', tiled=True)  12.8 us
    pallas_call x1, Pallas kernels, shards(): pair_call(next_kernel, 1, [shape((NSEC, WIDTH, WIDTH), jnp.float32)], [PA...  12.8 us
    all_gather x1, waiting for transfers between devices, shards(): came = lax.all_gather(came, 'core', tiled=True)  12 us
    pallas_call x1, Pallas kernels, shards(): pair_call(first_kernel, 0, [], [PACKED])  11.6 us
    all_to_all x1, waiting for transfers between devices, exchange(): return lax.all_to_all(value, axes, 0, 0)  9.94 us
    unnamed x30, local copies, waits for them, and re-layouts  9.59 us
  transfers between devices with their start and end apart: 5, of which 5 were waited for; matrix products, arithmetic and copies ran while one was open for 0% of the time, Pallas kernels for 0%

profile of v1, /device:TPU:25, one launch (start us, length us, event | category | flops | bytes accessed | tf_op | source)
XLA Modules:
  0.0 212.8 jit_solution(4919437211305755815)
XLA Ops:
  7.3 1.2 copy-done
  8.5 1.2 copy-done.2
  9.7 1.2 copy-done.4
  10.9 1.2 copy-done.6
  13.5 11.6 %shard_map.77 = (f32[1536,128]{1,0:T(8,128)S(1)}, bf16[1536,128]{1,0:T(8,128)(2,1)S(1)}) custom-call(s32[2]{0:T(128)S(1)} %pad_add_fusion.meta, s32[32]{0:T(128)S(1)} %bitcast.25, s32[32]{0:T(128)S(1)} %bitcast.28, bf16[32,128,128]{2,1,0:T(8,128)(2,1)S(1)} %bitcast.19, bf16[32,128,128]{2,1,0:T(8,128)(2,1)S(1)} %bitcast.21, ...), custom_call_target="tpu_custom_call" | custom-call | tf_op jit(solution)/shard_map/pallas_call | solution.py:179
  25.1 2.6 %collective-permute-start = (bf16[1536,128]{1,0:T(8,128)(2,1)S(1)}, bf16[1536,128]{1,0:T(8,128)(2,1)S(1)}, u32[]{:S(2)}, u32[]{:S(2)}) collective-permute-start(bf16[1536,128]{1,0:T(8,128)(2,1)S(1)} %get-tuple-element.10), channel_id=1, source_target_pairs={{0,1},{1,0},{2,3},{3,2},{4,5},{5,4},{6,7},{7,6},{8,9},{9,8},{10,11... | collective-permute-start | bytes 1179656 | tf_op jit(solution)/shard_map/ppermute | solution.py:159
  27.7 1.3 collective-permute-done
  29.1 20.2 %all_to_all.30 = bf16[16,96,128]{2,1,0:T(8,128)(2,1)S(1)} all-to-all(bf16[16,96,128]{2,1,0:T(8,128)(2,1)S(1)} %bitcast.31), channel_id=1, replica_groups=mesh['sweep'=4,'zh'=4,'zl'=4,'x'=4,'core'=2] {'zl','x'}, dimensions={0} | all-to-all | bytes 786432 | tf_op jit(solution)/shard_map/all_to_all | solution.py:155
  49.3 0.7 reduce_sum.48
  50.0 0.8 broadcast_in_dim.12
  50.7 24.5 %all_to_all.31 = bf16[4,96,128]{2,1,0:T(8,128)(2,1)S(1)} all-to-all(bf16[4,96,128]{2,1,0:T(8,128)(2,1)S(1)} %broadcast_in_dim.12), channel_id=1, replica_groups=mesh['sweep'=4,'zh'=4,'zl'=4,'x'=4,'core'=2] {'zh'}, dimensions={0} | all-to-all | bytes 196608 | tf_op jit(solution)/shard_map/all_to_all | solution.py:155
  75.3 14.1 %all_to_all.32 = bf16[16,96,128]{2,1,0:T(8,128)(2,1)S(1)} all-to-all(bf16[16,96,128]{2,1,0:T(8,128)(2,1)S(1)} %broadcast_in_dim.13), channel_id=1, replica_groups=mesh['sweep'=4,'zh'=4,'zl'=4,'x'=4,'core'=2] {'zl','x'}, dimensions={0} | all-to-all | bytes 786432 | tf_op jit(solution)/shard_map/all_to_all | solution.py:155
  89.5 6.4 %all_gather.9.sigma = bf16[3072,128]{1,0:T(8,128)(2,1)S(1)} all-gather(bf16[1536,128]{1,0:T(8,128)(2,1)S(1)} %bitcast.33), channel_id=1, replica_groups=mesh['sweep'=4,'zh'=4,'zl'=4,'x'=4,'core'=2] {'core'}, dimensions={0}, use_global_device_ids=true | all-gather | bytes 1179648 | tf_op jit(solution)/shard_map/all_gather | solution.py:165
  95.9 1.2 copy-done.7
  97.1 12.8 %shard_map.78 = (f32[1536,128]{1,0:T(8,128)S(1)}, bf16[1536,128]{1,0:T(8,128)(2,1)S(1)}, f32[32,128,128]{2,1,0:T(8,128)S(1)}) custom-call(s32[2]{0:T(128)S(1)} %pad_add_fusion.meta, s32[32]{0:T(128)S(1)} %bitcast.26, s32[32]{0:T(128)S(1)} %bitcast.29, bf16[32,128,128]{2,1,0:T(8,128)(2,1)S(1)} %bitcast.20, bf16[3072,128]{1,0:T(8,128)(2,1)S(1)} %all_gather.9.sigma, ...), custom_call_target="tpu_custom_call" | custom-call | tf_op jit(solution)/shard_map/pallas_call | solution.py:181
  109.9 1.3 copy-done.8
  111.3 2.3 %collective-permute-start.1 = (bf16[1536,128]{1,0:T(8,128)(2,1)S(1)}, bf16[1536,128]{1,0:T(8,128)(2,1)S(1)}, u32[]{:S(2)}, u32[]{:S(2)}) collective-permute-start(bf16[1536,128]{1,0:T(8,128)(2,1)S(1)} %get-tuple-element.13), channel_id=1, source_target_pairs={{0,1},{1,0},{2,3},{3,2},{4,5},{5,4},{6,7},{7,6},{8,9},{9,8},{10,11... | collective-permute-start | bytes 1179656 | tf_op jit(solution)/shard_map/ppermute | solution.py:159
  113.5 1.3 collective-permute-done.1
  115.0 15.3 %all_to_all.33 = bf16[16,96,128]{2,1,0:T(8,128)(2,1)S(1)} all-to-all(bf16[16,96,128]{2,1,0:T(8,128)(2,1)S(1)} %bitcast.32), channel_id=1, replica_groups=mesh['sweep'=4,'zh'=4,'zl'=4,'x'=4,'core'=2] {'zl','x'}, dimensions={0} | all-to-all | bytes 786432 | tf_op jit(solution)/shard_map/all_to_all | solution.py:155
  130.2 0.7 reduce_sum.50
  130.9 0.8 broadcast_in_dim.14
  131.7 15.1 %all_to_all.34 = bf16[4,96,128]{2,1,0:T(8,128)(2,1)S(1)} all-to-all(bf16[4,96,128]{2,1,0:T(8,128)(2,1)S(1)} %broadcast_in_dim.14), channel_id=1, replica_groups=mesh['sweep'=4,'zh'=4,'zl'=4,'x'=4,'core'=2] {'zh'}, dimensions={0} | all-to-all | bytes 196608 | tf_op jit(solution)/shard_map/all_to_all | solution.py:155
  146.8 0.8 broadcast_in_dim.15
  147.6 4.3 %all-to-all-start.5 = ((bf16[16,96,128]{2,1,0:T(8,128)(2,1)}), bf16[16,96,128]{2,1,0:T(8,128)(2,1)S(1)}, u32[]{:S(2)}, u32[]{:S(2)}) async-start(bf16[16,96,128]{2,1,0:T(8,128)(2,1)} %broadcast_in_dim.15), calls=%async_computation.5 | async-start | bytes 786432 | tf_op jit(solution)/shard_map/all_to_all | solution.py:155
  152.0 9.9 %all-to-all-done.5 = bf16[16,96,128]{2,1,0:T(8,128)(2,1)S(1)} async-done(((bf16[16,96,128]{2,1,0:T(8,128)(2,1)}), bf16[16,96,128]{2,1,0:T(8,128)(2,1)S(1)}, u32[]{:S(2)}, u32[]{:S(2)}) %all-to-all-start.5) | async-done | bytes 393248 | tf_op jit(solution)/shard_map/all_to_all | solution.py:155
  161.9 6.4 %all_gather.10.sigma = bf16[3072,128]{1,0:T(8,128)(2,1)S(1)} all-gather(bf16[1536,128]{1,0:T(8,128)(2,1)S(1)} %bitcast.30), channel_id=1, replica_groups=mesh['sweep'=4,'zh'=4,'zl'=4,'x'=4,'core'=2] {'core'}, dimensions={0}, use_global_device_ids=true | all-gather | bytes 1179648 | tf_op jit(solution)/shard_map/all_gather | solution.py:165
  168.3 7.2 %shard_map.79 = (bf16[32,128,128]{2,1,0:T(8,128)(2,1)}, bf16[32,128,128]{2,1,0:T(8,128)(2,1)S(1)}) custom-call(s32[32]{0:T(128)S(1)} %bitcast.27, f32[32,128,128]{2,1,0:T(8,128)S(1)} %copy-done.9, bf16[3072,128]{1,0:T(8,128)(2,1)S(1)} %all_gather.10.sigma, bf16[32,128,128]{2,1,0:T(8,128)(2,1)S(1)} %bitcast.18), custom_call_target="tpu_custom_call" | custom-call | tf_op jit(solution)/shard_map/pallas_call | solution.py:185
  175.6 1.3 collective-permute-start.2
  176.9 13.7 %collective-permute-done.2 = bf16[16,128,128]{2,1,0:T(8,128)(2,1)S(1)} collective-permute-done((bf16[16,128,128]{2,1,0:T(8,128)(2,1)S(1)}, bf16[16,128,128]{2,1,0:T(8,128)(2,1)S(1)}, u32[]{:S(2)}, u32[]{:S(2)}) %collective-permute-start.2) | collective-permute-done | bytes 524320 | tf_op jit(solution)/shard_map/ppermute | solution.py:196
  190.6 0.8 copy-done.14
  191.4 12.0 %all-gather.2.cloned.1.call-done = bf16[32,128,128]{2,1,0:T(8,128)(2,1)} async-done(((bf16[16,128,128]{2,1,0:T(8,128)(2,1)}), bf16[32,128,128]{2,1,0:T(8,128)(2,1)}) %all-gather.2.cloned.1.call-update) | async-done | bytes 1048592 | tf_op jit(solution)/shard_map/all_gather | solution.py:197
  203.4 2.6 %fusion = bf16[1,32,128,128]{3,2,1,0:T(8,128)(2,1)} fusion(bf16[32,128,128]{2,1,0:T(8,128)(2,1)} %all-gather.2.cloned.1.call-done, bf16[1,32,128,128]{3,2,1,0:T(8,128)(2,1)S(1)} %copy-done.1), kind=kLoop, calls=%fused_computation.1 | loop fusion | flops 2097152 | bytes 3145728 | tf_op jit(solution)/shard_map/broadcast_in_dim | solution.py:199
  (32 shorter events, 1.8 us)
Async XLA Ops:
  7.3 1.2 copy-start
  8.5 1.2 copy-start.2
  9.7 1.2 copy-start.4
  10.9 1.2 copy-start.6
  12.2 0.7 copy-start.10
  12.8 0.7 copy-start.12
  25.1 3.9 %collective-permute-start = (bf16[1536,128]{1,0:T(8,128)(2,1)S(1)}, bf16[1536,128]{1,0:T(8,128)(2,1)S(1)}, u32[]{:S(2)}, u32[]{:S(2)}) collective-permute-start(bf16[1536,128]{1,0:T(8,128)(2,1)S(1)} %get-tuple-element.10), channel_id=1, source_target_pairs={{0,1},{1,0},{2,3},{3,2},{4,5},{5,4},{6,7},{7,6},{8,9},{9,8},{10,11... | collective-permute-start | bytes 1179656 | tf_op jit(solution)/shard_map/ppermute | solution.py:159
  29.1 66.8 %copy-start.1 = (bf16[1,32,128,128]{3,2,1,0:T(8,128)(2,1)S(1)}, bf16[1,32,128,128]{3,2,1,0:T(8,128)(2,1)}, u32[]{:S(2)}) copy-start(bf16[1,32,128,128]{3,2,1,0:T(8,128)(2,1)} %param.11) | copy-start | bytes 3145732
  29.1 66.8 %copy-start.3 = (bf16[1,32,128,128]{3,2,1,0:T(8,128)(2,1)S(1)}, bf16[1,32,128,128]{3,2,1,0:T(8,128)(2,1)}, u32[]{:S(2)}) copy-start(bf16[1,32,128,128]{3,2,1,0:T(8,128)(2,1)} %param.6) | copy-start | bytes 3145732
  29.1 66.8 %copy-start.5 = (bf16[1,1,32,128,128]{4,3,2,1,0:T(8,128)(2,1)S(1)}, bf16[1,1,32,128,128]{4,3,2,1,0:T(8,128)(2,1)}, u32[]{:S(2)}) copy-start(bf16[1,1,32,128,128]{4,3,2,1,0:T(8,128)(2,1)} %param.7) | copy-start | bytes 3145732
  29.1 66.8 %copy-start.11 = (s32[1,32]{1,0:T(1,128)S(1)}, s32[1,32]{1,0:T(1,128)}, u32[]{:S(2)}) copy-start(s32[1,32]{1,0:T(1,128)} %param.10) | copy-start | bytes 388
  29.1 66.7 %copy-start.13 = (s32[1,1,32]{2,1,0:T(1,128)S(1)}, s32[1,1,32]{2,1,0:T(1,128)}, u32[]{:S(2)}) copy-start(s32[1,1,32]{2,1,0:T(1,128)} %param.9) | copy-start | bytes 388
  95.9 1.2 copy-start.7
  109.9 1.3 copy-start.8
  111.3 3.6 %collective-permute-start.1 = (bf16[1536,128]{1,0:T(8,128)(2,1)S(1)}, bf16[1536,128]{1,0:T(8,128)(2,1)S(1)}, u32[]{:S(2)}, u32[]{:S(2)}) collective-permute-start(bf16[1536,128]{1,0:T(8,128)(2,1)S(1)} %get-tuple-element.13), channel_id=1, source_target_pairs={{0,1},{1,0},{2,3},{3,2},{4,5},{5,4},{6,7},{7,6},{8,9},{9,8},{10,11... | collective-permute-start | bytes 1179656 | tf_op jit(solution)/shard_map/ppermute | solution.py:159
  115.0 53.3 %copy-start.9 = (f32[32,128,128]{2,1,0:T(8,128)S(1)}, f32[32,128,128]{2,1,0:T(8,128)}, u32[]{:S(2)}) copy-start(f32[32,128,128]{2,1,0:T(8,128)} %copy-done.8) | copy-start | bytes 6291460
  147.6 14.3 %all-to-all-start.5 = ((bf16[16,96,128]{2,1,0:T(8,128)(2,1)}), bf16[16,96,128]{2,1,0:T(8,128)(2,1)S(1)}, u32[]{:S(2)}, u32[]{:S(2)}) async-start(bf16[16,96,128]{2,1,0:T(8,128)(2,1)} %broadcast_in_dim.15), calls=%async_computation.5 | async-start | bytes 786432 | tf_op jit(solution)/shard_map/all_to_all | solution.py:155
  151.9 51.5 %all-gather.2.cloned.1.call-start = ((), (), s32[]{:S(2)}) async-start(), calls=%async_computation.6 | async-start | bytes 1572864 | tf_op jit(solution)/shard_map/all_gather | solution.py:197
  175.6 15.0 %collective-permute-start.2 = (bf16[16,128,128]{2,1,0:T(8,128)(2,1)S(1)}, bf16[16,128,128]{2,1,0:T(8,128)(2,1)S(1)}, u32[]{:S(2)}, u32[]{:S(2)}) collective-permute-start(bf16[16,128,128]{2,1,0:T(8,128)(2,1)S(1)} %constant_dynamic-slice_fusion), channel_id=1, source_target_pairs={{0,128},{128,256},{256,384},{1,129},{129,257},{257,385},{2,130},{1... | collective-permute-start | bytes 1572872 | tf_op jit(solution)/shard_map/ppermute | solution.py:196
  190.6 0.8 copy-start.14
Sparse Core Ops, SparseCore 0:
  191.5 11.8 all-gather.1

commit v2 on v1

v2 whole, which is shorter than its diff:
```python
import math

import jax
import jax.numpy as jnp
from jax import lax
from jax.experimental import pallas as pl
from jax.experimental.pallas import tpu as pltpu
from jax.sharding import Mesh, PartitionSpec as P

NSEC = 32
WIDTH = 128
PAIRS = 128
ROWS = 3 * NSEC * WIDTH // 4
HALF = ROWS // 2
TOTAL = NSEC * WIDTH * WIDTH
X, ZL, ZH = 4, 4, 4
NEAR = ZL * X
PIECE = HALF // NEAR
SCALE = 1.0 / math.sqrt(PAIRS)
GROUP = 8
GROUPS = NSEC // GROUP
TAIL = 16

VMEM = pl.BlockSpec(memory_space=pltpu.VMEM)
SMEM = pl.BlockSpec(memory_space=pltpu.SMEM)
HBM = pl.BlockSpec(memory_space=pltpu.HBM)
PACKED = pltpu.VMEM((ROWS + WIDTH, WIDTH), jnp.float32)
BLOCKS = pltpu.VMEM((NSEC, WIDTH, WIDTH), jnp.bfloat16)
SIZES = pltpu.SMEM((1, NSEC), jnp.int32)
PARAMS = pltpu.CompilerParams(vmem_limit_bytes=16 * 1024 * 1024)


def shape(dims, dtype):
    return jax.ShapeDtypeStruct(dims, dtype)


def square_mask(size):
    row = lax.broadcasted_iota(jnp.int32, (WIDTH, WIDTH), 0)
    col = lax.broadcasted_iota(jnp.int32, (WIDTH, WIDTH), 1)
    return (row < size) & (col < size)


def dot(a, b):
    return jnp.dot(a, b, preferred_element_type=jnp.float32)


def fold(value):
    return jnp.sum(value.reshape(WIDTH // 8, 8, WIDTH), axis=0)


def group_copies(pairs, sems):
    return [
        [
            pltpu.make_async_copy(
                source.at[pl.ds(g * GROUP, GROUP)], target.at[pl.ds(g * GROUP, GROUP)], sems.at[g, k]
            )
            for k, (source, target) in enumerate(pairs)
        ]
        for g in range(GROUPS)
    ]


def start_all(copies):
    for group in copies:
        for copy in group:
            copy.start()


def widened(packed, wide):
    wide[pl.ds(0, ROWS), :] = packed[...].astype(jnp.float32)
    wide[pl.ds(ROWS, WIDTH), :] = jnp.zeros((WIDTH, WIDTH), jnp.float32)


def block_of(wide, offset, mask):
    return jnp.where(mask, wide[pl.ds(offset, WIDTH), :], 0.0)


def step_factors(sizes, x_of, sigma, ready):
    zero = jnp.zeros((8, WIDTH), jnp.float32)
    offset, xx, xs, ss = 0, zero, zero, zero
    for g in range(GROUPS):
        ready(g)
        for i in range(g * GROUP, (g + 1) * GROUP):
            mask = square_mask(sizes[0, i])
            x = x_of(i, offset, mask)
            s = block_of(sigma, offset, mask)
            offset = offset + sizes[0, i]
            xx, xs, ss = xx + fold(x * x), xs + fold(x * s), ss + fold(s * s)
    xx, xs, ss = (jnp.sum(v, axis=(0, 1), keepdims=True) for v in (xx, xs, ss))
    rho = xs / xx
    yy = xx + 0.64 * jnp.maximum(ss - rho * xs, 0.0)
    shrink = 1.0 / jnp.sqrt(yy / TOTAL + 1e-06)
    return (1.0 + 0.8 * rho) * shrink, 0.8 * shrink


def run_pairs(meta, sizes, live, xb_of, left, right, env, ready, env_ready, packed, held, mine, other):
    sector = meta[1]

    def body(g, carry):
        offset, at, size_at = carry
        ready(g)
        sums = []
        place = offset
        for j in range(GROUP):
            i = g * GROUP + j
            size = sizes[0, i]
            xb = xb_of(i, place, square_mask(size))
            here = i == sector
            at = jnp.where(here, place, at)
            size_at = jnp.where(here, size, size_at)
            held[i] = xb
            place = place + size
            block = left[i]
            u = live[0, i].astype(jnp.float32) * dot(jnp.concatenate([block, block.T], 0), xb)
            u = u.astype(jnp.bfloat16)
            context = right[i]
            sums.append(
                SCALE
                * dot(
                    jnp.concatenate([u[:WIDTH], u[WIDTH:]], 1),
                    jnp.concatenate([context.T, context], 0),
                )
            )
        for j in range(GROUP):
            packed[pl.ds(offset, WIDTH), :] = sums[j]
            offset = offset + sizes[0, g * GROUP + j]
        return offset, at, size_at

    none = jnp.int32(0)
    _, at, size_at = lax.fori_loop(0, GROUPS, body, (none, none, none))
    env_ready()
    term = 0.25 * dot(env[...], held[sector])
    packed[pl.ds(at, WIDTH), :] += jnp.where(square_mask(size_at), term, 0.0)
    core = meta[0]
    mine[...] = packed[pl.ds(pl.multiple_of(core * HALF, 8), HALF), :]
    other[...] = packed[pl.ds(pl.multiple_of((1 - core) * HALF, 8), HALF), :].astype(jnp.bfloat16)


def scalars_in(sizes_in, live_in, sizes, live, sems):
    copies = [
        pltpu.make_async_copy(sizes_in, sizes, sems.at[0]),
        pltpu.make_async_copy(live_in, live, sems.at[1]),
    ]
    for copy in copies:
        copy.start()
    return copies


def first_kernel(
    meta, sizes_in, live_in, x0_in, left_in, right_in, env_in, mine, other,
    packed, held, x0, left, right, env, sizes, live, sems, own_sems,
):
    small = scalars_in(sizes_in, live_in, sizes, live, own_sems)
    pairs = [(x0_in, x0), (left_in, left), (right_in, right)]
    start_all(group_copies(pairs, sems))
    env_copy = pltpu.make_async_copy(env_in.at[meta[1]], env, own_sems.at[2])
    env_copy.start()
    for copy in small:
        copy.wait()

    def ready(g):
        some = pl.ds(g * GROUP, GROUP)
        for k, (source, target) in enumerate(pairs):
            pltpu.make_async_copy(source.at[some], target.at[some], sems.at[g, k]).wait()

    def xb_of(i, offset, mask):
        x = x0[i]
        return jnp.where(mask, x, jnp.zeros_like(x))

    run_pairs(
        meta, sizes, live, xb_of, left, right, env, ready, env_copy.wait, packed, held, mine, other
    )


def next_kernel(
    meta, sizes_in, live_in, sigma, x0_in, left_in, right_in, env_in, mine, other, factors,
    packed, held, x0, left, right, env, sizes, live, sems, own_sems, x_sems, wide,
):
    small = scalars_in(sizes_in, live_in, sizes, live, own_sems)
    x_copies = group_copies([(x0_in, x0)], x_sems)
    start_all(x_copies)
    pairs = [(left_in, left), (right_in, right)]
    start_all(group_copies(pairs, sems))
    env_copy = pltpu.make_async_copy(env_in.at[meta[1]], env, own_sems.at[2])
    env_copy.start()
    widened(sigma, wide)
    for copy in small:
        copy.wait()

    def x_of(i, offset, mask):
        return jnp.where(mask, x0[i].astype(jnp.float32), 0.0)

    grow, drop = step_factors(sizes, x_of, wide, lambda g: x_copies[g][0].wait())
    factors[0:1, :] = jnp.broadcast_to(grow, (1, WIDTH))
    factors[1:2, :] = jnp.broadcast_to(drop, (1, WIDTH))

    def ready(g):
        some = pl.ds(g * GROUP, GROUP)
        for k, (source, target) in enumerate(pairs):
            pltpu.make_async_copy(source.at[some], target.at[some], sems.at[g, k]).wait()

    def xb_of(i, offset, mask):
        x = grow * x0[i].astype(jnp.float32) - drop * wide[pl.ds(offset, WIDTH), :]
        return jnp.where(mask, x, 0.0).astype(jnp.bfloat16)

    run_pairs(
        meta, sizes, live, xb_of, left, right, env, ready, env_copy.wait, packed, held, mine, other
    )


def last_kernel(
    meta, sizes_in, factors, sigma_before, sigma, x0_in, env_in, psi_out, renorm_out,
    x0, env, psi, sizes, x_sems, env_sems, psi_sems, own_sems, before, wide, packed,
):
    sizes_copy = pltpu.make_async_copy(sizes_in, sizes, own_sems.at[0])
    sizes_copy.start()
    x_copies = group_copies([(x0_in, x0)], x_sems)
    start_all(x_copies)
    env_copies = group_copies([(env_in, env)], env_sems)
    start_all(env_copies)
    psi_copies = group_copies([(psi, psi_out)], psi_sems)
    widened(sigma_before, before)
    widened(sigma, wide)
    grow_before, drop_before = factors[0:1, :], factors[1:2, :]
    sizes_copy.wait()

    def x_of(i, offset, mask):
        x = grow_before * x0[i].astype(jnp.float32) - drop_before * before[pl.ds(offset, WIDTH), :]
        return jnp.where(mask, x, 0.0)

    grow, drop = step_factors(sizes, x_of, wide, lambda g: x_copies[g][0].wait())
    offset = 0
    for g in range(GROUPS):
        env_copies[g][0].wait()
        some = range(g * GROUP, (g + 1) * GROUP)
        blocks = []
        place = offset
        for i in some:
            mask = square_mask(sizes[0, i])
            new = grow * x_of(i, place, mask) - drop * block_of(wide, place, mask)
            new = new.astype(jnp.bfloat16)
            psi[i] = new
            place = place + sizes[0, i]
            applied = dot(env[i], new).astype(jnp.bfloat16)
            blocks.append(dot(new.T, applied) / math.sqrt(WIDTH))
        psi_copies[g][0].start()
        for i, block in zip(some, blocks):
            packed[pl.ds(offset, WIDTH), :] = block
            offset = offset + sizes[0, i]
    core = meta[0]
    renorm_out[pl.ds(0, HALF), :] = packed[
        pl.ds(pl.multiple_of(core * HALF, 8), HALF), :
    ].astype(jnp.bfloat16)
    lane = lax.broadcasted_iota(jnp.int32, (TAIL, WIDTH), 1)
    row = jnp.zeros((TAIL, WIDTH), jnp.int32)
    for i in range(NSEC):
        row = jnp.where(lane == i, sizes[0, i], row)
    renorm_out[pl.ds(HALF, TAIL), :] = row.astype(jnp.float32).astype(jnp.bfloat16)
    for copies in psi_copies:
        copies[0].wait()


def shift_kernel(came, env, out, wide, result, numbers, sizes, sems, own_sem):
    numbers[...] = came[pl.ds(HALF, 8), :].astype(jnp.float32).astype(jnp.int32)
    sizes_copy = pltpu.make_async_copy(numbers, sizes, own_sem.at[0])
    sizes_copy.start()
    wide[pl.ds(0, HALF), :] = came[pl.ds(0, HALF), :].astype(jnp.float32)
    wide[pl.ds(HALF, HALF), :] = came[pl.ds(HALF + TAIL, HALF), :].astype(jnp.float32)
    wide[pl.ds(ROWS, WIDTH), :] = jnp.zeros((WIDTH, WIDTH), jnp.float32)
    sizes_copy.wait()
    copies = group_copies([(result, out)], sems)
    offset = 0
    for g in range(GROUPS):
        for i in range(g * GROUP, (g + 1) * GROUP):
            block = block_of(wide, offset, square_mask(sizes[0, i]))
            result[i] = (env[i].astype(jnp.float32) + block).astype(jnp.bfloat16)
            offset = offset + sizes[0, i]
        copies[g][0].start()
    for group in copies:
        group[0].wait()


def sum_kernel(parts, out):
    total = jnp.sum(parts[...].astype(jnp.float32), axis=0).astype(jnp.bfloat16)
    for k in range(out.shape[0]):
        out[k] = total


def summed(parts, copies):
    return pl.pallas_call(
        sum_kernel,
        in_specs=[VMEM],
        out_specs=VMEM,
        out_shape=shape((copies,) + parts.shape[1:], parts.dtype),
    )(parts)


def exchange(value, axes):
    return lax.all_to_all(value, axes, 0, 0)


def all_summed(mine, other):
    came = lax.ppermute(other, "core", [(0, 1), (1, 0)])
    chip = (mine + came.astype(jnp.float32)).astype(jnp.bfloat16).reshape(NEAR, PIECE, WIDTH)
    near = summed(exchange(chip, ("zl", "x")), ZH)
    far = summed(exchange(near, "zh"), NEAR)
    half = exchange(far, ("zl", "x"))
    return lax.all_gather(half.reshape(HALF, WIDTH), "core", tiled=True)


def dma(*dims):
    return pltpu.SemaphoreType.DMA(dims)


def shards(initial_trial_state, left_ops, right_ops, pair_sectors, sector_size, left_env):
    x0 = initial_trial_state[0]
    left = left_ops[0, 0]
    right = right_ops[0, 0]
    live = pair_sectors[0]
    sizes = sector_size
    env = left_env[0]
    core = lax.axis_index("core")
    sector = lax.axis_index(("zh", "zl", "x", "core")) // (PAIRS // NSEC)
    meta = jnp.stack([core, sector]).astype(jnp.int32)

    sums = [shape((HALF, WIDTH), jnp.float32), shape((HALF, WIDTH), jnp.bfloat16)]
    scratch = [PACKED, BLOCKS, BLOCKS, BLOCKS, BLOCKS, pltpu.VMEM((WIDTH, WIDTH), jnp.bfloat16)]
    scratch += [SIZES, SIZES]
    mine, other = pl.pallas_call(
        first_kernel,
        in_specs=[SMEM] + [HBM] * 6,
        out_specs=[VMEM] * 2,
        out_shape=sums,
        scratch_shapes=scratch + [dma(GROUPS, 3), dma(3)],
        compiler_params=PARAMS,
    )(meta, sizes, live, x0, left, right, env)
    before = all_summed(mine, other)
    mine, other, factors = pl.pallas_call(
        next_kernel,
        in_specs=[SMEM, HBM, HBM, VMEM] + [HBM] * 4,
        out_specs=[VMEM] * 3,
        out_shape=sums + [shape((2, WIDTH), jnp.float32)],
        scratch_shapes=scratch + [dma(GROUPS, 2), dma(3), dma(GROUPS, 1), PACKED],
        compiler_params=PARAMS,
    )(meta, sizes, live, before, x0, left, right, env)
    sigma = all_summed(mine, other)
    psi, renorm = pl.pallas_call(
        last_kernel,
        in_specs=[SMEM, HBM] + [VMEM] * 3 + [HBM] * 2,
        out_specs=[HBM, VMEM],
        out_shape=[
            shape((NSEC, WIDTH, WIDTH), jnp.bfloat16),
            shape((HALF + TAIL, WIDTH), jnp.bfloat16),
        ],
        scratch_shapes=[BLOCKS, BLOCKS, BLOCKS, SIZES]
        + [dma(GROUPS, 1), dma(GROUPS, 1), dma(GROUPS, 1), dma(1), PACKED, PACKED, PACKED],
        compiler_params=PARAMS,
    )(meta, sizes, factors, before, sigma, x0, env)
    positions = lax.axis_size("sweep")
    came = lax.ppermute(renorm, "sweep", [(i, i + 1) for i in range(positions - 1)])
    came = lax.all_gather(came, "core", tiled=True)
    next_left = pl.pallas_call(
        shift_kernel,
        in_specs=[VMEM] * 2,
        out_specs=HBM,
        out_shape=shape((NSEC, WIDTH, WIDTH), jnp.bfloat16),
        scratch_shapes=[
            PACKED,
            BLOCKS,
            pltpu.VMEM((8, WIDTH), jnp.int32),
            pltpu.SMEM((8, WIDTH), jnp.int32),
            dma(GROUPS, 1),
            dma(1),
        ],
        compiler_params=PARAMS,
    )(came, env)
    return psi[None], next_left[None]


def solution(mesh):
    positions = mesh.shape["sweep"]
    split = Mesh(
        mesh.devices.reshape(positions, ZH, ZL, X, 2), ("sweep", "zh", "zl", "x", "core")
    )
    ops = ("zh", "zl", "x", "core")
    return jax.shard_map(
        shards,
        mesh=split,
        in_specs=(
            P("sweep", None, None, None),
            P("sweep", ops, None, None, None),
            P("sweep", ops, None, None, None),
            P("sweep", ops, None),
            P("sweep", None),
            P("sweep", None, None, None),
        ),
        out_specs=(P("sweep", None, None, None), P("sweep", None, None, None)),
        check_vma=False,
    )
```

time: 216 us -> 173 us (0.80)
  waiting for transfers between devices: 38.3 us -> 13.7 us
  blocking collectives: 102 us -> 121 us
  between operations: 14.2 us -> 0.72 us
  Pallas kernels: 31.6 us -> 22 us
  starting transfers between devices: 10.5 us -> 6.16 us
  local copies, waits for them, and re-layouts: 12 us -> 8.02 us
  other arithmetic: 4.17 us -> 0.23 us
    all_to_all x5 -> x6, blocking collectives: 89.2 us -> 105 us  [exchange(): return lax.all_to_all(value, axes, 0, 0)]
    all_gather x1 -> x0, waiting for transfers between devices: 12 us -> none  [shards(): came = lax.all_gather(came, 'core', tiled=True)]
    all_to_all x1 -> x0, waiting for transfers between devices: 9.94 us -> none  [exchange(): return lax.all_to_all(value, axes, 0, 0)]
    pallas_call x3 -> x8, Pallas kernels: 31.6 us -> 22 us  [the longest x4 6.81 us: summed(): pl.pallas_call(sum_kernel, in_specs=[VMEM], out_specs=VMEM, out_shape=sha...]
    all_to_all x1 -> x0, starting transfers between devices: 4.32 us -> none  [exchange(): return lax.all_to_all(value, axes, 0, 0)]
    all_gather x0 -> x1, blocking collectives: none -> 3.19 us  [shards(): came = lax.all_gather(came, 'core', tiled=True)]
    ppermute x1, waiting for transfers between devices: 13.7 us -> 11 us  [shards(): lax.ppermute(renorm, 'sweep', [(i, i + 1) for i in range(positions - 1)])]
    broadcast_in_dim x1 -> x0, other arithmetic: 2.57 us -> none  [shards(): return (psi[None], next_left[None])]
  transfers between devices with their start and end apart: 5 -> 3, of which waited for: 5 -> 3; matrix products, arithmetic and copies ran while one was open for 0% -> 0% of each run, Pallas kernels for 0% -> 0%
where the time goes in v2:
time: 173 us; the launch traced here: 172 us
  blocking collectives  121 us (70%)
  Pallas kernels  22 us (13%)
  waiting for transfers between devices  13.7 us (8%)
  local copies, waits for them, and re-layouts  8.02 us (5%)
  starting transfers between devices  6.16 us (4%)
    all_to_all x6, blocking collectives, exchange(): return lax.all_to_all(value, axes, 0, 0)  105 us
    all_gather x2, blocking collectives, all_summed(): return lax.all_gather(half.reshape(HALF, WIDTH), 'core', tiled=True)  12.5 us
    ppermute x1, waiting for transfers between devices, shards(): lax.ppermute(renorm, 'sweep', [(i, i + 1) for i in range(positions - 1)])  11 us
    unnamed x20, local copies, waits for them, and re-layouts  8.02 us
    pallas_call x4, Pallas kernels, summed(): pl.pallas_call(sum_kernel, in_specs=[VMEM], out_specs=VMEM, out_shape=sha...  6.81 us
    ppermute x2, starting transfers between devices, all_summed(): came = lax.ppermute(other, 'core', [(0, 1), (1, 0)])  4.87 us
    pallas_call x1, Pallas kernels, shards(): pl.pallas_call(last_kernel, in_specs=[SMEM, HBM] + [VMEM] * 3 + [HBM] * 2...  4.84 us
    pallas_call x1, Pallas kernels, shards(): pl.pallas_call(next_kernel, in_specs=[SMEM, HBM, HBM, VMEM] + [HBM] * 4,...  4.84 us
  transfers between devices with their start and end apart: 3, of which 3 were waited for; matrix products, arithmetic and copies ran while one was open for 0% of the time, Pallas kernels for 0%

profile of v2, /device:TPU:25, one launch (start us, length us, event | category | flops | bytes accessed | tf_op | source)
XLA Modules:
  0.0 171.9 jit_solution(6216962239086341190)
XLA Ops:
  0.7 0.7 copy-done.8
  1.4 1.2 copy-done
  2.6 1.2 copy-done.2
  3.8 1.2 copy-done.4
  5.1 1.2 copy-done.6
  6.3 3.8 %shard_map.77 = (f32[1536,128]{1,0:T(8,128)S(1)}, bf16[1536,128]{1,0:T(8,128)(2,1)S(1)}) custom-call(s32[2]{0:T(128)S(1)} %pad_add_fusion.meta, s32[1,32]{1,0:T(1,128)S(1)} %copy-done.8, s32[1,32]{1,0:T(1,128)S(1)} %bitcast.24, bf16[32,128,128]{2,1,0:T(8,128)(2,1)S(1)} %bitcast.17, bf16[32,128,128]{2,1,0:T(8,128)(2,1)S(1)} %bitcast.20, ...), custom_call_target="tpu_custom_call" | custom-call | tf_op jit(solution)/shard_map/pallas_call | solution.py:329
  10.1 2.6 %collective-permute-start = (bf16[1536,128]{1,0:T(8,128)(2,1)S(1)}, bf16[1536,128]{1,0:T(8,128)(2,1)S(1)}, u32[]{:S(2)}, u32[]{:S(2)}) collective-permute-start(bf16[1536,128]{1,0:T(8,128)(2,1)S(1)} %get-tuple-element.10), channel_id=1, source_target_pairs={{0,1},{1,0},{2,3},{3,2},{4,5},{5,4},{6,7},{7,6},{8,9},{9,8},{10,11... | collective-permute-start | bytes 1179656 | tf_op jit(solution)/shard_map/ppermute | solution.py:303
  12.7 1.3 collective-permute-done
  14.0 0.1 add_convert_fusion.1
  14.1 20.0 %all_to_all.30.parts = bf16[16,96,128]{2,1,0:T(8,128)(2,1)} all-to-all(bf16[16,96,128]{2,1,0:T(8,128)(2,1)S(1)} %bitcast.26), channel_id=1, replica_groups=mesh['sweep'=4,'zh'=4,'zl'=4,'x'=4,'core'=2] {'zl','x'}, dimensions={0} | all-to-all | bytes 786432 | tf_op jit(solution)/shard_map/all_to_all | solution.py:299
  34.1 1.7 shard_map.78
  35.8 24.8 %all_to_all.31.parts = bf16[4,96,128]{2,1,0:T(8,128)(2,1)} all-to-all(bf16[4,96,128]{2,1,0:T(8,128)(2,1)} %shard_map.78), channel_id=1, replica_groups=mesh['sweep'=4,'zh'=4,'zl'=4,'x'=4,'core'=2] {'zh'}, dimensions={0} | all-to-all | bytes 196608 | tf_op jit(solution)/shard_map/all_to_all | solution.py:299
  60.6 1.8 %shard_map.79 = bf16[16,96,128]{2,1,0:T(8,128)(2,1)} custom-call(bf16[4,96,128]{2,1,0:T(8,128)(2,1)} %all_to_all.31.parts), custom_call_target="tpu_custom_call" | custom-call | tf_op jit(solution)/shard_map/pallas_call | solution.py:290
  62.4 14.4 %all_to_all.32 = bf16[16,96,128]{2,1,0:T(8,128)(2,1)S(1)} all-to-all(bf16[16,96,128]{2,1,0:T(8,128)(2,1)} %shard_map.79), channel_id=1, replica_groups=mesh['sweep'=4,'zh'=4,'zl'=4,'x'=4,'core'=2] {'zl','x'}, dimensions={0} | all-to-all | bytes 786432 | tf_op jit(solution)/shard_map/all_to_all | solution.py:299
  76.8 6.4 %all_gather.9.sigma.sigma_before = bf16[3072,128]{1,0:T(8,128)(2,1)S(1)} all-gather(bf16[1536,128]{1,0:T(8,128)(2,1)S(1)} %bitcast.28), channel_id=1, replica_groups=mesh['sweep'=4,'zh'=4,'zl'=4,'x'=4,'core'=2] {'core'}, dimensions={0}, use_global_device_ids=true | all-gather | bytes 1179648 | tf_op jit(solution)/shard_map/all_gather | solution.py:308
  83.2 1.2 copy-done.5
  84.5 1.2 copy-done.7
  85.7 4.8 %shard_map.80 = (f32[1536,128]{1,0:T(8,128)S(1)}, bf16[1536,128]{1,0:T(8,128)(2,1)S(1)}, f32[2,128]{1,0:T(2,128)S(1)}) custom-call(s32[2]{0:T(128)S(1)} %pad_add_fusion.meta, s32[1,32]{1,0:T(1,128)S(1)} %copy-done.8, s32[1,32]{1,0:T(1,128)S(1)} %bitcast.25, bf16[3072,128]{1,0:T(8,128)(2,1)S(1)} %all_gather.9.sigma.sigma_before, ...), custom_call_target="tpu_custom_call" | custom-call | tf_op jit(solution)/shard_map/pallas_call | solution.py:338
  90.5 2.3 %collective-permute-start.1 = (bf16[1536,128]{1,0:T(8,128)(2,1)S(1)}, bf16[1536,128]{1,0:T(8,128)(2,1)S(1)}, u32[]{:S(2)}, u32[]{:S(2)}) collective-permute-start(bf16[1536,128]{1,0:T(8,128)(2,1)S(1)} %get-tuple-element.13), channel_id=1, source_target_pairs={{0,1},{1,0},{2,3},{3,2},{4,5},{5,4},{6,7},{7,6},{8,9},{9,8},{10,11... | collective-permute-start | bytes 1179656 | tf_op jit(solution)/shard_map/ppermute | solution.py:303
  92.8 1.3 collective-permute-done.1
  94.1 0.1 add_convert_fusion
  94.2 15.3 %all_to_all.33.parts = bf16[16,96,128]{2,1,0:T(8,128)(2,1)} all-to-all(bf16[16,96,128]{2,1,0:T(8,128)(2,1)S(1)} %bitcast.27), channel_id=1, replica_groups=mesh['sweep'=4,'zh'=4,'zl'=4,'x'=4,'core'=2] {'zl','x'}, dimensions={0} | all-to-all | bytes 786432 | tf_op jit(solution)/shard_map/all_to_all | solution.py:299
  109.5 1.7 shard_map.81
  111.2 17.4 %all_to_all.34.parts = bf16[4,96,128]{2,1,0:T(8,128)(2,1)} all-to-all(bf16[4,96,128]{2,1,0:T(8,128)(2,1)} %shard_map.81), channel_id=1, replica_groups=mesh['sweep'=4,'zh'=4,'zl'=4,'x'=4,'core'=2] {'zh'}, dimensions={0} | all-to-all | bytes 196608 | tf_op jit(solution)/shard_map/all_to_all | solution.py:299
  128.5 1.7 shard_map.82
  130.2 13.5 %all_to_all.35 = bf16[16,96,128]{2,1,0:T(8,128)(2,1)S(1)} all-to-all(bf16[16,96,128]{2,1,0:T(8,128)(2,1)} %shard_map.82), channel_id=1, replica_groups=mesh['sweep'=4,'zh'=4,'zl'=4,'x'=4,'core'=2] {'zl','x'}, dimensions={0} | all-to-all | bytes 786432 | tf_op jit(solution)/shard_map/all_to_all | solution.py:299
  143.7 6.1 %all_gather.10.sigma = bf16[3072,128]{1,0:T(8,128)(2,1)S(1)} all-gather(bf16[1536,128]{1,0:T(8,128)(2,1)S(1)} %bitcast.29), channel_id=1, replica_groups=mesh['sweep'=4,'zh'=4,'zl'=4,'x'=4,'core'=2] {'core'}, dimensions={0}, use_global_device_ids=true | all-gather | bytes 1179648 | tf_op jit(solution)/shard_map/all_gather | solution.py:308
  149.8 4.8 %shard_map.83 = (bf16[32,128,128]{2,1,0:T(8,128)(2,1)}, bf16[1552,128]{1,0:T(8,128)(2,1)S(1)}) custom-call(s32[2]{0:T(128)S(1)} %pad_add_fusion.meta, s32[1,32]{1,0:T(1,128)S(1)} %copy-done.8, f32[2,128]{1,0:T(2,128)S(1)} %get-tuple-element.11.factors, bf16[3072,128]{1,0:T(8,128)(2,1)S(1)} %all_gather.9.sigma.sigma_before, ...), custom_call_target="tpu_custom_call" | custom-call | tf_op jit(solution)/shard_map/pallas_call | solution.py:347
  154.6 1.3 collective-permute-start.2
  155.9 11.0 %collective-permute-done.2 = bf16[1552,128]{1,0:T(8,128)(2,1)S(1)} collective-permute-done((bf16[1552,128]{1,0:T(8,128)(2,1)S(1)}, bf16[1552,128]{1,0:T(8,128)(2,1)S(1)}, u32[]{:S(2)}, u32[]{:S(2)}) %collective-permute-start.2) | collective-permute-done | bytes 397344 | tf_op jit(solution)/shard_map/ppermute | solution.py:360
  166.9 3.2 %all_gather.11.came = bf16[3104,128]{1,0:T(8,128)(2,1)S(1)} all-gather(bf16[1552,128]{1,0:T(8,128)(2,1)S(1)} %collective-permute-done.2), channel_id=1, replica_groups=mesh['sweep'=4,'zh'=4,'zl'=4,'x'=4,'core'=2] {'core'}, dimensions={0}, use_global_device_ids=true | all-gather | bytes 1191936 | tf_op jit(solution)/shard_map/all_gather | solution.py:361
  170.1 1.8 %shard_map.84 = bf16[32,128,128]{2,1,0:T(8,128)(2,1)} custom-call(bf16[3104,128]{1,0:T(8,128)(2,1)S(1)} %all_gather.11.came, bf16[32,128,128]{2,1,0:T(8,128)(2,1)S(1)} %bitcast.16), custom_call_target="tpu_custom_call" | custom-call | tf_op jit(solution)/shard_map/pallas_call | solution.py:362
  (14 shorter events, 0.1 us)
Async XLA Ops:
  0.7 0.7 copy-start.8
  0.7 0.7 copy-start.9
  1.4 1.2 copy-start
  2.6 1.2 copy-start.2
  3.8 1.2 copy-start.4
  5.1 1.2 copy-start.6
  10.1 3.9 %collective-permute-start = (bf16[1536,128]{1,0:T(8,128)(2,1)S(1)}, bf16[1536,128]{1,0:T(8,128)(2,1)S(1)}, u32[]{:S(2)}, u32[]{:S(2)}) collective-permute-start(bf16[1536,128]{1,0:T(8,128)(2,1)S(1)} %get-tuple-element.10), channel_id=1, source_target_pairs={{0,1},{1,0},{2,3},{3,2},{4,5},{5,4},{6,7},{7,6},{8,9},{9,8},{10,11... | collective-permute-start | bytes 1179656 | tf_op jit(solution)/shard_map/ppermute | solution.py:303
  60.6 22.6 %copy-start.3 = (bf16[1,32,128,128]{3,2,1,0:T(8,128)(2,1)S(1)}, bf16[1,32,128,128]{3,2,1,0:T(8,128)(2,1)}, u32[]{:S(2)}) copy-start(bf16[1,32,128,128]{3,2,1,0:T(8,128)(2,1)} %param.6) | copy-start | bytes 3145732
  62.4 20.9 %copy-start.1 = (bf16[1,32,128,128]{3,2,1,0:T(8,128)(2,1)S(1)}, bf16[1,32,128,128]{3,2,1,0:T(8,128)(2,1)}, u32[]{:S(2)}) copy-start(bf16[1,32,128,128]{3,2,1,0:T(8,128)(2,1)} %param.11) | copy-start | bytes 3145732
  83.2 1.2 copy-start.5
  84.5 1.2 copy-start.7
  90.5 3.6 %collective-permute-start.1 = (bf16[1536,128]{1,0:T(8,128)(2,1)S(1)}, bf16[1536,128]{1,0:T(8,128)(2,1)S(1)}, u32[]{:S(2)}, u32[]{:S(2)}) collective-permute-start(bf16[1536,128]{1,0:T(8,128)(2,1)S(1)} %get-tuple-element.13), channel_id=1, source_target_pairs={{0,1},{1,0},{2,3},{3,2},{4,5},{5,4},{6,7},{7,6},{8,9},{9,8},{10,11... | collective-permute-start | bytes 1179656 | tf_op jit(solution)/shard_map/ppermute | solution.py:303
  154.6 12.3 %collective-permute-start.2 = (bf16[1552,128]{1,0:T(8,128)(2,1)S(1)}, bf16[1552,128]{1,0:T(8,128)(2,1)S(1)}, u32[]{:S(2)}, u32[]{:S(2)}) collective-permute-start(bf16[1552,128]{1,0:T(8,128)(2,1)S(1)} %get-tuple-element.15), channel_id=1, source_target_pairs={{0,128},{128,256},{256,384},{1,129},{129,257},{257,385},{2,130},{1... | collective-permute-start | bytes 1191944 | tf_op jit(solution)/shard_map/ppermute | solution.py:360

commit v3 on v2

--- a/solution.py
+++ b/solution.py
@@ -27,7 +27,10 @@
 PACKED = pltpu.VMEM((ROWS + WIDTH, WIDTH), jnp.float32)
 BLOCKS = pltpu.VMEM((NSEC, WIDTH, WIDTH), jnp.bfloat16)
 SIZES = pltpu.SMEM((1, NSEC), jnp.int32)
-PARAMS = pltpu.CompilerParams(vmem_limit_bytes=16 * 1024 * 1024)
+
+
+def limit(mib):
+    return pltpu.CompilerParams(vmem_limit_bytes=mib * 1024 * 1024)
 
 
 def shape(dims, dtype):
@@ -292,6 +295,7 @@
         in_specs=[VMEM],
         out_specs=VMEM,
         out_shape=shape((copies,) + parts.shape[1:], parts.dtype),
+        compiler_params=limit(4),
     )(parts)
 
 
@@ -332,7 +336,7 @@
         out_specs=[VMEM] * 2,
         out_shape=sums,
         scratch_shapes=scratch + [dma(GROUPS, 3), dma(3)],
-        compiler_params=PARAMS,
+        compiler_params=limit(52),
     )(meta, sizes, live, x0, left, right, env)
     before = all_summed(mine, other)
     mine, other, factors = pl.pallas_call(
@@ -341,7 +345,7 @@
         out_specs=[VMEM] * 3,
         out_shape=sums + [shape((2, WIDTH), jnp.float32)],
         scratch_shapes=scratch + [dma(GROUPS, 2), dma(3), dma(GROUPS, 1), PACKED],
-        compiler_params=PARAMS,
+        compiler_params=limit(12),
     )(meta, sizes, live, before, x0, left, right, env)
     sigma = all_summed(mine, other)
     psi, renorm = pl.pallas_call(
@@ -354,7 +358,7 @@
         ],
         scratch_shapes=[BLOCKS, BLOCKS, BLOCKS, SIZES]
         + [dma(GROUPS, 1), dma(GROUPS, 1), dma(GROUPS, 1), dma(1), PACKED, PACKED, PACKED],
-        compiler_params=PARAMS,
+        compiler_params=limit(12),
     )(meta, sizes, factors, before, sigma, x0, env)
     positions = lax.axis_size("sweep")
     came = lax.ppermute(renorm, "sweep", [(i, i + 1) for i in range(positions - 1)])
@@ -372,7 +376,7 @@
             dma(GROUPS, 1),
             dma(1),
         ],
-        compiler_params=PARAMS,
+        compiler_params=limit(8),
     )(came, env)
     return psi[None], next_left[None]
 

time: 173 us -> 157 us (0.908)
  local copies, waits for them, and re-layouts: 8.02 us -> 0.69 us
  Pallas kernels: 22 us -> 16 us
  blocking collectives: 121 us -> 119 us
    unnamed x20 -> x12, local copies, waits for them, and re-layouts: 8.02 us -> 0.69 us
    pallas_call x4, Pallas kernels: 6.81 us -> 0.18 us  [summed(): pl.pallas_call(sum_kernel, in_specs=[VMEM], out_specs=VMEM, out_shape=sha...]
    all_to_all x6, blocking collectives: 105 us -> 103 us  [exchange(): return lax.all_to_all(value, axes, 0, 0)]
where the time goes in v3:
time: 157 us
  blocking collectives  119 us (76%)
  Pallas kernels  16 us (10%)
  waiting for transfers between devices  13.7 us (9%)
  starting transfers between devices  6.17 us (4%)
    all_to_all x6, blocking collectives, exchange(): return lax.all_to_all(value, axes, 0, 0)  103 us
    all_gather x2, blocking collectives, all_summed(): return lax.all_gather(half.reshape(HALF, WIDTH), 'core', tiled=True)  12.8 us
    ppermute x1, waiting for transfers between devices, shards(): lax.ppermute(renorm, 'sweep', [(i, i + 1) for i in range(positions - 1)])  11 us
    ppermute x2, starting transfers between devices, all_summed(): came = lax.ppermute(other, 'core', [(0, 1), (1, 0)])  4.88 us
    pallas_call x1, Pallas kernels, shards(): pl.pallas_call(last_kernel, in_specs=[SMEM, HBM] + [VMEM] * 3 + [HBM] * 2...  4.85 us
    pallas_call x1, Pallas kernels, shards(): pl.pallas_call(next_kernel, in_specs=[SMEM, HBM, HBM, VMEM] + [HBM] * 4,...  4.84 us
    pallas_call x1, Pallas kernels, shards(): pl.pallas_call(first_kernel, in_specs=[SMEM] + [HBM] * 6, out_specs=[VMEM...  4.32 us
    all_gather x1, blocking collectives, shards(): came = lax.all_gather(came, 'core', tiled=True)  3.19 us
  transfers between devices with their start and end apart: 3, of which 3 were waited for; matrix products, arithmetic and copies ran while one was open for 0% of the time, Pallas kernels for 0%

profile of v3, /device:TPU:25, one launch (start us, length us, event | category | flops | bytes accessed | tf_op | source)
XLA Modules:
  0.0 156.8 jit_solution(18111261301286242250)
XLA Ops:
  0.6 0.1 pad_add_fusion.meta
  0.7 0.0 copy-start.4
  0.7 0.7 copy-done.4
  1.4 0.0 copy-done.5
  1.4 4.3 %shard_map.77 = (f32[1536,128]{1,0:T(8,128)S(1)}, bf16[1536,128]{1,0:T(8,128)(2,1)S(1)}) custom-call(s32[2]{0:T(128)S(1)} %pad_add_fusion.meta, s32[1,32]{1,0:T(1,128)S(1)} %copy-done.4, s32[1,32]{1,0:T(1,128)S(1)} %bitcast.24, bf16[32,128,128]{2,1,0:T(8,128)(2,1)} %bitcast.17, bf16[32,128,128]{2,1,0:T(8,128)(2,1)} %bitcast.20, ...), custom_call_target="tpu_custom_call" | custom-call | tf_op jit(solution)/shard_map/pallas_call | solution.py:333
  5.7 2.6 %collective-permute-start = (bf16[1536,128]{1,0:T(8,128)(2,1)S(1)}, bf16[1536,128]{1,0:T(8,128)(2,1)S(1)}, u32[]{:S(2)}, u32[]{:S(2)}) collective-permute-start(bf16[1536,128]{1,0:T(8,128)(2,1)S(1)} %get-tuple-element.10), channel_id=1, source_target_pairs={{0,1},{1,0},{2,3},{3,2},{4,5},{5,4},{6,7},{7,6},{8,9},{9,8},{10,11... | collective-permute-start | bytes 1179656 | tf_op jit(solution)/shard_map/ppermute | solution.py:307
  8.3 1.3 collective-permute-done
  9.7 0.1 add_convert_fusion.1
  9.8 20.0 %all_to_all.30.parts = bf16[16,96,128]{2,1,0:T(8,128)(2,1)S(1)} all-to-all(bf16[16,96,128]{2,1,0:T(8,128)(2,1)S(1)} %bitcast.26), channel_id=1, replica_groups=mesh['sweep'=4,'zh'=4,'zl'=4,'x'=4,'core'=2] {'zl','x'}, dimensions={0} | all-to-all | bytes 786432 | tf_op jit(solution)/shard_map/all_to_all | solution.py:303
  29.8 0.1 shard_map.78
  29.9 24.7 %all_to_all.31.parts = bf16[4,96,128]{2,1,0:T(8,128)(2,1)S(1)} all-to-all(bf16[4,96,128]{2,1,0:T(8,128)(2,1)S(1)} %shard_map.78), channel_id=1, replica_groups=mesh['sweep'=4,'zh'=4,'zl'=4,'x'=4,'core'=2] {'zh'}, dimensions={0} | all-to-all | bytes 196608 | tf_op jit(solution)/shard_map/all_to_all | solution.py:303
  54.6 0.0 copy-start
  54.6 14.2 %all_to_all.32 = bf16[16,96,128]{2,1,0:T(8,128)(2,1)S(1)} all-to-all(bf16[16,96,128]{2,1,0:T(8,128)(2,1)S(1)} %shard_map.79), channel_id=1, replica_groups=mesh['sweep'=4,'zh'=4,'zl'=4,'x'=4,'core'=2] {'zl','x'}, dimensions={0} | all-to-all | bytes 786432 | tf_op jit(solution)/shard_map/all_to_all | solution.py:303
  68.8 6.4 %all_gather.9.sigma.sigma_before = bf16[3072,128]{1,0:T(8,128)(2,1)S(1)} all-gather(bf16[1536,128]{1,0:T(8,128)(2,1)S(1)} %bitcast.28), channel_id=1, replica_groups=mesh['sweep'=4,'zh'=4,'zl'=4,'x'=4,'core'=2] {'core'}, dimensions={0}, use_global_device_ids=true | all-gather | bytes 1179648 | tf_op jit(solution)/shard_map/all_gather | solution.py:312
  75.2 0.0 copy-done.3
  75.2 0.0 copy-done.2
  75.2 0.0 copy-done.1
  75.2 0.0 copy-done
  75.2 4.8 %shard_map.80 = (f32[1536,128]{1,0:T(8,128)S(1)}, bf16[1536,128]{1,0:T(8,128)(2,1)S(1)}, f32[2,128]{1,0:T(2,128)S(1)}) custom-call(s32[2]{0:T(128)S(1)} %pad_add_fusion.meta, s32[1,32]{1,0:T(1,128)S(1)} %copy-done.4, s32[1,32]{1,0:T(1,128)S(1)} %bitcast.25, bf16[3072,128]{1,0:T(8,128)(2,1)S(1)} %all_gather.9.sigma.sigma_before, ...), custom_call_target="tpu_custom_call" | custom-call | tf_op jit(solution)/shard_map/pallas_call | solution.py:342
  80.1 2.3 %collective-permute-start.1 = (bf16[1536,128]{1,0:T(8,128)(2,1)S(1)}, bf16[1536,128]{1,0:T(8,128)(2,1)S(1)}, u32[]{:S(2)}, u32[]{:S(2)}) collective-permute-start(bf16[1536,128]{1,0:T(8,128)(2,1)S(1)} %get-tuple-element.13), channel_id=1, source_target_pairs={{0,1},{1,0},{2,3},{3,2},{4,5},{5,4},{6,7},{7,6},{8,9},{9,8},{10,11... | collective-permute-start | bytes 1179656 | tf_op jit(solution)/shard_map/ppermute | solution.py:307
  82.4 1.3 collective-permute-done.1
  83.7 0.1 add_convert_fusion
  83.8 15.1 %all_to_all.33.parts = bf16[16,96,128]{2,1,0:T(8,128)(2,1)S(1)} all-to-all(bf16[16,96,128]{2,1,0:T(8,128)(2,1)S(1)} %bitcast.27), channel_id=1, replica_groups=mesh['sweep'=4,'zh'=4,'zl'=4,'x'=4,'core'=2] {'zl','x'}, dimensions={0} | all-to-all | bytes 786432 | tf_op jit(solution)/shard_map/all_to_all | solution.py:303
  98.9 0.1 shard_map.81
  99.0 15.1 %all_to_all.34.parts = bf16[4,96,128]{2,1,0:T(8,128)(2,1)S(1)} all-to-all(bf16[4,96,128]{2,1,0:T(8,128)(2,1)S(1)} %shard_map.81), channel_id=1, replica_groups=mesh['sweep'=4,'zh'=4,'zl'=4,'x'=4,'core'=2] {'zh'}, dimensions={0} | all-to-all | bytes 196608 | tf_op jit(solution)/shard_map/all_to_all | solution.py:303
  114.1 14.1 %all_to_all.35 = bf16[16,96,128]{2,1,0:T(8,128)(2,1)S(1)} all-to-all(bf16[16,96,128]{2,1,0:T(8,128)(2,1)S(1)} %shard_map.82), channel_id=1, replica_groups=mesh['sweep'=4,'zh'=4,'zl'=4,'x'=4,'core'=2] {'zl','x'}, dimensions={0} | all-to-all | bytes 786432 | tf_op jit(solution)/shard_map/all_to_all | solution.py:303
  128.2 6.4 %all_gather.10.sigma = bf16[3072,128]{1,0:T(8,128)(2,1)S(1)} all-gather(bf16[1536,128]{1,0:T(8,128)(2,1)S(1)} %bitcast.29), channel_id=1, replica_groups=mesh['sweep'=4,'zh'=4,'zl'=4,'x'=4,'core'=2] {'core'}, dimensions={0}, use_global_device_ids=true | all-gather | bytes 1179648 | tf_op jit(solution)/shard_map/all_gather | solution.py:312
  134.6 4.8 %shard_map.83 = (bf16[32,128,128]{2,1,0:T(8,128)(2,1)}, bf16[1552,128]{1,0:T(8,128)(2,1)S(1)}) custom-call(s32[2]{0:T(128)S(1)} %pad_add_fusion.meta, s32[1,32]{1,0:T(1,128)S(1)} %copy-done.4, f32[2,128]{1,0:T(2,128)S(1)} %get-tuple-element.11.factors, bf16[3072,128]{1,0:T(8,128)(2,1)S(1)} %all_gather.9.sigma.sigma_before, ...), custom_call_target="tpu_custom_call" | custom-call | tf_op jit(solution)/shard_map/pallas_call | solution.py:351
  139.5 1.3 collective-permute-start.2
  140.8 11.0 %collective-permute-done.2 = bf16[1552,128]{1,0:T(8,128)(2,1)S(1)} collective-permute-done((bf16[1552,128]{1,0:T(8,128)(2,1)S(1)}, bf16[1552,128]{1,0:T(8,128)(2,1)S(1)}, u32[]{:S(2)}, u32[]{:S(2)}) %collective-permute-start.2) | collective-permute-done | bytes 397344 | tf_op jit(solution)/shard_map/ppermute | solution.py:364
  151.8 3.2 %all_gather.11.came = bf16[3104,128]{1,0:T(8,128)(2,1)S(1)} all-gather(bf16[1552,128]{1,0:T(8,128)(2,1)S(1)} %collective-permute-done.2), channel_id=1, replica_groups=mesh['sweep'=4,'zh'=4,'zl'=4,'x'=4,'core'=2] {'core'}, dimensions={0}, use_global_device_ids=true | all-gather | bytes 1191936 | tf_op jit(solution)/shard_map/all_gather | solution.py:365
  155.0 1.8 %shard_map.84 = bf16[32,128,128]{2,1,0:T(8,128)(2,1)} custom-call(bf16[3104,128]{1,0:T(8,128)(2,1)S(1)} %all_gather.11.came, bf16[32,128,128]{2,1,0:T(8,128)(2,1)S(1)} %bitcast.16), custom_call_target="tpu_custom_call" | custom-call | tf_op jit(solution)/shard_map/pallas_call | solution.py:366
  (6 shorter events, 0.1 us)
Async XLA Ops:
  0.7 0.7 copy-start.4
  0.7 0.7 copy-start.5
  5.7 3.9 %collective-permute-start = (bf16[1536,128]{1,0:T(8,128)(2,1)S(1)}, bf16[1536,128]{1,0:T(8,128)(2,1)S(1)}, u32[]{:S(2)}, u32[]{:S(2)}) collective-permute-start(bf16[1536,128]{1,0:T(8,128)(2,1)S(1)} %get-tuple-element.10), channel_id=1, source_target_pairs={{0,1},{1,0},{2,3},{3,2},{4,5},{5,4},{6,7},{7,6},{8,9},{9,8},{10,11... | collective-permute-start | bytes 1179656 | tf_op jit(solution)/shard_map/ppermute | solution.py:307
  9.7 65.6 %copy-start.3 = (bf16[1,1,32,128,128]{4,3,2,1,0:T(8,128)(2,1)S(1)}, bf16[1,1,32,128,128]{4,3,2,1,0:T(8,128)(2,1)}, u32[]{:S(2)}) copy-start(bf16[1,1,32,128,128]{4,3,2,1,0:T(8,128)(2,1)} %param.8) | copy-start | bytes 3145732
  29.8 45.4 %copy-start.2 = (bf16[1,1,32,128,128]{4,3,2,1,0:T(8,128)(2,1)S(1)}, bf16[1,1,32,128,128]{4,3,2,1,0:T(8,128)(2,1)}, u32[]{:S(2)}) copy-start(bf16[1,1,32,128,128]{4,3,2,1,0:T(8,128)(2,1)} %param.7) | copy-start | bytes 3145732
  54.5 20.7 %copy-start.1 = (bf16[1,32,128,128]{3,2,1,0:T(8,128)(2,1)S(1)}, bf16[1,32,128,128]{3,2,1,0:T(8,128)(2,1)}, u32[]{:S(2)}) copy-start(bf16[1,32,128,128]{3,2,1,0:T(8,128)(2,1)} %param.6) | copy-start | bytes 3145732
  54.6 20.7 %copy-start = (bf16[1,32,128,128]{3,2,1,0:T(8,128)(2,1)S(1)}, bf16[1,32,128,128]{3,2,1,0:T(8,128)(2,1)}, u32[]{:S(2)}) copy-start(bf16[1,32,128,128]{3,2,1,0:T(8,128)(2,1)} %param.11) | copy-start | bytes 3145732
  80.1 3.6 %collective-permute-start.1 = (bf16[1536,128]{1,0:T(8,128)(2,1)S(1)}, bf16[1536,128]{1,0:T(8,128)(2,1)S(1)}, u32[]{:S(2)}, u32[]{:S(2)}) collective-permute-start(bf16[1536,128]{1,0:T(8,128)(2,1)S(1)} %get-tuple-element.13), channel_id=1, source_target_pairs={{0,1},{1,0},{2,3},{3,2},{4,5},{5,4},{6,7},{7,6},{8,9},{9,8},{10,11... | collective-permute-start | bytes 1179656 | tf_op jit(solution)/shard_map/ppermute | solution.py:307
  139.5 12.3 %collective-permute-start.2 = (bf16[1552,128]{1,0:T(8,128)(2,1)S(1)}, bf16[1552,128]{1,0:T(8,128)(2,1)S(1)}, u32[]{:S(2)}, u32[]{:S(2)}) collective-permute-start(bf16[1552,128]{1,0:T(8,128)(2,1)S(1)} %get-tuple-element.15), channel_id=1, source_target_pairs={{0,128},{128,256},{256,384},{1,129},{129,257},{257,385},{2,130},{1... | collective-permute-start | bytes 1191944 | tf_op jit(solution)/shard_map/ppermute | solution.py:364

commit v4 on v3

v4 whole, which is shorter than its diff:
```python
import math

import jax
import jax.numpy as jnp
from jax import lax
from jax.experimental import pallas as pl
from jax.experimental.pallas import tpu as pltpu
from jax.sharding import Mesh, PartitionSpec as P

NSEC = 32
WIDTH = 128
PAIRS = 128
ROWS = 3 * NSEC * WIDTH // 4
HALF = ROWS // 2
TOTAL = NSEC * WIDTH * WIDTH
X, ZL, ZH = 4, 4, 4
NEAR = ZL * X
PIECE = HALF // NEAR
SCALE = 1.0 / math.sqrt(PAIRS)
GROUP = 8
GROUPS = NSEC // GROUP
TAIL = 16
CHUNK = 256

VMEM = pl.BlockSpec(memory_space=pltpu.VMEM)
SMEM = pl.BlockSpec(memory_space=pltpu.SMEM)
HBM = pl.BlockSpec(memory_space=pltpu.HBM)
PACKED = pltpu.VMEM((ROWS + WIDTH, WIDTH), jnp.float32)
BLOCKS = pltpu.VMEM((NSEC, WIDTH, WIDTH), jnp.bfloat16)


def limit(mib):
    return pltpu.CompilerParams(vmem_limit_bytes=mib * 1024 * 1024)


def shape(dims, dtype):
    return jax.ShapeDtypeStruct(dims, dtype)


def square_mask(size):
    row = lax.broadcasted_iota(jnp.int32, (WIDTH, WIDTH), 0)
    col = lax.broadcasted_iota(jnp.int32, (WIDTH, WIDTH), 1)
    return (row < size) & (col < size)


def dot(a, b):
    return jnp.dot(a, b, preferred_element_type=jnp.float32)


def group_copies(pairs, sems):
    return [
        [
            pltpu.make_async_copy(
                source.at[pl.ds(g * GROUP, GROUP)], target.at[pl.ds(g * GROUP, GROUP)], sems.at[g, k]
            )
            for k, (source, target) in enumerate(pairs)
        ]
        for g in range(GROUPS)
    ]


def start_all(copies):
    for group in copies:
        for copy in group:
            copy.start()


def flat_sums(pairs):
    totals = None
    for start in range(0, ROWS, CHUNK):
        parts = [
            jnp.sum((p * q).reshape(CHUNK // 8, 8, WIDTH), axis=0)
            for p, q in pairs(pl.ds(start, CHUNK))
        ]
        totals = parts if totals is None else [t + p for t, p in zip(totals, parts)]
    return [jnp.sum(t, axis=(0, 1), keepdims=True) for t in totals]


def step_factors(x_of, sigma):
    def products(rows):
        x, s = x_of(rows), sigma[rows, :].astype(jnp.float32)
        return [(x, x), (x, s), (s, s)]

    xx, xs, ss = flat_sums(products)
    rho = xs / xx
    yy = xx + 0.64 * jnp.maximum(ss - rho * xs, 0.0)
    shrink = 1.0 / jnp.sqrt(yy / TOTAL + 1e-06)
    return (1.0 + 0.8 * rho) * shrink, 0.8 * shrink


def size_of(meta, i):
    return meta[2 + i]


def rows_below(size):
    return lax.broadcasted_iota(jnp.int32, (WIDTH, WIDTH), 0) < size


def run_pairs(meta, xb_of, left, right, env, ready, env_ready, packed, mine, other):
    sector = meta[1]
    column = lax.broadcasted_iota(jnp.int32, (WIDTH, WIDTH), 1)

    def body(g, carry):
        offset, at = carry
        ready(g)
        sums = []
        place = offset
        for j in range(GROUP):
            i = g * GROUP + j
            xb = xb_of(i, place)
            at = jnp.where(i == sector, place, at)
            place = place + size_of(meta, i)
            block = left[i]
            live = meta[2 + NSEC + i].astype(jnp.float32)
            u = live * dot(jnp.concatenate([block, block.T], 0), xb)
            u = u.astype(jnp.bfloat16)
            context = right[i]
            total = SCALE * dot(
                jnp.concatenate([u[:WIDTH], u[WIDTH:]], 1),
                jnp.concatenate([context.T, context], 0),
            )
            sums.append(jnp.where(column < size_of(meta, i), total, 0.0))
        for j in range(GROUP):
            packed[pl.ds(offset, WIDTH), :] = sums[j]
            offset = offset + size_of(meta, g * GROUP + j)
        return offset, at

    _, at = lax.fori_loop(0, GROUPS, body, (jnp.int32(0), jnp.int32(0)))
    env_ready()
    term = 0.25 * dot(env[...], xb_of(sector, at, keep=False))
    packed[pl.ds(at, WIDTH), :] += jnp.where(square_mask(size_of(meta, sector)), term, 0.0)
    core = meta[0]
    mine[...] = packed[pl.ds(pl.multiple_of(core * HALF, 8), HALF), :]
    other[...] = packed[pl.ds(pl.multiple_of((1 - core) * HALF, 8), HALF), :].astype(jnp.bfloat16)


def first_kernel(
    meta, x0_in, left_in, right_in, env_in, mine, other, x_out,
    packed, x0, left, right, env, sems, env_sem, x_packed,
):
    pairs = [(x0_in, x0), (left_in, left), (right_in, right)]
    start_all(group_copies(pairs, sems))
    env_copy = pltpu.make_async_copy(env_in.at[meta[1]], env, env_sem.at[0])
    env_copy.start()

    def ready(g):
        some = pl.ds(g * GROUP, GROUP)
        for k, (source, target) in enumerate(pairs):
            pltpu.make_async_copy(source.at[some], target.at[some], sems.at[g, k]).wait()

    def xb_of(i, offset, keep=True):
        x = jnp.where(square_mask(size_of(meta, i)), x0[i].astype(jnp.float32), 0.0)
        if keep:
            x_packed[pl.ds(offset, WIDTH), :] = x
        return x.astype(jnp.bfloat16)

    run_pairs(meta, xb_of, left, right, env, ready, env_copy.wait, packed, mine, other)
    x_out[...] = x_packed[pl.ds(0, ROWS), :].astype(jnp.bfloat16)


def next_kernel(
    meta, sigma, x0, left, right, env_in, mine, other, factors, packed, env, env_sem, wide
):
    env_copy = pltpu.make_async_copy(env_in.at[meta[1]], env, env_sem.at[0])
    env_copy.start()

    def x_of(rows):
        return x0[rows, :].astype(jnp.float32)

    grow, drop = step_factors(x_of, sigma)
    factors[0:1, :] = jnp.broadcast_to(grow, (1, WIDTH))
    factors[1:2, :] = jnp.broadcast_to(drop, (1, WIDTH))
    wide[pl.ds(0, ROWS), :] = grow * x_of(pl.ds(0, ROWS)) - drop * sigma[...].astype(jnp.float32)

    def xb_of(i, offset, keep=True):
        mask = rows_below(size_of(meta, i))
        return jnp.where(mask, wide[pl.ds(offset, WIDTH), :], 0.0).astype(jnp.bfloat16)

    run_pairs(meta, xb_of, left, right, env, lambda g: None, env_copy.wait, packed, mine, other)


def renorm_kernel(
    meta, factors, sigma_before, sigma, x0, env, psi_out, renorm_out, wide, packed
):
    grow_before, drop_before = factors[0:1, :], factors[1:2, :]

    def x_of(rows):
        return grow_before * x0[rows, :].astype(jnp.float32) - drop_before * sigma_before[
            rows, :
        ].astype(jnp.float32)

    grow, drop = step_factors(x_of, sigma)
    psi = grow * x_of(pl.ds(0, ROWS)) - drop * sigma[...].astype(jnp.float32)
    psi = psi.astype(jnp.bfloat16)
    psi_out[...] = psi
    wide[pl.ds(0, ROWS), :] = psi.astype(jnp.float32)
    low = pl.multiple_of(meta[0] * HALF, 8)
    high = low + HALF
    offset = 0
    for g in range(GROUPS):
        places = [offset]
        for i in range(g * GROUP, (g + 1) * GROUP):
            places.append(places[-1] + size_of(meta, i))
        offset = places[-1]

        @pl.when((places[0] < high) & (offset > low))
        def _():
            blocks = []
            for i, place in zip(range(g * GROUP, (g + 1) * GROUP), places):
                block = jnp.where(rows_below(size_of(meta, i)), wide[pl.ds(place, WIDTH), :], 0.0)
                block = block.astype(jnp.bfloat16)
                applied = dot(env[i], block).astype(jnp.bfloat16)
                blocks.append(dot(block.T, applied) / math.sqrt(WIDTH))
            for place, block in zip(places, blocks):
                packed[pl.ds(place, WIDTH), :] = block

    renorm_out[pl.ds(0, HALF), :] = packed[pl.ds(low, HALF), :].astype(jnp.bfloat16)
    lane = lax.broadcasted_iota(jnp.int32, (TAIL, WIDTH), 1)
    row = jnp.zeros((TAIL, WIDTH), jnp.int32)
    for i in range(NSEC):
        row = jnp.where(lane == i, size_of(meta, i), row)
    renorm_out[pl.ds(HALF, TAIL), :] = row.astype(jnp.float32).astype(jnp.bfloat16)


def unpack(size_at, wide, result, out, sems, finish):
    copies = group_copies([(result, out)], sems)
    offset = 0
    for g in range(GROUPS):
        for i in range(g * GROUP, (g + 1) * GROUP):
            size = size_at(i)
            block = jnp.where(rows_below(size), wide[pl.ds(offset, WIDTH), :], 0.0)
            result[i] = finish(i, block).astype(jnp.bfloat16)
            offset = offset + size
        copies[g][0].start()
    for group in copies:
        group[0].wait()


def psi_kernel(meta, psi, out, wide, result, sems):
    wide[pl.ds(0, ROWS), :] = psi[...].astype(jnp.float32)
    unpack(lambda i: size_of(meta, i), wide, result, out, sems, lambda i, block: block)


def shift_kernel(came, env, out, wide, result, numbers, sizes, sems, own_sem):
    numbers[...] = came[pl.ds(HALF, 8), :].astype(jnp.float32).astype(jnp.int32)
    sizes_copy = pltpu.make_async_copy(numbers, sizes, own_sem.at[0])
    sizes_copy.start()
    wide[pl.ds(0, HALF), :] = came[pl.ds(0, HALF), :].astype(jnp.float32)
    wide[pl.ds(HALF, HALF), :] = came[pl.ds(HALF + TAIL, HALF), :].astype(jnp.float32)
    sizes_copy.wait()
    unpack(
        lambda i: sizes[0, i],
        wide,
        result,
        out,
        sems,
        lambda i, block: env[i].astype(jnp.float32) + block,
    )


def sum_kernel(parts, out):
    total = jnp.sum(parts[...].astype(jnp.float32), axis=0).astype(jnp.bfloat16)
    for k in range(out.shape[0]):
        out[k] = total


def summed(parts, copies):
    return pl.pallas_call(
        sum_kernel,
        in_specs=[VMEM],
        out_specs=VMEM,
        out_shape=shape((copies,) + parts.shape[1:], parts.dtype),
        compiler_params=limit(4),
    )(parts)


def exchange(value, axes):
    return lax.all_to_all(value, axes, 0, 0)


def all_summed(mine, other):
    came = lax.ppermute(other, "core", [(0, 1), (1, 0)])
    chip = (mine + came.astype(jnp.float32)).astype(jnp.bfloat16).reshape(NEAR, PIECE, WIDTH)
    near = summed(exchange(chip, ("zl", "x")), ZH)
    far = summed(exchange(near, "zh"), NEAR)
    half = exchange(far, ("zl", "x"))
    return lax.all_gather(half.reshape(HALF, WIDTH), "core", tiled=True)


def dma(*dims):
    return pltpu.SemaphoreType.DMA(dims)


def shards(initial_trial_state, left_ops, right_ops, pair_sectors, sector_size, left_env):
    x0 = initial_trial_state[0]
    left = left_ops[0, 0]
    right = right_ops[0, 0]
    env = left_env[0]
    core = lax.axis_index("core")
    sector = lax.axis_index(("zh", "zl", "x", "core")) // (PAIRS // NSEC)
    own = jnp.stack([core, sector]).astype(jnp.int32)
    meta = jnp.concatenate([own, sector_size[0], pair_sectors[0, 0]])

    sums = [shape((HALF, WIDTH), jnp.float32), shape((HALF, WIDTH), jnp.bfloat16)]
    rows = shape((ROWS, WIDTH), jnp.bfloat16)
    blocks = shape((NSEC, WIDTH, WIDTH), jnp.bfloat16)
    env_scratch = [pltpu.VMEM((WIDTH, WIDTH), jnp.bfloat16)]
    mine, other, x0 = pl.pallas_call(
        first_kernel,
        in_specs=[SMEM] + [HBM] * 4,
        out_specs=[VMEM] * 3,
        out_shape=sums + [rows],
        scratch_shapes=[PACKED, BLOCKS, BLOCKS, BLOCKS]
        + env_scratch
        + [dma(GROUPS, 3), dma(1), PACKED],
        compiler_params=limit(52),
    )(meta, x0, left, right, env)
    before = all_summed(mine, other)
    mine, other, factors = pl.pallas_call(
        next_kernel,
        in_specs=[SMEM] + [VMEM] * 4 + [HBM],
        out_specs=[VMEM] * 3,
        out_shape=sums + [shape((2, WIDTH), jnp.float32)],
        scratch_shapes=[PACKED] + env_scratch + [dma(1), PACKED],
        compiler_params=limit(12),
    )(meta, before, x0, left, right, env)
    sigma = all_summed(mine, other)
    psi, renorm = pl.pallas_call(
        renorm_kernel,
        in_specs=[SMEM] + [VMEM] * 5,
        out_specs=[VMEM] * 2,
        out_shape=[rows, shape((HALF + TAIL, WIDTH), jnp.bfloat16)],
        scratch_shapes=[PACKED, PACKED],
        compiler_params=limit(12),
    )(meta, factors, before, sigma, x0, env)
    positions = lax.axis_size("sweep")
    came = lax.ppermute(renorm, "sweep", [(i, i + 1) for i in range(positions - 1)])
    psi = pl.pallas_call(
        psi_kernel,
        in_specs=[SMEM, VMEM],
        out_specs=HBM,
        out_shape=blocks,
        scratch_shapes=[PACKED, BLOCKS, dma(GROUPS, 1)],
        compiler_params=limit(8),
        cost_estimate=pl.CostEstimate(flops=10**7, bytes_accessed=4 * 10**6, transcendentals=0),
    )(meta, psi)
    came = lax.all_gather(came, "core", tiled=True)
    next_left = pl.pallas_call(
        shift_kernel,
        in_specs=[VMEM] * 2,
        out_specs=HBM,
        out_shape=blocks,
        scratch_shapes=[
            PACKED,
            BLOCKS,
            pltpu.VMEM((8, WIDTH), jnp.int32),
            pltpu.SMEM((8, WIDTH), jnp.int32),
            dma(GROUPS, 1),
            dma(1),
        ],
        compiler_params=limit(8),
    )(came, env)
    return psi[None], next_left[None]


def solution(mesh):
    positions = mesh.shape["sweep"]
    split = Mesh(
        mesh.devices.reshape(positions, ZH, ZL, X, 2), ("sweep", "zh", "zl", "x", "core")
    )
    ops = ("zh", "zl", "x", "core")
    return jax.shard_map(
        shards,
        mesh=split,
        in_specs=(
            P("sweep", None, None, None),
            P("sweep", ops, None, None, None),
            P("sweep", ops, None, None, None),
            P("sweep", ops, None),
            P("sweep", None),
            P("sweep", None, None, None),
        ),
        out_specs=(P("sweep", None, None, None), P("sweep", None, None, None)),
        check_vma=False,
    )
```

time: 157 us -> 155 us (0.987)
    pallas_call x3 -> x4, Pallas kernels: 14 us -> 13.8 us  [the longest x1 4.44 us: shards(): pl.pallas_call(first_kernel, in_specs=[SMEM] + [HBM] * 4, out_specs=[VMEM...]
  transfers between devices with their start and end apart: 3 -> 3, of which waited for: 3 -> 3; matrix products, arithmetic and copies ran while one was open for 0% -> 0% of each run, Pallas kernels for 0% -> 1%
where the time goes in v4:
time: 155 us
  blocking collectives  119 us (77%)
  Pallas kernels  15.7 us (10%)
  waiting for transfers between devices  12.4 us (8%)
  starting transfers between devices  6.17 us (4%)
    all_to_all x6, blocking collectives, exchange(): return lax.all_to_all(value, axes, 0, 0)  103 us
    all_gather x2, blocking collectives, all_summed(): return lax.all_gather(half.reshape(HALF, WIDTH), 'core', tiled=True)  12.8 us
    ppermute x1, waiting for transfers between devices, shards(): lax.ppermute(renorm, 'sweep', [(i, i + 1) for i in range(positions - 1)])  9.77 us
    ppermute x2, starting transfers between devices, all_summed(): came = lax.ppermute(other, 'core', [(0, 1), (1, 0)])  4.88 us
    pallas_call x1, Pallas kernels, shards(): pl.pallas_call(first_kernel, in_specs=[SMEM] + [HBM] * 4, out_specs=[VMEM...  4.44 us
    pallas_call x1, Pallas kernels, shards(): pl.pallas_call(next_kernel, in_specs=[SMEM] + [VMEM] * 4 + [HBM], out_spe...  4.16 us
    pallas_call x1, Pallas kernels, shards(): pl.pallas_call(renorm_kernel, in_specs=[SMEM] + [VMEM] * 5, out_specs=[VM...  3.5 us
  transfers between devices with their start and end apart: 3, of which 3 were waited for; matrix products, arithmetic and copies ran while one was open for 0% of the time, Pallas kernels for 1%

profile of v4, /device:TPU:25, one launch (start us, length us, event | category | flops | bytes accessed | tf_op | source)
XLA Modules:
  0.0 154.7 jit_solution(15560935753524582457)
XLA Ops:
  0.7 0.0 copy-start.3
  0.7 0.0 copy-start.4
  0.7 0.6 copy-done.3
  1.3 0.0 copy-done.4
  1.3 0.1 pad_add_fusion.meta
  1.4 4.4 %shard_map.77 = (f32[1536,128]{1,0:T(8,128)S(1)}, bf16[1536,128]{1,0:T(8,128)(2,1)S(1)}, bf16[3072,128]{1,0:T(8,128)(2,1)S(1)}) custom-call(s32[66]{0:T(128)S(1)} %pad_add_fusion.meta, bf16[32,128,128]{2,1,0:T(8,128)(2,1)} %bitcast.26, bf16[32,128,128]{2,1,0:T(8,128)(2,1)} %bitcast.18, bf16[32,128,128]{2,1,0:T(8,128)(2,1)} %bitcast.20, ...), custom_call_target="tpu_custom_call" | custom-call | tf_op jit(solution)/shard_map/pallas_call | solution.py:308
  5.8 2.6 %collective-permute-start = (bf16[1536,128]{1,0:T(8,128)(2,1)S(1)}, bf16[1536,128]{1,0:T(8,128)(2,1)S(1)}, u32[]{:S(2)}, u32[]{:S(2)}) collective-permute-start(bf16[1536,128]{1,0:T(8,128)(2,1)S(1)} %get-tuple-element.11), channel_id=1, source_target_pairs={{0,1},{1,0},{2,3},{3,2},{4,5},{5,4},{6,7},{7,6},{8,9},{9,8},{10,11... | collective-permute-start | bytes 1179656 | tf_op jit(solution)/shard_map/ppermute | solution.py:282
  8.4 1.3 collective-permute-done
  9.8 0.1 add_convert_fusion.1
  9.9 19.9 %all_to_all.30.parts = bf16[16,96,128]{2,1,0:T(8,128)(2,1)S(1)} all-to-all(bf16[16,96,128]{2,1,0:T(8,128)(2,1)S(1)} %bitcast.22), channel_id=1, replica_groups=mesh['sweep'=4,'zh'=4,'zl'=4,'x'=4,'core'=2] {'zl','x'}, dimensions={0} | all-to-all | bytes 786432 | tf_op jit(solution)/shard_map/all_to_all | solution.py:278
  29.8 0.1 shard_map.78
  29.8 24.7 %all_to_all.31.parts = bf16[4,96,128]{2,1,0:T(8,128)(2,1)S(1)} all-to-all(bf16[4,96,128]{2,1,0:T(8,128)(2,1)S(1)} %shard_map.78), channel_id=1, replica_groups=mesh['sweep'=4,'zh'=4,'zl'=4,'x'=4,'core'=2] {'zh'}, dimensions={0} | all-to-all | bytes 196608 | tf_op jit(solution)/shard_map/all_to_all | solution.py:278
  54.5 0.0 copy-start
  54.6 14.2 %all_to_all.32 = bf16[16,96,128]{2,1,0:T(8,128)(2,1)S(1)} all-to-all(bf16[16,96,128]{2,1,0:T(8,128)(2,1)S(1)} %shard_map.79), channel_id=1, replica_groups=mesh['sweep'=4,'zh'=4,'zl'=4,'x'=4,'core'=2] {'zl','x'}, dimensions={0} | all-to-all | bytes 786432 | tf_op jit(solution)/shard_map/all_to_all | solution.py:278
  68.8 6.4 %all_gather.9.sigma.sigma_before = bf16[3072,128]{1,0:T(8,128)(2,1)S(1)} all-gather(bf16[1536,128]{1,0:T(8,128)(2,1)S(1)} %bitcast.24), channel_id=1, replica_groups=mesh['sweep'=4,'zh'=4,'zl'=4,'x'=4,'core'=2] {'core'}, dimensions={0}, use_global_device_ids=true | all-gather | bytes 1179648 | tf_op jit(solution)/shard_map/all_gather | solution.py:287
  75.2 0.0 copy-done.2
  75.2 0.0 copy-done.1
  75.2 4.2 %shard_map.80 = (f32[1536,128]{1,0:T(8,128)S(1)}, bf16[1536,128]{1,0:T(8,128)(2,1)S(1)}, f32[2,128]{1,0:T(2,128)S(1)}) custom-call(s32[66]{0:T(128)S(1)} %pad_add_fusion.meta, bf16[3072,128]{1,0:T(8,128)(2,1)S(1)} %all_gather.9.sigma.sigma_before, bf16[3072,128]{1,0:T(8,128)(2,1)S(1)} %get-tuple-element.12.x0, bf16[32,128,128]{2,1,0:T(8,128)(2,1)S(1)} %bitcast.19, ...), custom_call_target="tpu_custom_call" | custom-call | tf_op jit(solution)/shard_map/pallas_call | solution.py:319
  79.4 2.3 %collective-permute-start.1 = (bf16[1536,128]{1,0:T(8,128)(2,1)S(1)}, bf16[1536,128]{1,0:T(8,128)(2,1)S(1)}, u32[]{:S(2)}, u32[]{:S(2)}) collective-permute-start(bf16[1536,128]{1,0:T(8,128)(2,1)S(1)} %get-tuple-element.15), channel_id=1, source_target_pairs={{0,1},{1,0},{2,3},{3,2},{4,5},{5,4},{6,7},{7,6},{8,9},{9,8},{10,11... | collective-permute-start | bytes 1179656 | tf_op jit(solution)/shard_map/ppermute | solution.py:282
  81.7 1.3 collective-permute-done.1
  83.0 0.1 add_convert_fusion
  83.1 15.1 %all_to_all.33.parts = bf16[16,96,128]{2,1,0:T(8,128)(2,1)S(1)} all-to-all(bf16[16,96,128]{2,1,0:T(8,128)(2,1)S(1)} %bitcast.23), channel_id=1, replica_groups=mesh['sweep'=4,'zh'=4,'zl'=4,'x'=4,'core'=2] {'zl','x'}, dimensions={0} | all-to-all | bytes 786432 | tf_op jit(solution)/shard_map/all_to_all | solution.py:278
  98.2 0.1 shard_map.81
  98.3 15.1 %all_to_all.34.parts = bf16[4,96,128]{2,1,0:T(8,128)(2,1)S(1)} all-to-all(bf16[4,96,128]{2,1,0:T(8,128)(2,1)S(1)} %shard_map.81), channel_id=1, replica_groups=mesh['sweep'=4,'zh'=4,'zl'=4,'x'=4,'core'=2] {'zh'}, dimensions={0} | all-to-all | bytes 196608 | tf_op jit(solution)/shard_map/all_to_all | solution.py:278
  113.4 14.1 %all_to_all.35 = bf16[16,96,128]{2,1,0:T(8,128)(2,1)S(1)} all-to-all(bf16[16,96,128]{2,1,0:T(8,128)(2,1)S(1)} %shard_map.82), channel_id=1, replica_groups=mesh['sweep'=4,'zh'=4,'zl'=4,'x'=4,'core'=2] {'zl','x'}, dimensions={0} | all-to-all | bytes 786432 | tf_op jit(solution)/shard_map/all_to_all | solution.py:278
  127.5 6.4 %all_gather.10.sigma = bf16[3072,128]{1,0:T(8,128)(2,1)S(1)} all-gather(bf16[1536,128]{1,0:T(8,128)(2,1)S(1)} %bitcast.25), channel_id=1, replica_groups=mesh['sweep'=4,'zh'=4,'zl'=4,'x'=4,'core'=2] {'core'}, dimensions={0}, use_global_device_ids=true | all-gather | bytes 1179648 | tf_op jit(solution)/shard_map/all_gather | solution.py:287
  133.9 3.5 %shard_map.83 = (bf16[3072,128]{1,0:T(8,128)(2,1)S(1)}, bf16[1552,128]{1,0:T(8,128)(2,1)S(1)}) custom-call(s32[66]{0:T(128)S(1)} %pad_add_fusion.meta, f32[2,128]{1,0:T(2,128)S(1)} %get-tuple-element.13.factors, bf16[3072,128]{1,0:T(8,128)(2,1)S(1)} %all_gather.9.sigma.sigma_before, bf16[3072,128]{1,0:T(8,128)(2,1)S(1)} %all_gather.10.sigma, ...), custom_call_target="tpu_custom_call" | custom-call | tf_op jit(solution)/shard_map/pallas_call | solution.py:328
  137.4 1.3 collective-permute-start.2
  138.7 1.7 %shard_map.84 = bf16[32,128,128]{2,1,0:T(8,128)(2,1)} custom-call(s32[66]{0:T(128)S(1)} %pad_add_fusion.meta, bf16[3072,128]{1,0:T(8,128)(2,1)S(1)} %get-tuple-element.16.psi), custom_call_target="tpu_custom_call" | custom-call | flops 10000000 | bytes 4000000 | tf_op jit(solution)/shard_map/pallas_call | solution.py:338
  140.4 9.8 %collective-permute-done.2 = bf16[1552,128]{1,0:T(8,128)(2,1)S(1)} collective-permute-done((bf16[1552,128]{1,0:T(8,128)(2,1)S(1)}, bf16[1552,128]{1,0:T(8,128)(2,1)S(1)}, u32[]{:S(2)}, u32[]{:S(2)}) %collective-permute-start.2) | collective-permute-done | bytes 397344 | tf_op jit(solution)/shard_map/ppermute | solution.py:337
  150.2 2.7 %all_gather.11.came = bf16[3104,128]{1,0:T(8,128)(2,1)S(1)} all-gather(bf16[1552,128]{1,0:T(8,128)(2,1)S(1)} %collective-permute-done.2), channel_id=1, replica_groups=mesh['sweep'=4,'zh'=4,'zl'=4,'x'=4,'core'=2] {'core'}, dimensions={0}, use_global_device_ids=true | all-gather | bytes 1191936 | tf_op jit(solution)/shard_map/all_gather | solution.py:347
  152.9 1.7 %shard_map.85 = bf16[32,128,128]{2,1,0:T(8,128)(2,1)} custom-call(bf16[3104,128]{1,0:T(8,128)(2,1)S(1)} %all_gather.11.came, bf16[32,128,128]{2,1,0:T(8,128)(2,1)S(1)} %bitcast.17), custom_call_target="tpu_custom_call" | custom-call | tf_op jit(solution)/shard_map/pallas_call | solution.py:348
  (5 shorter events, 0.1 us)
Async XLA Ops:
  0.7 0.7 copy-start.3
  0.7 0.7 copy-start.4
  5.8 3.9 %collective-permute-start = (bf16[1536,128]{1,0:T(8,128)(2,1)S(1)}, bf16[1536,128]{1,0:T(8,128)(2,1)S(1)}, u32[]{:S(2)}, u32[]{:S(2)}) collective-permute-start(bf16[1536,128]{1,0:T(8,128)(2,1)S(1)} %get-tuple-element.11), channel_id=1, source_target_pairs={{0,1},{1,0},{2,3},{3,2},{4,5},{5,4},{6,7},{7,6},{8,9},{9,8},{10,11... | collective-permute-start | bytes 1179656 | tf_op jit(solution)/shard_map/ppermute | solution.py:282
  29.8 45.4 %copy-start.2 = (bf16[1,1,32,128,128]{4,3,2,1,0:T(8,128)(2,1)S(1)}, bf16[1,1,32,128,128]{4,3,2,1,0:T(8,128)(2,1)}, u32[]{:S(2)}) copy-start(bf16[1,1,32,128,128]{4,3,2,1,0:T(8,128)(2,1)} %param.8) | copy-start | bytes 3145732
  54.5 20.7 %copy-start.1 = (bf16[1,1,32,128,128]{4,3,2,1,0:T(8,128)(2,1)S(1)}, bf16[1,1,32,128,128]{4,3,2,1,0:T(8,128)(2,1)}, u32[]{:S(2)}) copy-start(bf16[1,1,32,128,128]{4,3,2,1,0:T(8,128)(2,1)} %param.7) | copy-start | bytes 3145732
  54.5 20.7 %copy-start = (bf16[1,32,128,128]{3,2,1,0:T(8,128)(2,1)S(1)}, bf16[1,32,128,128]{3,2,1,0:T(8,128)(2,1)}, u32[]{:S(2)}) copy-start(bf16[1,32,128,128]{3,2,1,0:T(8,128)(2,1)} %param.11) | copy-start | bytes 3145732
  79.4 3.6 %collective-permute-start.1 = (bf16[1536,128]{1,0:T(8,128)(2,1)S(1)}, bf16[1536,128]{1,0:T(8,128)(2,1)S(1)}, u32[]{:S(2)}, u32[]{:S(2)}) collective-permute-start(bf16[1536,128]{1,0:T(8,128)(2,1)S(1)} %get-tuple-element.15), channel_id=1, source_target_pairs={{0,1},{1,0},{2,3},{3,2},{4,5},{5,4},{6,7},{7,6},{8,9},{9,8},{10,11... | collective-permute-start | bytes 1179656 | tf_op jit(solution)/shard_map/ppermute | solution.py:282
  137.4 12.8 %collective-permute-start.2 = (bf16[1552,128]{1,0:T(8,128)(2,1)S(1)}, bf16[1552,128]{1,0:T(8,128)(2,1)S(1)}, u32[]{:S(2)}, u32[]{:S(2)}) collective-permute-start(bf16[1552,128]{1,0:T(8,128)(2,1)S(1)} %get-tuple-element.17), channel_id=1, source_target_pairs={{0,128},{128,256},{256,384},{1,129},{129,257},{257,385},{2,130},{1... | collective-permute-start | bytes 1191944 | tf_op jit(solution)/shard_map/ppermute | solution.py:337

commit v5 on v4

--- a/solution.py
+++ b/solution.py
@@ -19,6 +19,7 @@
 SCALE = 1.0 / math.sqrt(PAIRS)
 GROUP = 8
 GROUPS = NSEC // GROUP
+FIRST_GROUP = 16
 TAIL = 16
 CHUNK = 256
 
@@ -47,15 +48,15 @@
     return jnp.dot(a, b, preferred_element_type=jnp.float32)
 
 
-def group_copies(pairs, sems):
+def group_copies(pairs, sems, group=GROUP):
     return [
         [
             pltpu.make_async_copy(
-                source.at[pl.ds(g * GROUP, GROUP)], target.at[pl.ds(g * GROUP, GROUP)], sems.at[g, k]
+                source.at[pl.ds(g * group, group)], target.at[pl.ds(g * group, group)], sems.at[g, k]
             )
             for k, (source, target) in enumerate(pairs)
         ]
-        for g in range(GROUPS)
+        for g in range(NSEC // group)
     ]
 
 
@@ -96,7 +97,7 @@
     return lax.broadcasted_iota(jnp.int32, (WIDTH, WIDTH), 0) < size
 
 
-def run_pairs(meta, xb_of, left, right, env, ready, env_ready, packed, mine, other):
+def run_pairs(meta, xb_of, left, right, env, group, ready, env_ready, packed, mine, other):
     sector = meta[1]
     column = lax.broadcasted_iota(jnp.int32, (WIDTH, WIDTH), 1)
 
@@ -105,8 +106,8 @@
         ready(g)
         sums = []
         place = offset
-        for j in range(GROUP):
-            i = g * GROUP + j
+        for j in range(group):
+            i = g * group + j
             xb = xb_of(i, place)
             at = jnp.where(i == sector, place, at)
             place = place + size_of(meta, i)
@@ -120,12 +121,12 @@
                 jnp.concatenate([context.T, context], 0),
             )
             sums.append(jnp.where(column < size_of(meta, i), total, 0.0))
-        for j in range(GROUP):
+        for j in range(group):
             packed[pl.ds(offset, WIDTH), :] = sums[j]
-            offset = offset + size_of(meta, g * GROUP + j)
+            offset = offset + size_of(meta, g * group + j)
         return offset, at
 
-    _, at = lax.fori_loop(0, GROUPS, body, (jnp.int32(0), jnp.int32(0)))
+    _, at = lax.fori_loop(0, NSEC // group, body, (jnp.int32(0), jnp.int32(0)))
     env_ready()
     term = 0.25 * dot(env[...], xb_of(sector, at, keep=False))
     packed[pl.ds(at, WIDTH), :] += jnp.where(square_mask(size_of(meta, sector)), term, 0.0)
@@ -139,12 +140,12 @@
     packed, x0, left, right, env, sems, env_sem, x_packed,
 ):
     pairs = [(x0_in, x0), (left_in, left), (right_in, right)]
-    start_all(group_copies(pairs, sems))
+    start_all(group_copies(pairs, sems, FIRST_GROUP))
     env_copy = pltpu.make_async_copy(env_in.at[meta[1]], env, env_sem.at[0])
     env_copy.start()
 
     def ready(g):
-        some = pl.ds(g * GROUP, GROUP)
+        some = pl.ds(g * FIRST_GROUP, FIRST_GROUP)
         for k, (source, target) in enumerate(pairs):
             pltpu.make_async_copy(source.at[some], target.at[some], sems.at[g, k]).wait()
 
@@ -154,7 +155,7 @@
             x_packed[pl.ds(offset, WIDTH), :] = x
         return x.astype(jnp.bfloat16)
 
-    run_pairs(meta, xb_of, left, right, env, ready, env_copy.wait, packed, mine, other)
+    run_pairs(meta, xb_of, left, right, env, FIRST_GROUP, ready, env_copy.wait, packed, mine, other)
     x_out[...] = x_packed[pl.ds(0, ROWS), :].astype(jnp.bfloat16)
 
 
@@ -176,7 +177,7 @@
         mask = rows_below(size_of(meta, i))
         return jnp.where(mask, wide[pl.ds(offset, WIDTH), :], 0.0).astype(jnp.bfloat16)
 
-    run_pairs(meta, xb_of, left, right, env, lambda g: None, env_copy.wait, packed, mine, other)
+    run_pairs(meta, xb_of, left, right, env, NSEC, lambda g: None, env_copy.wait, packed, mine, other)
 
 
 def renorm_kernel(
@@ -195,25 +196,16 @@
     psi_out[...] = psi
     wide[pl.ds(0, ROWS), :] = psi.astype(jnp.float32)
     low = pl.multiple_of(meta[0] * HALF, 8)
-    high = low + HALF
     offset = 0
-    for g in range(GROUPS):
-        places = [offset]
-        for i in range(g * GROUP, (g + 1) * GROUP):
-            places.append(places[-1] + size_of(meta, i))
-        offset = places[-1]
-
-        @pl.when((places[0] < high) & (offset > low))
-        def _():
-            blocks = []
-            for i, place in zip(range(g * GROUP, (g + 1) * GROUP), places):
-                block = jnp.where(rows_below(size_of(meta, i)), wide[pl.ds(place, WIDTH), :], 0.0)
-                block = block.astype(jnp.bfloat16)
-                applied = dot(env[i], block).astype(jnp.bfloat16)
-                blocks.append(dot(block.T, applied) / math.sqrt(WIDTH))
-            for place, block in zip(places, blocks):
-                packed[pl.ds(place, WIDTH), :] = block
-
+    blocks = []
+    for i in range(NSEC):
+        block = jnp.where(rows_below(size_of(meta, i)), wide[pl.ds(offset, WIDTH), :], 0.0)
+        block = block.astype(jnp.bfloat16)
+        applied = dot(env[i], block).astype(jnp.bfloat16)
+        blocks.append((offset, dot(block.T, applied) / math.sqrt(WIDTH)))
+        offset = offset + size_of(meta, i)
+    for place, block in blocks:
+        packed[pl.ds(place, WIDTH), :] = block
     renorm_out[pl.ds(0, HALF), :] = packed[pl.ds(low, HALF), :].astype(jnp.bfloat16)
     lane = lax.broadcasted_iota(jnp.int32, (TAIL, WIDTH), 1)
     row = jnp.zeros((TAIL, WIDTH), jnp.int32)
@@ -279,7 +271,8 @@
 
 
 def all_summed(mine, other):
-    came = lax.ppermute(other, "core", [(0, 1), (1, 0)])
+    both = lax.all_gather(other, "core")
+    came = lax.dynamic_index_in_dim(both, 1 - lax.axis_index("core"), keepdims=False)
     chip = (mine + came.astype(jnp.float32)).astype(jnp.bfloat16).reshape(NEAR, PIECE, WIDTH)
     near = summed(exchange(chip, ("zl", "x")), ZH)
     far = summed(exchange(near, "zh"), NEAR)
@@ -312,7 +305,7 @@
         out_shape=sums + [rows],
         scratch_shapes=[PACKED, BLOCKS, BLOCKS, BLOCKS]
         + env_scratch
-        + [dma(GROUPS, 3), dma(1), PACKED],
+        + [dma(NSEC // FIRST_GROUP, 3), dma(1), PACKED],
         compiler_params=limit(52),
     )(meta, x0, left, right, env)
     before = all_summed(mine, other)

time: 155 us -> 151 us (0.974)
  blocking collectives: 119 us -> 124 us
  starting transfers between devices: 6.17 us -> 1.29 us
  waiting for transfers between devices: 12.4 us -> 9.32 us
    all_gather x0 -> x2, blocking collectives: none -> 5.05 us  [all_summed(): both = lax.all_gather(other, 'core')]
    ppermute x2 -> x0, starting transfers between devices: 4.88 us -> none  [all_summed(): came = lax.ppermute(other, 'core', [(0, 1), (1, 0)])]
    ppermute x2 -> x0, waiting for transfers between devices: 2.65 us -> none  [all_summed(): came = lax.ppermute(other, 'core', [(0, 1), (1, 0)])]
  transfers between devices with their start and end apart: 3 -> 1, of which waited for: 3 -> 1; matrix products, arithmetic and copies ran while one was open for 0% -> 0% of each run, Pallas kernels for 1% -> 1%
where the time goes in v5:
time: 151 us
  blocking collectives  124 us (82%)
  Pallas kernels  14.3 us (9%)
  waiting for transfers between devices  9.32 us (6%)
    all_to_all x6, blocking collectives, exchange(): return lax.all_to_all(value, axes, 0, 0)  103 us
    all_gather x2, blocking collectives, all_summed(): return lax.all_gather(half.reshape(HALF, WIDTH), 'core', tiled=True)  12.8 us
    ppermute x1, waiting for transfers between devices, shards(): lax.ppermute(renorm, 'sweep', [(i, i + 1) for i in range(positions - 1)])  9.32 us
    all_gather x2, blocking collectives, all_summed(): both = lax.all_gather(other, 'core')  5.05 us
    pallas_call x1, Pallas kernels, shards(): pl.pallas_call(first_kernel, in_specs=[SMEM] + [HBM] * 4, out_specs=[VMEM...  4.11 us
    pallas_call x1, Pallas kernels, shards(): pl.pallas_call(renorm_kernel, in_specs=[SMEM] + [VMEM] * 5, out_specs=[VM...  3.35 us
    pallas_call x1, Pallas kernels, shards(): pl.pallas_call(next_kernel, in_specs=[SMEM] + [VMEM] * 4 + [HBM], out_spe...  3.31 us
    all_gather x1, blocking collectives, shards(): came = lax.all_gather(came, 'core', tiled=True)  3.19 us
  transfers between devices with their start and end apart: 1, of which 1 were waited for; matrix products, arithmetic and copies ran while one was open for 0% of the time, Pallas kernels for 1%

profile of v5, /device:TPU:25, one launch (start us, length us, event | category | flops | bytes accessed | tf_op | source)
XLA Modules:
  0.0 150.8 jit_solution(5458602280323251804)
XLA Ops:
  0.7 0.0 copy-start.3
  0.7 0.0 copy-start.4
  0.7 0.6 copy-done.3
  1.3 0.0 copy-done.4
  1.3 0.1 pad_add_fusion.meta
  1.4 4.1 %shard_map.77 = (f32[1536,128]{1,0:T(8,128)S(1)}, bf16[1536,128]{1,0:T(8,128)(2,1)S(1)}, bf16[3072,128]{1,0:T(8,128)(2,1)S(1)}) custom-call(s32[66]{0:T(128)S(1)} %pad_add_fusion.meta, bf16[32,128,128]{2,1,0:T(8,128)(2,1)} %bitcast.36, bf16[32,128,128]{2,1,0:T(8,128)(2,1)} %bitcast.26, bf16[32,128,128]{2,1,0:T(8,128)(2,1)} %bitcast.28, ...), custom_call_target="tpu_custom_call" | custom-call | tf_op jit(solution)/shard_map/pallas_call | solution.py:301
  5.5 2.7 %all-gather = bf16[3072,128]{1,0:T(8,128)(2,1)S(1)} all-gather(bf16[1536,128]{1,0:T(8,128)(2,1)S(1)} %get-tuple-element.11), channel_id=2, replica_groups=mesh['sweep'=4,'zh'=4,'zl'=4,'x'=4,'core'=2] {'core'}, dimensions={0}, use_global_device_ids=true | all-gather | bytes 1179648 | tf_op jit(solution)/shard_map/all_gather | solution.py:274
  8.2 0.1 fusion.1
  8.3 19.9 %all_to_all.30.parts = bf16[16,96,128]{2,1,0:T(8,128)(2,1)S(1)} all-to-all(bf16[16,96,128]{2,1,0:T(8,128)(2,1)S(1)} %bitcast.33), channel_id=1, replica_groups=mesh['sweep'=4,'zh'=4,'zl'=4,'x'=4,'core'=2] {'zl','x'}, dimensions={0} | all-to-all | bytes 786432 | tf_op jit(solution)/shard_map/all_to_all | solution.py:270
  28.2 0.0 copy-start.2
  28.2 0.1 shard_map.78
  28.2 24.7 %all_to_all.31.parts = bf16[4,96,128]{2,1,0:T(8,128)(2,1)S(1)} all-to-all(bf16[4,96,128]{2,1,0:T(8,128)(2,1)S(1)} %shard_map.78), channel_id=1, replica_groups=mesh['sweep'=4,'zh'=4,'zl'=4,'x'=4,'core'=2] {'zh'}, dimensions={0} | all-to-all | bytes 196608 | tf_op jit(solution)/shard_map/all_to_all | solution.py:270
  52.9 0.0 copy-start
  53.0 14.2 %all_to_all.32 = bf16[16,96,128]{2,1,0:T(8,128)(2,1)S(1)} all-to-all(bf16[16,96,128]{2,1,0:T(8,128)(2,1)S(1)} %shard_map.79), channel_id=1, replica_groups=mesh['sweep'=4,'zh'=4,'zl'=4,'x'=4,'core'=2] {'zl','x'}, dimensions={0} | all-to-all | bytes 786432 | tf_op jit(solution)/shard_map/all_to_all | solution.py:270
  67.2 6.4 %all_gather.23.sigma.sigma_before = bf16[3072,128]{1,0:T(8,128)(2,1)S(1)} all-gather(bf16[1536,128]{1,0:T(8,128)(2,1)S(1)} %bitcast.34), channel_id=1, replica_groups=mesh['sweep'=4,'zh'=4,'zl'=4,'x'=4,'core'=2] {'core'}, dimensions={0}, use_global_device_ids=true | all-gather | bytes 1179648 | tf_op jit(solution)/shard_map/all_gather | solution.py:280
  73.6 0.0 copy-done.2
  73.6 0.0 copy-done.1
  73.6 0.0 copy-done
  73.6 3.3 %shard_map.80 = (f32[1536,128]{1,0:T(8,128)S(1)}, bf16[1536,128]{1,0:T(8,128)(2,1)S(1)}, f32[2,128]{1,0:T(2,128)S(1)}) custom-call(s32[66]{0:T(128)S(1)} %pad_add_fusion.meta, bf16[3072,128]{1,0:T(8,128)(2,1)S(1)} %all_gather.23.sigma.sigma_before, bf16[3072,128]{1,0:T(8,128)(2,1)S(1)} %get-tuple-element.12.x0, bf16[32,128,128]{2,1,0:T(8,128)(2,1)S(1)} %bitcast.27, ...), custom_call_target="tpu_custom_call" | custom-call | tf_op jit(solution)/shard_map/pallas_call | solution.py:312
  76.9 2.4 %all-gather.1 = bf16[3072,128]{1,0:T(8,128)(2,1)S(1)} all-gather(bf16[1536,128]{1,0:T(8,128)(2,1)S(1)} %get-tuple-element.15), channel_id=3, replica_groups=mesh['sweep'=4,'zh'=4,'zl'=4,'x'=4,'core'=2] {'core'}, dimensions={0}, use_global_device_ids=true | all-gather | bytes 1179648 | tf_op jit(solution)/shard_map/all_gather | solution.py:274
  79.3 0.1 fusion
  79.4 15.1 %all_to_all.33.parts = bf16[16,96,128]{2,1,0:T(8,128)(2,1)S(1)} all-to-all(bf16[16,96,128]{2,1,0:T(8,128)(2,1)S(1)} %bitcast.32), channel_id=1, replica_groups=mesh['sweep'=4,'zh'=4,'zl'=4,'x'=4,'core'=2] {'zl','x'}, dimensions={0} | all-to-all | bytes 786432 | tf_op jit(solution)/shard_map/all_to_all | solution.py:270
  94.6 0.1 shard_map.81
  94.6 15.1 %all_to_all.34.parts = bf16[4,96,128]{2,1,0:T(8,128)(2,1)S(1)} all-to-all(bf16[4,96,128]{2,1,0:T(8,128)(2,1)S(1)} %shard_map.81), channel_id=1, replica_groups=mesh['sweep'=4,'zh'=4,'zl'=4,'x'=4,'core'=2] {'zh'}, dimensions={0} | all-to-all | bytes 196608 | tf_op jit(solution)/shard_map/all_to_all | solution.py:270
  109.7 14.1 %all_to_all.35 = bf16[16,96,128]{2,1,0:T(8,128)(2,1)S(1)} all-to-all(bf16[16,96,128]{2,1,0:T(8,128)(2,1)S(1)} %shard_map.82), channel_id=1, replica_groups=mesh['sweep'=4,'zh'=4,'zl'=4,'x'=4,'core'=2] {'zl','x'}, dimensions={0} | all-to-all | bytes 786432 | tf_op jit(solution)/shard_map/all_to_all | solution.py:270
  123.8 6.4 %all_gather.26.sigma = bf16[3072,128]{1,0:T(8,128)(2,1)S(1)} all-gather(bf16[1536,128]{1,0:T(8,128)(2,1)S(1)} %bitcast.35), channel_id=1, replica_groups=mesh['sweep'=4,'zh'=4,'zl'=4,'x'=4,'core'=2] {'core'}, dimensions={0}, use_global_device_ids=true | all-gather | bytes 1179648 | tf_op jit(solution)/shard_map/all_gather | solution.py:280
  130.3 3.4 %shard_map.83 = (bf16[3072,128]{1,0:T(8,128)(2,1)S(1)}, bf16[1552,128]{1,0:T(8,128)(2,1)S(1)}) custom-call(s32[66]{0:T(128)S(1)} %pad_add_fusion.meta, f32[2,128]{1,0:T(2,128)S(1)} %get-tuple-element.13.factors, bf16[3072,128]{1,0:T(8,128)(2,1)S(1)} %all_gather.23.sigma.sigma_before, bf16[3072,128]{1,0:T(8,128)(2,1)S(1)} %all_gather.26.sigma, ...), custom_call_target="tpu_custom_call" | custom-call | tf_op jit(solution)/shard_map/pallas_call | solution.py:321
  133.6 1.3 collective-permute-start
  134.9 1.7 %shard_map.84 = bf16[32,128,128]{2,1,0:T(8,128)(2,1)} custom-call(s32[66]{0:T(128)S(1)} %pad_add_fusion.meta, bf16[3072,128]{1,0:T(8,128)(2,1)S(1)} %get-tuple-element.16.psi), custom_call_target="tpu_custom_call" | custom-call | flops 10000000 | bytes 4000000 | tf_op jit(solution)/shard_map/pallas_call | solution.py:331
  136.6 9.3 %collective-permute-done = bf16[1552,128]{1,0:T(8,128)(2,1)S(1)} collective-permute-done((bf16[1552,128]{1,0:T(8,128)(2,1)S(1)}, bf16[1552,128]{1,0:T(8,128)(2,1)S(1)}, u32[]{:S(2)}, u32[]{:S(2)}) %collective-permute-start) | collective-permute-done | bytes 397344 | tf_op jit(solution)/shard_map/ppermute | solution.py:330
  145.9 3.2 %all_gather.27.came = bf16[3104,128]{1,0:T(8,128)(2,1)S(1)} all-gather(bf16[1552,128]{1,0:T(8,128)(2,1)S(1)} %collective-permute-done), channel_id=1, replica_groups=mesh['sweep'=4,'zh'=4,'zl'=4,'x'=4,'core'=2] {'core'}, dimensions={0}, use_global_device_ids=true | all-gather | bytes 1191936 | tf_op jit(solution)/shard_map/all_gather | solution.py:340
  149.1 1.7 %shard_map.85 = bf16[32,128,128]{2,1,0:T(8,128)(2,1)} custom-call(bf16[3104,128]{1,0:T(8,128)(2,1)S(1)} %all_gather.27.came, bf16[32,128,128]{2,1,0:T(8,128)(2,1)S(1)} %bitcast.25), custom_call_target="tpu_custom_call" | custom-call | tf_op jit(solution)/shard_map/pallas_call | solution.py:341
  (3 shorter events, 0.1 us)
Async XLA Ops:
  0.7 0.7 copy-start.3
  0.7 0.7 copy-start.4
  28.2 45.4 %copy-start.2 = (bf16[1,1,32,128,128]{4,3,2,1,0:T(8,128)(2,1)S(1)}, bf16[1,1,32,128,128]{4,3,2,1,0:T(8,128)(2,1)}, u32[]{:S(2)}) copy-start(bf16[1,1,32,128,128]{4,3,2,1,0:T(8,128)(2,1)} %param.8) | copy-start | bytes 3145732
  52.9 20.7 %copy-start.1 = (bf16[1,1,32,128,128]{4,3,2,1,0:T(8,128)(2,1)S(1)}, bf16[1,1,32,128,128]{4,3,2,1,0:T(8,128)(2,1)}, u32[]{:S(2)}) copy-start(bf16[1,1,32,128,128]{4,3,2,1,0:T(8,128)(2,1)} %param.7) | copy-start | bytes 3145732
  52.9 20.7 %copy-start = (bf16[1,32,128,128]{3,2,1,0:T(8,128)(2,1)S(1)}, bf16[1,32,128,128]{3,2,1,0:T(8,128)(2,1)}, u32[]{:S(2)}) copy-start(bf16[1,32,128,128]{3,2,1,0:T(8,128)(2,1)} %param.11) | copy-start | bytes 3145732
  133.6 12.3 %collective-permute-start = (bf16[1552,128]{1,0:T(8,128)(2,1)S(1)}, bf16[1552,128]{1,0:T(8,128)(2,1)S(1)}, u32[]{:S(2)}, u32[]{:S(2)}) collective-permute-start(bf16[1552,128]{1,0:T(8,128)(2,1)S(1)} %get-tuple-element.17), channel_id=1, source_target_pairs={{0,128},{128,256},{256,384},{1,129},{129,257},{257,385},{2,130},{1... | collective-permute-start | bytes 1191944 | tf_op jit(solution)/shard_map/ppermute | solution.py:330

commit v6 on v5

--- a/solution.py
+++ b/solution.py
@@ -20,6 +20,7 @@
 GROUP = 8
 GROUPS = NSEC // GROUP
 FIRST_GROUP = 16
+REACH = NSEC - HALF // WIDTH
 TAIL = 16
 CHUNK = 256
 
@@ -180,25 +181,33 @@
     run_pairs(meta, xb_of, left, right, env, NSEC, lambda g: None, env_copy.wait, packed, mine, other)
 
 
+def second_state(factors, x0, sigma_before):
+    grow, drop = factors[0:1, :], factors[1:2, :]
+
+    def x_of(rows):
+        return grow * x0[rows, :].astype(jnp.float32) - drop * sigma_before[rows, :].astype(
+            jnp.float32
+        )
+
+    return x_of
+
+
 def renorm_kernel(
-    meta, factors, sigma_before, sigma, x0, env, psi_out, renorm_out, wide, packed
+    meta, factors, sigma_before, sigma, x0, env, factors_out, renorm_out, wide, packed
 ):
-    grow_before, drop_before = factors[0:1, :], factors[1:2, :]
-
-    def x_of(rows):
-        return grow_before * x0[rows, :].astype(jnp.float32) - drop_before * sigma_before[
-            rows, :
-        ].astype(jnp.float32)
-
+    x_of = second_state(factors, x0, sigma_before)
     grow, drop = step_factors(x_of, sigma)
-    psi = grow * x_of(pl.ds(0, ROWS)) - drop * sigma[...].astype(jnp.float32)
-    psi = psi.astype(jnp.bfloat16)
-    psi_out[...] = psi
-    wide[pl.ds(0, ROWS), :] = psi.astype(jnp.float32)
-    low = pl.multiple_of(meta[0] * HALF, 8)
-    offset = 0
+    factors_out[0:1, :] = jnp.broadcast_to(grow, (1, WIDTH))
+    factors_out[1:2, :] = jnp.broadcast_to(drop, (1, WIDTH))
+    core = meta[0]
+    near = pl.ds(pl.multiple_of(core * (HALF - WIDTH), 16), HALF + WIDTH)
+    psi = grow * x_of(near) - drop * sigma[near, :].astype(jnp.float32)
+    wide[near, :] = psi.astype(jnp.bfloat16).astype(jnp.float32)
+    first = core * (NSEC - REACH)
+    offset = lax.fori_loop(0, first, lambda i, total: total + size_of(meta, i), jnp.int32(0))
     blocks = []
-    for i in range(NSEC):
+    for j in range(REACH):
+        i = first + j
         block = jnp.where(rows_below(size_of(meta, i)), wide[pl.ds(offset, WIDTH), :], 0.0)
         block = block.astype(jnp.bfloat16)
         applied = dot(env[i], block).astype(jnp.bfloat16)
@@ -206,7 +215,9 @@
         offset = offset + size_of(meta, i)
     for place, block in blocks:
         packed[pl.ds(place, WIDTH), :] = block
-    renorm_out[pl.ds(0, HALF), :] = packed[pl.ds(low, HALF), :].astype(jnp.bfloat16)
+    renorm_out[pl.ds(0, HALF), :] = packed[
+        pl.ds(pl.multiple_of(core * HALF, 8), HALF), :
+    ].astype(jnp.bfloat16)
     lane = lax.broadcasted_iota(jnp.int32, (TAIL, WIDTH), 1)
     row = jnp.zeros((TAIL, WIDTH), jnp.int32)
     for i in range(NSEC):
@@ -228,8 +239,11 @@
         group[0].wait()
 
 
-def psi_kernel(meta, psi, out, wide, result, sems):
-    wide[pl.ds(0, ROWS), :] = psi[...].astype(jnp.float32)
+def psi_kernel(meta, factors, factors_last, sigma_before, sigma, x0, out, wide, result, sems):
+    grow, drop = factors_last[0:1, :], factors_last[1:2, :]
+    rows = pl.ds(0, ROWS)
+    x = second_state(factors, x0, sigma_before)(rows)
+    wide[rows, :] = grow * x - drop * sigma[...].astype(jnp.float32)
     unpack(lambda i: size_of(meta, i), wide, result, out, sems, lambda i, block: block)
 
 
@@ -318,11 +332,14 @@
         compiler_params=limit(12),
     )(meta, before, x0, left, right, env)
     sigma = all_summed(mine, other)
-    psi, renorm = pl.pallas_call(
+    factors_last, renorm = pl.pallas_call(
         renorm_kernel,
         in_specs=[SMEM] + [VMEM] * 5,
         out_specs=[VMEM] * 2,
-        out_shape=[rows, shape((HALF + TAIL, WIDTH), jnp.bfloat16)],
+        out_shape=[
+            shape((2, WIDTH), jnp.float32),
+            shape((HALF + TAIL, WIDTH), jnp.bfloat16),
+        ],
         scratch_shapes=[PACKED, PACKED],
         compiler_params=limit(12),
     )(meta, factors, before, sigma, x0, env)
@@ -330,13 +347,13 @@
     came = lax.ppermute(renorm, "sweep", [(i, i + 1) for i in range(positions - 1)])
     psi = pl.pallas_call(
         psi_kernel,
-        in_specs=[SMEM, VMEM],
+        in_specs=[SMEM] + [VMEM] * 5,
         out_specs=HBM,
         out_shape=blocks,
         scratch_shapes=[PACKED, BLOCKS, dma(GROUPS, 1)],
         compiler_params=limit(8),
         cost_estimate=pl.CostEstimate(flops=10**7, bytes_accessed=4 * 10**6, transcendentals=0),
-    )(meta, psi)
+    )(meta, factors, factors_last, before, sigma, x0)
     came = lax.all_gather(came, "core", tiled=True)
     next_left = pl.pallas_call(
         shift_kernel,

time: 151 us -> 150 us (level)
  transfers between devices with their start and end apart: 1 -> 1, of which waited for: 1 -> 1; matrix products, arithmetic and copies ran while one was open for 0% -> 0% of each run, Pallas kernels for 1% -> 2%
where the time goes in v6:
time: 150 us
  blocking collectives  124 us (83%)
  Pallas kernels  14.3 us (10%)
  waiting for transfers between devices  8.57 us (6%)
    all_to_all x6, blocking collectives, exchange(): return lax.all_to_all(value, axes, 0, 0)  103 us
    all_gather x2, blocking collectives, all_summed(): return lax.all_gather(half.reshape(HALF, WIDTH), 'core', tiled=True)  12.8 us
    ppermute x1, waiting for transfers between devices, shards(): lax.ppermute(renorm, 'sweep', [(i, i + 1) for i in range(positions - 1)])  8.57 us
    all_gather x2, blocking collectives, all_summed(): both = lax.all_gather(other, 'core')  5.05 us
    pallas_call x1, Pallas kernels, shards(): pl.pallas_call(first_kernel, in_specs=[SMEM] + [HBM] * 4, out_specs=[VMEM...  4.11 us
    pallas_call x1, Pallas kernels, shards(): pl.pallas_call(next_kernel, in_specs=[SMEM] + [VMEM] * 4 + [HBM], out_spe...  3.32 us
    all_gather x1, blocking collectives, shards(): came = lax.all_gather(came, 'core', tiled=True)  3.13 us
  transfers between devices with their start and end apart: 1, of which 1 were waited for; matrix products, arithmetic and copies ran while one was open for 0% of the time, Pallas kernels for 2%

profile of v6, /device:TPU:25, one launch (start us, length us, event | category | flops | bytes accessed | tf_op | source)
XLA Modules:
  0.0 150.0 jit_solution(13771650921183426445)
XLA Ops:
  0.7 0.0 copy-start.3
  0.7 0.0 copy-start.4
  0.7 0.6 copy-done.3
  1.3 0.0 copy-done.4
  1.3 0.1 pad_add_fusion.meta
  1.4 4.1 %shard_map.77 = (f32[1536,128]{1,0:T(8,128)S(1)}, bf16[1536,128]{1,0:T(8,128)(2,1)S(1)}, bf16[3072,128]{1,0:T(8,128)(2,1)S(1)}) custom-call(s32[66]{0:T(128)S(1)} %pad_add_fusion.meta, bf16[32,128,128]{2,1,0:T(8,128)(2,1)} %bitcast.36, bf16[32,128,128]{2,1,0:T(8,128)(2,1)} %bitcast.26, bf16[32,128,128]{2,1,0:T(8,128)(2,1)} %bitcast.28, ...), custom_call_target="tpu_custom_call" | custom-call | tf_op jit(solution)/shard_map/pallas_call | solution.py:315
  5.5 2.7 %all-gather = bf16[3072,128]{1,0:T(8,128)(2,1)S(1)} all-gather(bf16[1536,128]{1,0:T(8,128)(2,1)S(1)} %get-tuple-element.11), channel_id=2, replica_groups=mesh['sweep'=4,'zh'=4,'zl'=4,'x'=4,'core'=2] {'core'}, dimensions={0}, use_global_device_ids=true | all-gather | bytes 1179648 | tf_op jit(solution)/shard_map/all_gather | solution.py:288
  8.2 0.1 fusion.1
  8.3 19.9 %all_to_all.30.parts = bf16[16,96,128]{2,1,0:T(8,128)(2,1)S(1)} all-to-all(bf16[16,96,128]{2,1,0:T(8,128)(2,1)S(1)} %bitcast.33), channel_id=1, replica_groups=mesh['sweep'=4,'zh'=4,'zl'=4,'x'=4,'core'=2] {'zl','x'}, dimensions={0} | all-to-all | bytes 786432 | tf_op jit(solution)/shard_map/all_to_all | solution.py:284
  28.2 0.0 copy-start.2
  28.2 0.1 shard_map.78
  28.3 24.7 %all_to_all.31.parts = bf16[4,96,128]{2,1,0:T(8,128)(2,1)S(1)} all-to-all(bf16[4,96,128]{2,1,0:T(8,128)(2,1)S(1)} %shard_map.78), channel_id=1, replica_groups=mesh['sweep'=4,'zh'=4,'zl'=4,'x'=4,'core'=2] {'zh'}, dimensions={0} | all-to-all | bytes 196608 | tf_op jit(solution)/shard_map/all_to_all | solution.py:284
  52.9 0.0 copy-start
  53.0 14.2 %all_to_all.32 = bf16[16,96,128]{2,1,0:T(8,128)(2,1)S(1)} all-to-all(bf16[16,96,128]{2,1,0:T(8,128)(2,1)S(1)} %shard_map.79), channel_id=1, replica_groups=mesh['sweep'=4,'zh'=4,'zl'=4,'x'=4,'core'=2] {'zl','x'}, dimensions={0} | all-to-all | bytes 786432 | tf_op jit(solution)/shard_map/all_to_all | solution.py:284
  67.2 6.4 %all_gather.23.sigma.sigma_before = bf16[3072,128]{1,0:T(8,128)(2,1)S(1)} all-gather(bf16[1536,128]{1,0:T(8,128)(2,1)S(1)} %bitcast.34), channel_id=1, replica_groups=mesh['sweep'=4,'zh'=4,'zl'=4,'x'=4,'core'=2] {'core'}, dimensions={0}, use_global_device_ids=true | all-gather | bytes 1179648 | tf_op jit(solution)/shard_map/all_gather | solution.py:294
  73.6 0.0 copy-done.2
  73.6 0.0 copy-done.1
  73.6 0.0 copy-done
  73.6 3.3 %shard_map.80 = (f32[1536,128]{1,0:T(8,128)S(1)}, bf16[1536,128]{1,0:T(8,128)(2,1)S(1)}, f32[2,128]{1,0:T(2,128)S(1)}) custom-call(s32[66]{0:T(128)S(1)} %pad_add_fusion.meta, bf16[3072,128]{1,0:T(8,128)(2,1)S(1)} %all_gather.23.sigma.sigma_before, bf16[3072,128]{1,0:T(8,128)(2,1)S(1)} %get-tuple-element.12.x0, bf16[32,128,128]{2,1,0:T(8,128)(2,1)S(1)} %bitcast.27, ...), custom_call_target="tpu_custom_call" | custom-call | tf_op jit(solution)/shard_map/pallas_call | solution.py:326
  76.9 2.4 %all-gather.1 = bf16[3072,128]{1,0:T(8,128)(2,1)S(1)} all-gather(bf16[1536,128]{1,0:T(8,128)(2,1)S(1)} %get-tuple-element.15), channel_id=3, replica_groups=mesh['sweep'=4,'zh'=4,'zl'=4,'x'=4,'core'=2] {'core'}, dimensions={0}, use_global_device_ids=true | all-gather | bytes 1179648 | tf_op jit(solution)/shard_map/all_gather | solution.py:288
  79.3 0.1 fusion
  79.4 15.1 %all_to_all.33.parts = bf16[16,96,128]{2,1,0:T(8,128)(2,1)S(1)} all-to-all(bf16[16,96,128]{2,1,0:T(8,128)(2,1)S(1)} %bitcast.32), channel_id=1, replica_groups=mesh['sweep'=4,'zh'=4,'zl'=4,'x'=4,'core'=2] {'zl','x'}, dimensions={0} | all-to-all | bytes 786432 | tf_op jit(solution)/shard_map/all_to_all | solution.py:284
  94.6 0.1 shard_map.81
  94.7 15.1 %all_to_all.34.parts = bf16[4,96,128]{2,1,0:T(8,128)(2,1)S(1)} all-to-all(bf16[4,96,128]{2,1,0:T(8,128)(2,1)S(1)} %shard_map.81), channel_id=1, replica_groups=mesh['sweep'=4,'zh'=4,'zl'=4,'x'=4,'core'=2] {'zh'}, dimensions={0} | all-to-all | bytes 196608 | tf_op jit(solution)/shard_map/all_to_all | solution.py:284
  109.8 14.1 %all_to_all.35 = bf16[16,96,128]{2,1,0:T(8,128)(2,1)S(1)} all-to-all(bf16[16,96,128]{2,1,0:T(8,128)(2,1)S(1)} %shard_map.82), channel_id=1, replica_groups=mesh['sweep'=4,'zh'=4,'zl'=4,'x'=4,'core'=2] {'zl','x'}, dimensions={0} | all-to-all | bytes 786432 | tf_op jit(solution)/shard_map/all_to_all | solution.py:284
  123.9 6.4 %all_gather.26.sigma = bf16[3072,128]{1,0:T(8,128)(2,1)S(1)} all-gather(bf16[1536,128]{1,0:T(8,128)(2,1)S(1)} %bitcast.35), channel_id=1, replica_groups=mesh['sweep'=4,'zh'=4,'zl'=4,'x'=4,'core'=2] {'core'}, dimensions={0}, use_global_device_ids=true | all-gather | bytes 1179648 | tf_op jit(solution)/shard_map/all_gather | solution.py:294
  130.3 2.5 %shard_map.83 = (f32[2,128]{1,0:T(2,128)S(1)}, bf16[1552,128]{1,0:T(8,128)(2,1)S(1)}) custom-call(s32[66]{0:T(128)S(1)} %pad_add_fusion.meta, f32[2,128]{1,0:T(2,128)S(1)} %get-tuple-element.13.factors, bf16[3072,128]{1,0:T(8,128)(2,1)S(1)} %all_gather.23.sigma.sigma_before, bf16[3072,128]{1,0:T(8,128)(2,1)S(1)} %all_gather.26.sigma, ...), custom_call_target="tpu_custom_call" | custom-call | tf_op jit(solution)/shard_map/pallas_call | solution.py:335
  132.8 1.3 collective-permute-start
  134.1 2.5 %shard_map.84 = bf16[32,128,128]{2,1,0:T(8,128)(2,1)} custom-call(s32[66]{0:T(128)S(1)} %pad_add_fusion.meta, f32[2,128]{1,0:T(2,128)S(1)} %get-tuple-element.13.factors, f32[2,128]{1,0:T(2,128)S(1)} %get-tuple-element.16.factors_last, bf16[3072,128]{1,0:T(8,128)(2,1)S(1)} %all_gather.23.sigma.sigma_before, bf16[3072,128]{1,0:T(8,128)(2,1)S(1)} %all_gather.26.sigma, ...), custom_call_target="tpu_custom_call" | custom-call | flops 10000000 | bytes 4000000 | tf_op jit(solution)/shard_map/pallas_call | solution.py:348
  136.6 8.6 %collective-permute-done = bf16[1552,128]{1,0:T(8,128)(2,1)S(1)} collective-permute-done((bf16[1552,128]{1,0:T(8,128)(2,1)S(1)}, bf16[1552,128]{1,0:T(8,128)(2,1)S(1)}, u32[]{:S(2)}, u32[]{:S(2)}) %collective-permute-start) | collective-permute-done | bytes 397344 | tf_op jit(solution)/shard_map/ppermute | solution.py:347
  145.2 3.1 %all_gather.27.came = bf16[3104,128]{1,0:T(8,128)(2,1)S(1)} all-gather(bf16[1552,128]{1,0:T(8,128)(2,1)S(1)} %collective-permute-done), channel_id=1, replica_groups=mesh['sweep'=4,'zh'=4,'zl'=4,'x'=4,'core'=2] {'core'}, dimensions={0}, use_global_device_ids=true | all-gather | bytes 1191936 | tf_op jit(solution)/shard_map/all_gather | solution.py:357
  148.3 1.7 %shard_map.85 = bf16[32,128,128]{2,1,0:T(8,128)(2,1)} custom-call(bf16[3104,128]{1,0:T(8,128)(2,1)S(1)} %all_gather.27.came, bf16[32,128,128]{2,1,0:T(8,128)(2,1)S(1)} %bitcast.25), custom_call_target="tpu_custom_call" | custom-call | tf_op jit(solution)/shard_map/pallas_call | solution.py:358
  (3 shorter events, 0.1 us)
Async XLA Ops:
  0.7 0.7 copy-start.3
  0.7 0.7 copy-start.4
  28.2 45.4 %copy-start.2 = (bf16[1,1,32,128,128]{4,3,2,1,0:T(8,128)(2,1)S(1)}, bf16[1,1,32,128,128]{4,3,2,1,0:T(8,128)(2,1)}, u32[]{:S(2)}) copy-start(bf16[1,1,32,128,128]{4,3,2,1,0:T(8,128)(2,1)} %param.8) | copy-start | bytes 3145732
  52.9 20.7 %copy-start.1 = (bf16[1,1,32,128,128]{4,3,2,1,0:T(8,128)(2,1)S(1)}, bf16[1,1,32,128,128]{4,3,2,1,0:T(8,128)(2,1)}, u32[]{:S(2)}) copy-start(bf16[1,1,32,128,128]{4,3,2,1,0:T(8,128)(2,1)} %param.7) | copy-start | bytes 3145732
  52.9 20.7 %copy-start = (bf16[1,32,128,128]{3,2,1,0:T(8,128)(2,1)S(1)}, bf16[1,32,128,128]{3,2,1,0:T(8,128)(2,1)}, u32[]{:S(2)}) copy-start(bf16[1,32,128,128]{3,2,1,0:T(8,128)(2,1)} %param.11) | copy-start | bytes 3145732
  132.8 12.4 %collective-permute-start = (bf16[1552,128]{1,0:T(8,128)(2,1)S(1)}, bf16[1552,128]{1,0:T(8,128)(2,1)S(1)}, u32[]{:S(2)}, u32[]{:S(2)}) collective-permute-start(bf16[1552,128]{1,0:T(8,128)(2,1)S(1)} %get-tuple-element.17), channel_id=1, source_target_pairs={{0,128},{128,256},{256,384},{1,129},{129,257},{257,385},{2,130},{1... | collective-permute-start | bytes 1191944 | tf_op jit(solution)/shard_map/ppermute | solution.py:347

commit v7 on v6

--- a/solution.py
+++ b/solution.py
@@ -78,10 +78,10 @@
     return [jnp.sum(t, axis=(0, 1), keepdims=True) for t in totals]
 
 
-def step_factors(x_of, sigma):
+def step_factors(x, sigma):
     def products(rows):
-        x, s = x_of(rows), sigma[rows, :].astype(jnp.float32)
-        return [(x, x), (x, s), (s, s)]
+        xs, s = x[rows, :].astype(jnp.float32), sigma[rows, :].astype(jnp.float32)
+        return [(xs, xs), (xs, s), (s, s)]
 
     xx, xs, ss = flat_sums(products)
     rho = xs / xx
@@ -161,18 +161,14 @@
 
 
 def next_kernel(
-    meta, sigma, x0, left, right, env_in, mine, other, factors, packed, env, env_sem, wide
+    meta, sigma, x0, left, right, env_in, mine, other, wide, packed, env, env_sem
 ):
     env_copy = pltpu.make_async_copy(env_in.at[meta[1]], env, env_sem.at[0])
     env_copy.start()
 
-    def x_of(rows):
-        return x0[rows, :].astype(jnp.float32)
-
-    grow, drop = step_factors(x_of, sigma)
-    factors[0:1, :] = jnp.broadcast_to(grow, (1, WIDTH))
-    factors[1:2, :] = jnp.broadcast_to(drop, (1, WIDTH))
-    wide[pl.ds(0, ROWS), :] = grow * x_of(pl.ds(0, ROWS)) - drop * sigma[...].astype(jnp.float32)
+    rows = pl.ds(0, ROWS)
+    grow, drop = step_factors(x0, sigma)
+    wide[rows, :] = grow * x0[...].astype(jnp.float32) - drop * sigma[...].astype(jnp.float32)
 
     def xb_of(i, offset, keep=True):
         mask = rows_below(size_of(meta, i))
@@ -181,27 +177,15 @@
     run_pairs(meta, xb_of, left, right, env, NSEC, lambda g: None, env_copy.wait, packed, mine, other)
 
 
-def second_state(factors, x0, sigma_before):
-    grow, drop = factors[0:1, :], factors[1:2, :]
-
-    def x_of(rows):
-        return grow * x0[rows, :].astype(jnp.float32) - drop * sigma_before[rows, :].astype(
-            jnp.float32
-        )
-
-    return x_of
-
-
 def renorm_kernel(
-    meta, factors, sigma_before, sigma, x0, env, factors_out, renorm_out, wide, packed
+    meta, x, sigma, env, factors_out, renorm_out, wide, packed
 ):
-    x_of = second_state(factors, x0, sigma_before)
-    grow, drop = step_factors(x_of, sigma)
+    grow, drop = step_factors(x, sigma)
     factors_out[0:1, :] = jnp.broadcast_to(grow, (1, WIDTH))
     factors_out[1:2, :] = jnp.broadcast_to(drop, (1, WIDTH))
     core = meta[0]
     near = pl.ds(pl.multiple_of(core * (HALF - WIDTH), 16), HALF + WIDTH)
-    psi = grow * x_of(near) - drop * sigma[near, :].astype(jnp.float32)
+    psi = grow * x[near, :] - drop * sigma[near, :].astype(jnp.float32)
     wide[near, :] = psi.astype(jnp.bfloat16).astype(jnp.float32)
     first = core * (NSEC - REACH)
     offset = lax.fori_loop(0, first, lambda i, total: total + size_of(meta, i), jnp.int32(0))
@@ -239,11 +223,10 @@
         group[0].wait()
 
 
-def psi_kernel(meta, factors, factors_last, sigma_before, sigma, x0, out, wide, result, sems):
-    grow, drop = factors_last[0:1, :], factors_last[1:2, :]
+def psi_kernel(meta, factors, x, sigma, out, wide, result, sems):
+    grow, drop = factors[0:1, :], factors[1:2, :]
     rows = pl.ds(0, ROWS)
-    x = second_state(factors, x0, sigma_before)(rows)
-    wide[rows, :] = grow * x - drop * sigma[...].astype(jnp.float32)
+    wide[rows, :] = grow * x[rows, :] - drop * sigma[...].astype(jnp.float32)
     unpack(lambda i: size_of(meta, i), wide, result, out, sems, lambda i, block: block)
 
 
@@ -309,32 +292,32 @@
     meta = jnp.concatenate([own, sector_size[0], pair_sectors[0, 0]])
 
     sums = [shape((HALF, WIDTH), jnp.float32), shape((HALF, WIDTH), jnp.bfloat16)]
-    rows = shape((ROWS, WIDTH), jnp.bfloat16)
+    state = shape((ROWS + WIDTH, WIDTH), jnp.float32)
     blocks = shape((NSEC, WIDTH, WIDTH), jnp.bfloat16)
     env_scratch = [pltpu.VMEM((WIDTH, WIDTH), jnp.bfloat16)]
     mine, other, x0 = pl.pallas_call(
         first_kernel,
         in_specs=[SMEM] + [HBM] * 4,
         out_specs=[VMEM] * 3,
-        out_shape=sums + [rows],
+        out_shape=sums + [shape((ROWS, WIDTH), jnp.bfloat16)],
         scratch_shapes=[PACKED, BLOCKS, BLOCKS, BLOCKS]
         + env_scratch
         + [dma(NSEC // FIRST_GROUP, 3), dma(1), PACKED],
         compiler_params=limit(52),
     )(meta, x0, left, right, env)
-    before = all_summed(mine, other)
-    mine, other, factors = pl.pallas_call(
+    sigma = all_summed(mine, other)
+    mine, other, x = pl.pallas_call(
         next_kernel,
         in_specs=[SMEM] + [VMEM] * 4 + [HBM],
         out_specs=[VMEM] * 3,
-        out_shape=sums + [shape((2, WIDTH), jnp.float32)],
-        scratch_shapes=[PACKED] + env_scratch + [dma(1), PACKED],
+        out_shape=sums + [state],
+        scratch_shapes=[PACKED] + env_scratch + [dma(1)],
         compiler_params=limit(12),
-    )(meta, before, x0, left, right, env)
+    )(meta, sigma, x0, left, right, env)
     sigma = all_summed(mine, other)
-    factors_last, renorm = pl.pallas_call(
+    factors, renorm = pl.pallas_call(
         renorm_kernel,
-        in_specs=[SMEM] + [VMEM] * 5,
+        in_specs=[SMEM] + [VMEM] * 3,
         out_specs=[VMEM] * 2,
         out_shape=[
             shape((2, WIDTH), jnp.float32),
@@ -342,18 +325,18 @@
         ],
         scratch_shapes=[PACKED, PACKED],
         compiler_params=limit(12),
-    )(meta, factors, before, sigma, x0, env)
+    )(meta, x, sigma, env)
     positions = lax.axis_size("sweep")
     came = lax.ppermute(renorm, "sweep", [(i, i + 1) for i in range(positions - 1)])
     psi = pl.pallas_call(
         psi_kernel,
-        in_specs=[SMEM] + [VMEM] * 5,
+        in_specs=[SMEM] + [VMEM] * 3,
         out_specs=HBM,
         out_shape=blocks,
         scratch_shapes=[PACKED, BLOCKS, dma(GROUPS, 1)],
         compiler_params=limit(8),
         cost_estimate=pl.CostEstimate(flops=10**7, bytes_accessed=4 * 10**6, transcendentals=0),
-    )(meta, factors, factors_last, before, sigma, x0)
+    )(meta, factors, x, sigma)
     came = lax.all_gather(came, "core", tiled=True)
     next_left = pl.pallas_call(
         shift_kernel,

time: 150 us -> 150 us (level)
  transfers between devices with their start and end apart: 1 -> 1, of which waited for: 1 -> 1; matrix products, arithmetic and copies ran while one was open for 0% -> 0% of each run, Pallas kernels for 2% -> 1%
where the time goes in v7:
time: 150 us
  blocking collectives  124 us (83%)
  Pallas kernels  13.4 us (9%)
  waiting for transfers between devices  9.04 us (6%)
    all_to_all x6, blocking collectives, exchange(): return lax.all_to_all(value, axes, 0, 0)  103 us
    all_gather x2, blocking collectives, all_summed(): return lax.all_gather(half.reshape(HALF, WIDTH), 'core', tiled=True)  12.8 us
    ppermute x1, waiting for transfers between devices, shards(): lax.ppermute(renorm, 'sweep', [(i, i + 1) for i in range(positions - 1)])  9.04 us
    all_gather x2, blocking collectives, all_summed(): both = lax.all_gather(other, 'core')  5.05 us
    pallas_call x1, Pallas kernels, shards(): pl.pallas_call(first_kernel, in_specs=[SMEM] + [HBM] * 4, out_specs=[VMEM...  4.1 us
    pallas_call x1, Pallas kernels, shards(): pl.pallas_call(next_kernel, in_specs=[SMEM] + [VMEM] * 4 + [HBM], out_spe...  3.29 us
    all_gather x1, blocking collectives, shards(): came = lax.all_gather(came, 'core', tiled=True)  3.13 us
  transfers between devices with their start and end apart: 1, of which 1 were waited for; matrix products, arithmetic and copies ran while one was open for 0% of the time, Pallas kernels for 1%

profile of v7, /device:TPU:25, one launch (start us, length us, event | category | flops | bytes accessed | tf_op | source)
XLA Modules:
  0.0 149.6 jit_solution(156100207171933379)
XLA Ops:
  0.7 0.8 pad_add_fusion.meta
  1.4 4.1 %shard_map.77 = (f32[1536,128]{1,0:T(8,128)S(1)}, bf16[1536,128]{1,0:T(8,128)(2,1)S(1)}, bf16[3072,128]{1,0:T(8,128)(2,1)S(1)}) custom-call(s32[66]{0:T(128)S(1)} %pad_add_fusion.meta, bf16[32,128,128]{2,1,0:T(8,128)(2,1)} %bitcast.36, bf16[32,128,128]{2,1,0:T(8,128)(2,1)} %bitcast.26, bf16[32,128,128]{2,1,0:T(8,128)(2,1)} %bitcast.28, ...), custom_call_target="tpu_custom_call" | custom-call | tf_op jit(solution)/shard_map/pallas_call | solution.py:298
  5.5 2.7 %all-gather = bf16[3072,128]{1,0:T(8,128)(2,1)S(1)} all-gather(bf16[1536,128]{1,0:T(8,128)(2,1)S(1)} %get-tuple-element.11), channel_id=2, replica_groups=mesh['sweep'=4,'zh'=4,'zl'=4,'x'=4,'core'=2] {'core'}, dimensions={0}, use_global_device_ids=true | all-gather | bytes 1179648 | tf_op jit(solution)/shard_map/all_gather | solution.py:271
  8.2 0.1 fusion.1
  8.3 19.9 %all_to_all.30.parts = bf16[16,96,128]{2,1,0:T(8,128)(2,1)S(1)} all-to-all(bf16[16,96,128]{2,1,0:T(8,128)(2,1)S(1)} %bitcast.33), channel_id=1, replica_groups=mesh['sweep'=4,'zh'=4,'zl'=4,'x'=4,'core'=2] {'zl','x'}, dimensions={0} | all-to-all | bytes 786432 | tf_op jit(solution)/shard_map/all_to_all | solution.py:267
  28.2 0.0 copy-start
  28.2 0.0 copy-start.1
  28.2 0.0 copy-start.2
  28.2 0.1 shard_map.78
  28.3 24.8 %all_to_all.31.parts = bf16[4,96,128]{2,1,0:T(8,128)(2,1)S(1)} all-to-all(bf16[4,96,128]{2,1,0:T(8,128)(2,1)S(1)} %shard_map.78), channel_id=1, replica_groups=mesh['sweep'=4,'zh'=4,'zl'=4,'x'=4,'core'=2] {'zh'}, dimensions={0} | all-to-all | bytes 196608 | tf_op jit(solution)/shard_map/all_to_all | solution.py:267
  53.1 14.1 %all_to_all.32 = bf16[16,96,128]{2,1,0:T(8,128)(2,1)S(1)} all-to-all(bf16[16,96,128]{2,1,0:T(8,128)(2,1)S(1)} %shard_map.79), channel_id=1, replica_groups=mesh['sweep'=4,'zh'=4,'zl'=4,'x'=4,'core'=2] {'zl','x'}, dimensions={0} | all-to-all | bytes 786432 | tf_op jit(solution)/shard_map/all_to_all | solution.py:267
  67.2 6.4 %all_gather.23.sigma = bf16[3072,128]{1,0:T(8,128)(2,1)S(1)} all-gather(bf16[1536,128]{1,0:T(8,128)(2,1)S(1)} %bitcast.34), channel_id=1, replica_groups=mesh['sweep'=4,'zh'=4,'zl'=4,'x'=4,'core'=2] {'core'}, dimensions={0}, use_global_device_ids=true | all-gather | bytes 1179648 | tf_op jit(solution)/shard_map/all_gather | solution.py:277
  73.6 0.0 copy-done
  73.6 0.0 copy-done.1
  73.6 0.0 copy-done.2
  73.6 3.3 %shard_map.80 = (f32[1536,128]{1,0:T(8,128)S(1)}, bf16[1536,128]{1,0:T(8,128)(2,1)S(1)}, f32[3200,128]{1,0:T(8,128)S(1)}) custom-call(s32[66]{0:T(128)S(1)} %pad_add_fusion.meta, bf16[3072,128]{1,0:T(8,128)(2,1)S(1)} %all_gather.23.sigma, bf16[3072,128]{1,0:T(8,128)(2,1)S(1)} %get-tuple-element.12.x0, bf16[32,128,128]{2,1,0:T(8,128)(2,1)S(1)} %bitcast.27, ...), custom_call_target="tpu_custom_call" | custom-call | tf_op jit(solution)/shard_map/pallas_call | solution.py:309
  76.9 2.4 %all-gather.1 = bf16[3072,128]{1,0:T(8,128)(2,1)S(1)} all-gather(bf16[1536,128]{1,0:T(8,128)(2,1)S(1)} %get-tuple-element.15), channel_id=3, replica_groups=mesh['sweep'=4,'zh'=4,'zl'=4,'x'=4,'core'=2] {'core'}, dimensions={0}, use_global_device_ids=true | all-gather | bytes 1179648 | tf_op jit(solution)/shard_map/all_gather | solution.py:271
  79.3 0.1 fusion
  79.4 15.1 %all_to_all.33.parts = bf16[16,96,128]{2,1,0:T(8,128)(2,1)S(1)} all-to-all(bf16[16,96,128]{2,1,0:T(8,128)(2,1)S(1)} %bitcast.32), channel_id=1, replica_groups=mesh['sweep'=4,'zh'=4,'zl'=4,'x'=4,'core'=2] {'zl','x'}, dimensions={0} | all-to-all | bytes 786432 | tf_op jit(solution)/shard_map/all_to_all | solution.py:267
  94.6 0.1 shard_map.81
  94.6 15.1 %all_to_all.34.parts = bf16[4,96,128]{2,1,0:T(8,128)(2,1)S(1)} all-to-all(bf16[4,96,128]{2,1,0:T(8,128)(2,1)S(1)} %shard_map.81), channel_id=1, replica_groups=mesh['sweep'=4,'zh'=4,'zl'=4,'x'=4,'core'=2] {'zh'}, dimensions={0} | all-to-all | bytes 196608 | tf_op jit(solution)/shard_map/all_to_all | solution.py:267
  109.7 14.1 %all_to_all.35 = bf16[16,96,128]{2,1,0:T(8,128)(2,1)S(1)} all-to-all(bf16[16,96,128]{2,1,0:T(8,128)(2,1)S(1)} %shard_map.82), channel_id=1, replica_groups=mesh['sweep'=4,'zh'=4,'zl'=4,'x'=4,'core'=2] {'zl','x'}, dimensions={0} | all-to-all | bytes 786432 | tf_op jit(solution)/shard_map/all_to_all | solution.py:267
  123.9 6.4 %all_gather.26.sigma = bf16[3072,128]{1,0:T(8,128)(2,1)S(1)} all-gather(bf16[1536,128]{1,0:T(8,128)(2,1)S(1)} %bitcast.35), channel_id=1, replica_groups=mesh['sweep'=4,'zh'=4,'zl'=4,'x'=4,'core'=2] {'core'}, dimensions={0}, use_global_device_ids=true | all-gather | bytes 1179648 | tf_op jit(solution)/shard_map/all_gather | solution.py:277
  130.3 2.1 %shard_map.83 = (f32[2,128]{1,0:T(2,128)S(1)}, bf16[1552,128]{1,0:T(8,128)(2,1)S(1)}) custom-call(s32[66]{0:T(128)S(1)} %pad_add_fusion.meta, f32[3200,128]{1,0:T(8,128)S(1)} %get-tuple-element.13.x, bf16[3072,128]{1,0:T(8,128)(2,1)S(1)} %all_gather.26.sigma, bf16[32,128,128]{2,1,0:T(8,128)(2,1)S(1)} %bitcast.24), custom_call_target="tpu_custom_call" | custom-call | tf_op jit(solution)/shard_map/pallas_call | solution.py:318
  132.3 1.3 collective-permute-start
  133.6 2.0 %shard_map.84 = bf16[32,128,128]{2,1,0:T(8,128)(2,1)} custom-call(s32[66]{0:T(128)S(1)} %pad_add_fusion.meta, f32[2,128]{1,0:T(2,128)S(1)} %get-tuple-element.16.factors, f32[3200,128]{1,0:T(8,128)S(1)} %get-tuple-element.13.x, bf16[3072,128]{1,0:T(8,128)(2,1)S(1)} %all_gather.26.sigma), custom_call_target="tpu_custom_call" | custom-call | flops 10000000 | bytes 4000000 | tf_op jit(solution)/shard_map/pallas_call | solution.py:331
  135.7 9.0 %collective-permute-done = bf16[1552,128]{1,0:T(8,128)(2,1)S(1)} collective-permute-done((bf16[1552,128]{1,0:T(8,128)(2,1)S(1)}, bf16[1552,128]{1,0:T(8,128)(2,1)S(1)}, u32[]{:S(2)}, u32[]{:S(2)}) %collective-permute-start) | collective-permute-done | bytes 397344 | tf_op jit(solution)/shard_map/ppermute | solution.py:330
  144.7 3.1 %all_gather.27.came = bf16[3104,128]{1,0:T(8,128)(2,1)S(1)} all-gather(bf16[1552,128]{1,0:T(8,128)(2,1)S(1)} %collective-permute-done), channel_id=1, replica_groups=mesh['sweep'=4,'zh'=4,'zl'=4,'x'=4,'core'=2] {'core'}, dimensions={0}, use_global_device_ids=true | all-gather | bytes 1191936 | tf_op jit(solution)/shard_map/all_gather | solution.py:340
  147.9 1.7 %shard_map.85 = bf16[32,128,128]{2,1,0:T(8,128)(2,1)} custom-call(bf16[3104,128]{1,0:T(8,128)(2,1)S(1)} %all_gather.27.came, bf16[32,128,128]{2,1,0:T(8,128)(2,1)S(1)} %bitcast.25), custom_call_target="tpu_custom_call" | custom-call | tf_op jit(solution)/shard_map/pallas_call | solution.py:341
  (2 shorter events, 0.1 us)
Async XLA Ops:
  28.2 45.4 %copy-start = (bf16[1,32,128,128]{3,2,1,0:T(8,128)(2,1)S(1)}, bf16[1,32,128,128]{3,2,1,0:T(8,128)(2,1)}, u32[]{:S(2)}) copy-start(bf16[1,32,128,128]{3,2,1,0:T(8,128)(2,1)} %param.11) | copy-start | bytes 3145732
  28.2 45.4 %copy-start.1 = (bf16[1,1,32,128,128]{4,3,2,1,0:T(8,128)(2,1)S(1)}, bf16[1,1,32,128,128]{4,3,2,1,0:T(8,128)(2,1)}, u32[]{:S(2)}) copy-start(bf16[1,1,32,128,128]{4,3,2,1,0:T(8,128)(2,1)} %param.7) | copy-start | bytes 3145732
  28.2 45.4 %copy-start.2 = (bf16[1,1,32,128,128]{4,3,2,1,0:T(8,128)(2,1)S(1)}, bf16[1,1,32,128,128]{4,3,2,1,0:T(8,128)(2,1)}, u32[]{:S(2)}) copy-start(bf16[1,1,32,128,128]{4,3,2,1,0:T(8,128)(2,1)} %param.8) | copy-start | bytes 3145732
  132.3 12.4 %collective-permute-start = (bf16[1552,128]{1,0:T(8,128)(2,1)S(1)}, bf16[1552,128]{1,0:T(8,128)(2,1)S(1)}, u32[]{:S(2)}, u32[]{:S(2)}) collective-permute-start(bf16[1552,128]{1,0:T(8,128)(2,1)S(1)} %get-tuple-element.17), channel_id=1, source_target_pairs={{0,128},{128,256},{256,384},{1,129},{129,257},{257,385},{2,130},{1... | collective-permute-start | bytes 1191944 | tf_op jit(solution)/shard_map/ppermute | solution.py:330

commit v8 on v7

--- a/solution.py
+++ b/solution.py
@@ -231,7 +231,7 @@
 
 
 def shift_kernel(came, env, out, wide, result, numbers, sizes, sems, own_sem):
-    numbers[...] = came[pl.ds(HALF, 8), :].astype(jnp.float32).astype(jnp.int32)
+    numbers[...] = came[pl.ds(HALF, TAIL), :].astype(jnp.float32).astype(jnp.int32)
     sizes_copy = pltpu.make_async_copy(numbers, sizes, own_sem.at[0])
     sizes_copy.start()
     wide[pl.ds(0, HALF), :] = came[pl.ds(0, HALF), :].astype(jnp.float32)
@@ -346,8 +346,8 @@
         scratch_shapes=[
             PACKED,
             BLOCKS,
-            pltpu.VMEM((8, WIDTH), jnp.int32),
-            pltpu.SMEM((8, WIDTH), jnp.int32),
+            pltpu.VMEM((TAIL, WIDTH), jnp.int32),
+            pltpu.SMEM((TAIL, WIDTH), jnp.int32),
             dma(GROUPS, 1),
             dma(1),
         ],

time: 150 us -> 150 us (level)
  no operation moved by 1% of the time
where the time goes in v8:
time: 150 us
  blocking collectives  124 us (83%)
  Pallas kernels  13.5 us (9%)
  waiting for transfers between devices  9.04 us (6%)
    all_to_all x6, blocking collectives, exchange(): return lax.all_to_all(value, axes, 0, 0)  103 us
    all_gather x2, blocking collectives, all_summed(): return lax.all_gather(half.reshape(HALF, WIDTH), 'core', tiled=True)  12.8 us
    ppermute x1, waiting for transfers between devices, shards(): lax.ppermute(renorm, 'sweep', [(i, i + 1) for i in range(positions - 1)])  9.04 us
    all_gather x2, blocking collectives, all_summed(): both = lax.all_gather(other, 'core')  5.05 us
    pallas_call x1, Pallas kernels, shards(): pl.pallas_call(first_kernel, in_specs=[SMEM] + [HBM] * 4, out_specs=[VMEM...  4.1 us
    pallas_call x1, Pallas kernels, shards(): pl.pallas_call(next_kernel, in_specs=[SMEM] + [VMEM] * 4 + [HBM], out_spe...  3.3 us
    all_gather x1, blocking collectives, shards(): came = lax.all_gather(came, 'core', tiled=True)  3.13 us
  transfers between devices with their start and end apart: 1, of which 1 were waited for; matrix products, arithmetic and copies ran while one was open for 0% of the time, Pallas kernels for 1%

profile of v8, /device:TPU:25, one launch (start us, length us, event | category | flops | bytes accessed | tf_op | source)
XLA Modules:
  0.0 149.6 jit_solution(11247759054948857949)
XLA Ops:
  0.7 0.8 pad_add_fusion.meta
  1.4 4.1 %shard_map.77 = (f32[1536,128]{1,0:T(8,128)S(1)}, bf16[1536,128]{1,0:T(8,128)(2,1)S(1)}, bf16[3072,128]{1,0:T(8,128)(2,1)S(1)}) custom-call(s32[66]{0:T(128)S(1)} %pad_add_fusion.meta, bf16[32,128,128]{2,1,0:T(8,128)(2,1)} %bitcast.36, bf16[32,128,128]{2,1,0:T(8,128)(2,1)} %bitcast.26, bf16[32,128,128]{2,1,0:T(8,128)(2,1)} %bitcast.28, ...), custom_call_target="tpu_custom_call" | custom-call | tf_op jit(solution)/shard_map/pallas_call | solution.py:298
  5.5 2.7 %all-gather = bf16[3072,128]{1,0:T(8,128)(2,1)S(1)} all-gather(bf16[1536,128]{1,0:T(8,128)(2,1)S(1)} %get-tuple-element.11), channel_id=2, replica_groups=mesh['sweep'=4,'zh'=4,'zl'=4,'x'=4,'core'=2] {'core'}, dimensions={0}, use_global_device_ids=true | all-gather | bytes 1179648 | tf_op jit(solution)/shard_map/all_gather | solution.py:271
  8.2 0.1 fusion.1
  8.3 19.9 %all_to_all.30.parts = bf16[16,96,128]{2,1,0:T(8,128)(2,1)S(1)} all-to-all(bf16[16,96,128]{2,1,0:T(8,128)(2,1)S(1)} %bitcast.33), channel_id=1, replica_groups=mesh['sweep'=4,'zh'=4,'zl'=4,'x'=4,'core'=2] {'zl','x'}, dimensions={0} | all-to-all | bytes 786432 | tf_op jit(solution)/shard_map/all_to_all | solution.py:267
  28.2 0.0 copy-start
  28.2 0.0 copy-start.1
  28.2 0.0 copy-start.2
  28.2 0.1 shard_map.78
  28.3 24.8 %all_to_all.31.parts = bf16[4,96,128]{2,1,0:T(8,128)(2,1)S(1)} all-to-all(bf16[4,96,128]{2,1,0:T(8,128)(2,1)S(1)} %shard_map.78), channel_id=1, replica_groups=mesh['sweep'=4,'zh'=4,'zl'=4,'x'=4,'core'=2] {'zh'}, dimensions={0} | all-to-all | bytes 196608 | tf_op jit(solution)/shard_map/all_to_all | solution.py:267
  53.1 14.1 %all_to_all.32 = bf16[16,96,128]{2,1,0:T(8,128)(2,1)S(1)} all-to-all(bf16[16,96,128]{2,1,0:T(8,128)(2,1)S(1)} %shard_map.79), channel_id=1, replica_groups=mesh['sweep'=4,'zh'=4,'zl'=4,'x'=4,'core'=2] {'zl','x'}, dimensions={0} | all-to-all | bytes 786432 | tf_op jit(solution)/shard_map/all_to_all | solution.py:267
  67.2 6.4 %all_gather.23.sigma = bf16[3072,128]{1,0:T(8,128)(2,1)S(1)} all-gather(bf16[1536,128]{1,0:T(8,128)(2,1)S(1)} %bitcast.34), channel_id=1, replica_groups=mesh['sweep'=4,'zh'=4,'zl'=4,'x'=4,'core'=2] {'core'}, dimensions={0}, use_global_device_ids=true | all-gather | bytes 1179648 | tf_op jit(solution)/shard_map/all_gather | solution.py:277
  73.6 0.0 copy-done
  73.6 0.0 copy-done.1
  73.6 0.0 copy-done.2
  73.6 3.3 %shard_map.80 = (f32[1536,128]{1,0:T(8,128)S(1)}, bf16[1536,128]{1,0:T(8,128)(2,1)S(1)}, f32[3200,128]{1,0:T(8,128)S(1)}) custom-call(s32[66]{0:T(128)S(1)} %pad_add_fusion.meta, bf16[3072,128]{1,0:T(8,128)(2,1)S(1)} %all_gather.23.sigma, bf16[3072,128]{1,0:T(8,128)(2,1)S(1)} %get-tuple-element.12.x0, bf16[32,128,128]{2,1,0:T(8,128)(2,1)S(1)} %bitcast.27, ...), custom_call_target="tpu_custom_call" | custom-call | tf_op jit(solution)/shard_map/pallas_call | solution.py:309
  76.9 2.4 %all-gather.1 = bf16[3072,128]{1,0:T(8,128)(2,1)S(1)} all-gather(bf16[1536,128]{1,0:T(8,128)(2,1)S(1)} %get-tuple-element.15), channel_id=3, replica_groups=mesh['sweep'=4,'zh'=4,'zl'=4,'x'=4,'core'=2] {'core'}, dimensions={0}, use_global_device_ids=true | all-gather | bytes 1179648 | tf_op jit(solution)/shard_map/all_gather | solution.py:271
  79.3 0.1 fusion
  79.4 15.1 %all_to_all.33.parts = bf16[16,96,128]{2,1,0:T(8,128)(2,1)S(1)} all-to-all(bf16[16,96,128]{2,1,0:T(8,128)(2,1)S(1)} %bitcast.32), channel_id=1, replica_groups=mesh['sweep'=4,'zh'=4,'zl'=4,'x'=4,'core'=2] {'zl','x'}, dimensions={0} | all-to-all | bytes 786432 | tf_op jit(solution)/shard_map/all_to_all | solution.py:267
  94.6 0.1 shard_map.81
  94.6 15.1 %all_to_all.34.parts = bf16[4,96,128]{2,1,0:T(8,128)(2,1)S(1)} all-to-all(bf16[4,96,128]{2,1,0:T(8,128)(2,1)S(1)} %shard_map.81), channel_id=1, replica_groups=mesh['sweep'=4,'zh'=4,'zl'=4,'x'=4,'core'=2] {'zh'}, dimensions={0} | all-to-all | bytes 196608 | tf_op jit(solution)/shard_map/all_to_all | solution.py:267
  109.7 14.1 %all_to_all.35 = bf16[16,96,128]{2,1,0:T(8,128)(2,1)S(1)} all-to-all(bf16[16,96,128]{2,1,0:T(8,128)(2,1)S(1)} %shard_map.82), channel_id=1, replica_groups=mesh['sweep'=4,'zh'=4,'zl'=4,'x'=4,'core'=2] {'zl','x'}, dimensions={0} | all-to-all | bytes 786432 | tf_op jit(solution)/shard_map/all_to_all | solution.py:267
  123.9 6.4 %all_gather.26.sigma = bf16[3072,128]{1,0:T(8,128)(2,1)S(1)} all-gather(bf16[1536,128]{1,0:T(8,128)(2,1)S(1)} %bitcast.35), channel_id=1, replica_groups=mesh['sweep'=4,'zh'=4,'zl'=4,'x'=4,'core'=2] {'core'}, dimensions={0}, use_global_device_ids=true | all-gather | bytes 1179648 | tf_op jit(solution)/shard_map/all_gather | solution.py:277
  130.3 2.1 %shard_map.83 = (f32[2,128]{1,0:T(2,128)S(1)}, bf16[1552,128]{1,0:T(8,128)(2,1)S(1)}) custom-call(s32[66]{0:T(128)S(1)} %pad_add_fusion.meta, f32[3200,128]{1,0:T(8,128)S(1)} %get-tuple-element.13.x, bf16[3072,128]{1,0:T(8,128)(2,1)S(1)} %all_gather.26.sigma, bf16[32,128,128]{2,1,0:T(8,128)(2,1)S(1)} %bitcast.24), custom_call_target="tpu_custom_call" | custom-call | tf_op jit(solution)/shard_map/pallas_call | solution.py:318
  132.4 1.3 collective-permute-start
  133.7 2.0 %shard_map.84 = bf16[32,128,128]{2,1,0:T(8,128)(2,1)} custom-call(s32[66]{0:T(128)S(1)} %pad_add_fusion.meta, f32[2,128]{1,0:T(2,128)S(1)} %get-tuple-element.16.factors, f32[3200,128]{1,0:T(8,128)S(1)} %get-tuple-element.13.x, bf16[3072,128]{1,0:T(8,128)(2,1)S(1)} %all_gather.26.sigma), custom_call_target="tpu_custom_call" | custom-call | flops 10000000 | bytes 4000000 | tf_op jit(solution)/shard_map/pallas_call | solution.py:331
  135.7 9.0 %collective-permute-done = bf16[1552,128]{1,0:T(8,128)(2,1)S(1)} collective-permute-done((bf16[1552,128]{1,0:T(8,128)(2,1)S(1)}, bf16[1552,128]{1,0:T(8,128)(2,1)S(1)}, u32[]{:S(2)}, u32[]{:S(2)}) %collective-permute-start) | collective-permute-done | bytes 397344 | tf_op jit(solution)/shard_map/ppermute | solution.py:330
  144.7 3.1 %all_gather.27.came = bf16[3104,128]{1,0:T(8,128)(2,1)S(1)} all-gather(bf16[1552,128]{1,0:T(8,128)(2,1)S(1)} %collective-permute-done), channel_id=1, replica_groups=mesh['sweep'=4,'zh'=4,'zl'=4,'x'=4,'core'=2] {'core'}, dimensions={0}, use_global_device_ids=true | all-gather | bytes 1191936 | tf_op jit(solution)/shard_map/all_gather | solution.py:340
  147.9 1.8 %shard_map.85 = bf16[32,128,128]{2,1,0:T(8,128)(2,1)} custom-call(bf16[3104,128]{1,0:T(8,128)(2,1)S(1)} %all_gather.27.came, bf16[32,128,128]{2,1,0:T(8,128)(2,1)S(1)} %bitcast.25), custom_call_target="tpu_custom_call" | custom-call | tf_op jit(solution)/shard_map/pallas_call | solution.py:341
  (2 shorter events, 0.1 us)
Async XLA Ops:
  28.2 45.4 %copy-start = (bf16[1,32,128,128]{3,2,1,0:T(8,128)(2,1)S(1)}, bf16[1,32,128,128]{3,2,1,0:T(8,128)(2,1)}, u32[]{:S(2)}) copy-start(bf16[1,32,128,128]{3,2,1,0:T(8,128)(2,1)} %param.11) | copy-start | bytes 3145732
  28.2 45.4 %copy-start.1 = (bf16[1,1,32,128,128]{4,3,2,1,0:T(8,128)(2,1)S(1)}, bf16[1,1,32,128,128]{4,3,2,1,0:T(8,128)(2,1)}, u32[]{:S(2)}) copy-start(bf16[1,1,32,128,128]{4,3,2,1,0:T(8,128)(2,1)} %param.7) | copy-start | bytes 3145732
  28.2 45.4 %copy-start.2 = (bf16[1,1,32,128,128]{4,3,2,1,0:T(8,128)(2,1)S(1)}, bf16[1,1,32,128,128]{4,3,2,1,0:T(8,128)(2,1)}, u32[]{:S(2)}) copy-start(bf16[1,1,32,128,128]{4,3,2,1,0:T(8,128)(2,1)} %param.8) | copy-start | bytes 3145732
  132.4 12.4 %collective-permute-start = (bf16[1552,128]{1,0:T(8,128)(2,1)S(1)}, bf16[1552,128]{1,0:T(8,128)(2,1)S(1)}, u32[]{:S(2)}, u32[]{:S(2)}) collective-permute-start(bf16[1552,128]{1,0:T(8,128)(2,1)S(1)} %get-tuple-element.17), channel_id=1, source_target_pairs={{0,128},{128,256},{256,384},{1,129},{129,257},{257,385},{2,130},{1... | collective-permute-start | bytes 1191944 | tf_op jit(solution)/shard_map/ppermute | solution.py:330

commit v9 on v8

--- a/solution.py
+++ b/solution.py
@@ -98,7 +98,7 @@
     return lax.broadcasted_iota(jnp.int32, (WIDTH, WIDTH), 0) < size
 
 
-def run_pairs(meta, xb_of, left, right, env, group, ready, env_ready, packed, mine, other):
+def run_pairs(meta, xb_of, left, right, env_block, group, ready, packed, mine, other):
     sector = meta[1]
     column = lax.broadcasted_iota(jnp.int32, (WIDTH, WIDTH), 1)
 
@@ -128,8 +128,7 @@
         return offset, at
 
     _, at = lax.fori_loop(0, NSEC // group, body, (jnp.int32(0), jnp.int32(0)))
-    env_ready()
-    term = 0.25 * dot(env[...], xb_of(sector, at, keep=False))
+    term = 0.25 * dot(env_block(), xb_of(sector, at, keep=False))
     packed[pl.ds(at, WIDTH), :] += jnp.where(square_mask(size_of(meta, sector)), term, 0.0)
     core = meta[0]
     mine[...] = packed[pl.ds(pl.multiple_of(core * HALF, 8), HALF), :]
@@ -156,16 +155,17 @@
             x_packed[pl.ds(offset, WIDTH), :] = x
         return x.astype(jnp.bfloat16)
 
-    run_pairs(meta, xb_of, left, right, env, FIRST_GROUP, ready, env_copy.wait, packed, mine, other)
+    def env_block():
+        env_copy.wait()
+        return env[...]
+
+    run_pairs(meta, xb_of, left, right, env_block, FIRST_GROUP, ready, packed, mine, other)
     x_out[...] = x_packed[pl.ds(0, ROWS), :].astype(jnp.bfloat16)
 
 
 def next_kernel(
-    meta, sigma, x0, left, right, env_in, mine, other, wide, packed, env, env_sem
+    meta, sigma, x0, left, right, env, mine, other, wide, packed
 ):
-    env_copy = pltpu.make_async_copy(env_in.at[meta[1]], env, env_sem.at[0])
-    env_copy.start()
-
     rows = pl.ds(0, ROWS)
     grow, drop = step_factors(x0, sigma)
     wide[rows, :] = grow * x0[...].astype(jnp.float32) - drop * sigma[...].astype(jnp.float32)
@@ -174,7 +174,9 @@
         mask = rows_below(size_of(meta, i))
         return jnp.where(mask, wide[pl.ds(offset, WIDTH), :], 0.0).astype(jnp.bfloat16)
 
-    run_pairs(meta, xb_of, left, right, env, NSEC, lambda g: None, env_copy.wait, packed, mine, other)
+    run_pairs(
+        meta, xb_of, left, right, lambda: env[meta[1]], NSEC, lambda g: None, packed, mine, other
+    )
 
 
 def renorm_kernel(
@@ -308,10 +310,10 @@
     sigma = all_summed(mine, other)
     mine, other, x = pl.pallas_call(
         next_kernel,
-        in_specs=[SMEM] + [VMEM] * 4 + [HBM],
+        in_specs=[SMEM] + [VMEM] * 5,
         out_specs=[VMEM] * 3,
         out_shape=sums + [state],
-        scratch_shapes=[PACKED] + env_scratch + [dma(1)],
+        scratch_shapes=[PACKED],
         compiler_params=limit(12),
     )(meta, sigma, x0, left, right, env)
     sigma = all_summed(mine, other)

time: 150 us -> 150 us (level)
  no operation moved by 1% of the time
where the time goes in v9:
time: 150 us; the launch traced here: 149 us
  blocking collectives  124 us (83%)
  Pallas kernels  13.3 us (9%)
  waiting for transfers between devices  9.04 us (6%)
    all_to_all x6, blocking collectives, exchange(): return lax.all_to_all(value, axes, 0, 0)  103 us
    all_gather x2, blocking collectives, all_summed(): return lax.all_gather(half.reshape(HALF, WIDTH), 'core', tiled=True)  12.8 us
    ppermute x1, waiting for transfers between devices, shards(): lax.ppermute(renorm, 'sweep', [(i, i + 1) for i in range(positions - 1)])  9.04 us
    all_gather x2, blocking collectives, all_summed(): both = lax.all_gather(other, 'core')  5.05 us
    pallas_call x1, Pallas kernels, shards(): pl.pallas_call(first_kernel, in_specs=[SMEM] + [HBM] * 4, out_specs=[VMEM...  4.1 us
    all_gather x1, blocking collectives, shards(): came = lax.all_gather(came, 'core', tiled=True)  3.13 us
    pallas_call x1, Pallas kernels, shards(): pl.pallas_call(next_kernel, in_specs=[SMEM] + [VMEM] * 5, out_specs=[VMEM...  3.11 us
  transfers between devices with their start and end apart: 1, of which 1 were waited for; matrix products, arithmetic and copies ran while one was open for 0% of the time, Pallas kernels for 1%

profile of v9, /device:TPU:25, one launch (start us, length us, event | category | flops | bytes accessed | tf_op | source)
XLA Modules:
  0.0 149.4 jit_solution(5539194697066593665)
XLA Ops:
  0.7 0.8 pad_add_fusion.meta
  1.4 4.1 %shard_map.77 = (f32[1536,128]{1,0:T(8,128)S(1)}, bf16[1536,128]{1,0:T(8,128)(2,1)S(1)}, bf16[3072,128]{1,0:T(8,128)(2,1)S(1)}) custom-call(s32[66]{0:T(128)S(1)} %pad_add_fusion.meta, bf16[32,128,128]{2,1,0:T(8,128)(2,1)} %bitcast.36, bf16[32,128,128]{2,1,0:T(8,128)(2,1)} %bitcast.26, bf16[32,128,128]{2,1,0:T(8,128)(2,1)} %bitcast.28, ...), custom_call_target="tpu_custom_call" | custom-call | tf_op jit(solution)/shard_map/pallas_call | solution.py:300
  5.5 2.7 %all-gather = bf16[3072,128]{1,0:T(8,128)(2,1)S(1)} all-gather(bf16[1536,128]{1,0:T(8,128)(2,1)S(1)} %get-tuple-element.11), channel_id=2, replica_groups=mesh['sweep'=4,'zh'=4,'zl'=4,'x'=4,'core'=2] {'core'}, dimensions={0}, use_global_device_ids=true | all-gather | bytes 1179648 | tf_op jit(solution)/shard_map/all_gather | solution.py:273
  8.2 0.1 fusion.1
  8.3 19.9 %all_to_all.30.parts = bf16[16,96,128]{2,1,0:T(8,128)(2,1)S(1)} all-to-all(bf16[16,96,128]{2,1,0:T(8,128)(2,1)S(1)} %bitcast.33), channel_id=1, replica_groups=mesh['sweep'=4,'zh'=4,'zl'=4,'x'=4,'core'=2] {'zl','x'}, dimensions={0} | all-to-all | bytes 786432 | tf_op jit(solution)/shard_map/all_to_all | solution.py:269
  28.2 0.0 copy-start
  28.2 0.0 copy-start.1
  28.2 0.0 copy-start.2
  28.2 0.1 shard_map.78
  28.3 24.8 %all_to_all.31.parts = bf16[4,96,128]{2,1,0:T(8,128)(2,1)S(1)} all-to-all(bf16[4,96,128]{2,1,0:T(8,128)(2,1)S(1)} %shard_map.78), channel_id=1, replica_groups=mesh['sweep'=4,'zh'=4,'zl'=4,'x'=4,'core'=2] {'zh'}, dimensions={0} | all-to-all | bytes 196608 | tf_op jit(solution)/shard_map/all_to_all | solution.py:269
  53.1 14.1 %all_to_all.32 = bf16[16,96,128]{2,1,0:T(8,128)(2,1)S(1)} all-to-all(bf16[16,96,128]{2,1,0:T(8,128)(2,1)S(1)} %shard_map.79), channel_id=1, replica_groups=mesh['sweep'=4,'zh'=4,'zl'=4,'x'=4,'core'=2] {'zl','x'}, dimensions={0} | all-to-all | bytes 786432 | tf_op jit(solution)/shard_map/all_to_all | solution.py:269
  67.2 6.4 %all_gather.23.sigma = bf16[3072,128]{1,0:T(8,128)(2,1)S(1)} all-gather(bf16[1536,128]{1,0:T(8,128)(2,1)S(1)} %bitcast.34), channel_id=1, replica_groups=mesh['sweep'=4,'zh'=4,'zl'=4,'x'=4,'core'=2] {'core'}, dimensions={0}, use_global_device_ids=true | all-gather | bytes 1179648 | tf_op jit(solution)/shard_map/all_gather | solution.py:279
  73.6 0.0 copy-done
  73.6 0.0 copy-done.1
  73.6 0.0 copy-done.2
  73.6 3.1 %shard_map.80 = (f32[1536,128]{1,0:T(8,128)S(1)}, bf16[1536,128]{1,0:T(8,128)(2,1)S(1)}, f32[3200,128]{1,0:T(8,128)S(1)}) custom-call(s32[66]{0:T(128)S(1)} %pad_add_fusion.meta, bf16[3072,128]{1,0:T(8,128)(2,1)S(1)} %all_gather.23.sigma, bf16[3072,128]{1,0:T(8,128)(2,1)S(1)} %get-tuple-element.12.x0, bf16[32,128,128]{2,1,0:T(8,128)(2,1)S(1)} %bitcast.27, ...), custom_call_target="tpu_custom_call" | custom-call | tf_op jit(solution)/shard_map/pallas_call | solution.py:311
  76.7 2.4 %all-gather.1 = bf16[3072,128]{1,0:T(8,128)(2,1)S(1)} all-gather(bf16[1536,128]{1,0:T(8,128)(2,1)S(1)} %get-tuple-element.15), channel_id=3, replica_groups=mesh['sweep'=4,'zh'=4,'zl'=4,'x'=4,'core'=2] {'core'}, dimensions={0}, use_global_device_ids=true | all-gather | bytes 1179648 | tf_op jit(solution)/shard_map/all_gather | solution.py:273
  79.1 0.1 fusion
  79.2 15.1 %all_to_all.33.parts = bf16[16,96,128]{2,1,0:T(8,128)(2,1)S(1)} all-to-all(bf16[16,96,128]{2,1,0:T(8,128)(2,1)S(1)} %bitcast.32), channel_id=1, replica_groups=mesh['sweep'=4,'zh'=4,'zl'=4,'x'=4,'core'=2] {'zl','x'}, dimensions={0} | all-to-all | bytes 786432 | tf_op jit(solution)/shard_map/all_to_all | solution.py:269
  94.4 0.1 shard_map.81
  94.4 15.1 %all_to_all.34.parts = bf16[4,96,128]{2,1,0:T(8,128)(2,1)S(1)} all-to-all(bf16[4,96,128]{2,1,0:T(8,128)(2,1)S(1)} %shard_map.81), channel_id=1, replica_groups=mesh['sweep'=4,'zh'=4,'zl'=4,'x'=4,'core'=2] {'zh'}, dimensions={0} | all-to-all | bytes 196608 | tf_op jit(solution)/shard_map/all_to_all | solution.py:269
  109.6 14.1 %all_to_all.35 = bf16[16,96,128]{2,1,0:T(8,128)(2,1)S(1)} all-to-all(bf16[16,96,128]{2,1,0:T(8,128)(2,1)S(1)} %shard_map.82), channel_id=1, replica_groups=mesh['sweep'=4,'zh'=4,'zl'=4,'x'=4,'core'=2] {'zl','x'}, dimensions={0} | all-to-all | bytes 786432 | tf_op jit(solution)/shard_map/all_to_all | solution.py:269
  123.7 6.4 %all_gather.26.sigma = bf16[3072,128]{1,0:T(8,128)(2,1)S(1)} all-gather(bf16[1536,128]{1,0:T(8,128)(2,1)S(1)} %bitcast.35), channel_id=1, replica_groups=mesh['sweep'=4,'zh'=4,'zl'=4,'x'=4,'core'=2] {'core'}, dimensions={0}, use_global_device_ids=true | all-gather | bytes 1179648 | tf_op jit(solution)/shard_map/all_gather | solution.py:279
  130.1 2.1 %shard_map.83 = (f32[2,128]{1,0:T(2,128)S(1)}, bf16[1552,128]{1,0:T(8,128)(2,1)S(1)}) custom-call(s32[66]{0:T(128)S(1)} %pad_add_fusion.meta, f32[3200,128]{1,0:T(8,128)S(1)} %get-tuple-element.13.x, bf16[3072,128]{1,0:T(8,128)(2,1)S(1)} %all_gather.26.sigma, bf16[32,128,128]{2,1,0:T(8,128)(2,1)S(1)} %bitcast.24), custom_call_target="tpu_custom_call" | custom-call | tf_op jit(solution)/shard_map/pallas_call | solution.py:320
  132.2 1.3 collective-permute-start
  133.5 2.0 %shard_map.84 = bf16[32,128,128]{2,1,0:T(8,128)(2,1)} custom-call(s32[66]{0:T(128)S(1)} %pad_add_fusion.meta, f32[2,128]{1,0:T(2,128)S(1)} %get-tuple-element.16.factors, f32[3200,128]{1,0:T(8,128)S(1)} %get-tuple-element.13.x, bf16[3072,128]{1,0:T(8,128)(2,1)S(1)} %all_gather.26.sigma), custom_call_target="tpu_custom_call" | custom-call | flops 10000000 | bytes 4000000 | tf_op jit(solution)/shard_map/pallas_call | solution.py:333
  135.5 9.0 %collective-permute-done = bf16[1552,128]{1,0:T(8,128)(2,1)S(1)} collective-permute-done((bf16[1552,128]{1,0:T(8,128)(2,1)S(1)}, bf16[1552,128]{1,0:T(8,128)(2,1)S(1)}, u32[]{:S(2)}, u32[]{:S(2)}) %collective-permute-start) | collective-permute-done | bytes 397344 | tf_op jit(solution)/shard_map/ppermute | solution.py:332
  144.5 3.1 %all_gather.27.came = bf16[3104,128]{1,0:T(8,128)(2,1)S(1)} all-gather(bf16[1552,128]{1,0:T(8,128)(2,1)S(1)} %collective-permute-done), channel_id=1, replica_groups=mesh['sweep'=4,'zh'=4,'zl'=4,'x'=4,'core'=2] {'core'}, dimensions={0}, use_global_device_ids=true | all-gather | bytes 1191936 | tf_op jit(solution)/shard_map/all_gather | solution.py:342
  147.7 1.8 %shard_map.85 = bf16[32,128,128]{2,1,0:T(8,128)(2,1)} custom-call(bf16[3104,128]{1,0:T(8,128)(2,1)S(1)} %all_gather.27.came, bf16[32,128,128]{2,1,0:T(8,128)(2,1)S(1)} %bitcast.25), custom_call_target="tpu_custom_call" | custom-call | tf_op jit(solution)/shard_map/pallas_call | solution.py:343
  (2 shorter events, 0.1 us)
Async XLA Ops:
  28.2 45.4 %copy-start = (bf16[1,32,128,128]{3,2,1,0:T(8,128)(2,1)S(1)}, bf16[1,32,128,128]{3,2,1,0:T(8,128)(2,1)}, u32[]{:S(2)}) copy-start(bf16[1,32,128,128]{3,2,1,0:T(8,128)(2,1)} %param.11) | copy-start | bytes 3145732
  28.2 45.4 %copy-start.1 = (bf16[1,1,32,128,128]{4,3,2,1,0:T(8,128)(2,1)S(1)}, bf16[1,1,32,128,128]{4,3,2,1,0:T(8,128)(2,1)}, u32[]{:S(2)}) copy-start(bf16[1,1,32,128,128]{4,3,2,1,0:T(8,128)(2,1)} %param.7) | copy-start | bytes 3145732
  28.2 45.4 %copy-start.2 = (bf16[1,1,32,128,128]{4,3,2,1,0:T(8,128)(2,1)S(1)}, bf16[1,1,32,128,128]{4,3,2,1,0:T(8,128)(2,1)}, u32[]{:S(2)}) copy-start(bf16[1,1,32,128,128]{4,3,2,1,0:T(8,128)(2,1)} %param.8) | copy-start | bytes 3145732
  132.2 12.4 %collective-permute-start = (bf16[1552,128]{1,0:T(8,128)(2,1)S(1)}, bf16[1552,128]{1,0:T(8,128)(2,1)S(1)}, u32[]{:S(2)}, u32[]{:S(2)}) collective-permute-start(bf16[1552,128]{1,0:T(8,128)(2,1)S(1)} %get-tuple-element.17), channel_id=1, source_target_pairs={{0,128},{128,256},{256,384},{1,129},{129,257},{257,385},{2,130},{1... | collective-permute-start | bytes 1191944 | tf_op jit(solution)/shard_map/ppermute | solution.py:332
